TPU v7x, 128 devices: a whole 4x4x4 slice. The times are simulated.
128 devices in a mesh: wide: 16 (over x_lo, y, core), narrow: 8 (over x_hi, z).
Axes of the slice: x: 4 (x_hi: 2, x_lo: 2; x = x_hi * 2 + x_lo), y: 4, z: 4, core: 2. Of those that a mesh axis runs over, the one named last changes fastest.
Arguments:
- coupling: bfloat16 [32768, 32768], P('wide', 'narrow'), may hold values from -0.046875 to 0.046875
- hashes: int32 [32768, 128], P(('wide', 'narrow')), may hold values from 0 to 65535
- momentum: float32 [32768, 128], P(('wide', 'narrow')), may hold values from -4 to 4
- linear: float32 [32768], P(('wide', 'narrow')), may hold values from -4 to 4
Outputs:
- positions: float32 [32768, 128], P(('wide', 'narrow'))
- velocity: float32 [32768, 128], P(('wide', 'narrow'))
All inputs are finite; a program needn't handle non-finite values.
Results may differ from a plain program's by a relative error of at most 0.0037.
Values may be sent and summed in bfloat16 or wider, within the bound.
No kernel may reach another device: no remote copies, remote signals or barrier semaphores. Data moves between devices by JAX's collectives and lax.ppermute only.
A program may use at most 128 MiB of HBM per device.

v0:
```python
import jax
import jax.numpy as jnp
from jax import lax
from jax.sharding import PartitionSpec as P

STEPS = 4


time_step = 1.25
coupling_scale = 0.5


def on_device(coupling, hashes, momentum, linear):
    columns = coupling.shape[1]
    column_index = lax.axis_index("narrow")
    positions = (hashes.astype(jnp.float32) - 32768.0) / 65536.0
    velocity = momentum
    linear_term = linear[:, None]
    for step_index in range(STEPS):
        lowered = positions.astype(jnp.bfloat16)
        row_block = lax.all_gather(lowered, "narrow", axis=0, tiled=True)
        everything = lax.all_gather(row_block, "wide", axis=0, tiled=True)
        column_block = lax.dynamic_slice_in_dim(everything, column_index * columns, columns, 0)
        local_field = lax.psum_scatter(
            jnp.dot(coupling, column_block, preferred_element_type=jnp.float32),
            "narrow",
            scatter_dimension=0,
            tiled=True,
        )
        pump_level = (step_index + 1.0) / (STEPS + 1.0)
        velocity = velocity + time_step * (
            -(1.0 - pump_level) * positions + coupling_scale * (local_field + linear_term)
        )
        moved = positions + time_step * velocity
        clamped = jnp.clip(moved, -1.0, 1.0)
        velocity = velocity - (moved - clamped) / time_step
        positions = clamped
    return (positions, velocity)


def solution(mesh):
    return jax.shard_map(
        on_device,
        mesh=mesh,
        in_specs=(
            P("wide", "narrow"),
            P(("wide", "narrow"), None),
            P(("wide", "narrow"), None),
            P(("wide", "narrow")),
        ),
        out_specs=(P(("wide", "narrow"), None), P(("wide", "narrow"), None)),
        check_vma=False,
    )
```

profile of v0, /device:TPU:0, one launch (start us, length us, event | category | flops | bytes accessed | tf_op | source)
XLA Modules:
  0.0 719.9 jit_solution(15806095188110680459)
XLA Ops:
  7.2 0.0 all-gather.5.cloned.1.call-start
  7.2 1.0 copy.6
  8.3 38.2 %all_gather.24 = bf16[2048,128]{0,1:T(8,128)(2,1)} all-gather(bf16[256,128]{0,1:T(8,128)(2,1)S(1)} %fusion.20), channel_id=1, replica_groups=mesh['wide'=16,'narrow'=8] {'narrow'}, dimensions={0}, use_global_device_ids=true | all-gather | bytes 589824 | tf_op jit(solution)/shard_map/all_gather | solution.py:21
  46.5 0.0 reduce-scatter.5.cloned.1.call-start
  46.5 53.4 %all-gather.5.cloned.1.call-done = bf16[32768,128]{0,1:T(8,128)(2,1)} async-done(((bf16[2048,128]{0,1:T(8,128)(2,1)}), bf16[32768,128]{0,1:T(8,128)(2,1)}) %all-gather.5.cloned.1.call-update) | async-done | bytes 8388624 | tf_op jit(solution)/shard_map/all_gather | solution.py:22
  99.9 12.8 %convolution_bitcast_fusion.3 = f32[2048,128]{0,1:T(8,128)} fusion(bf16[2048,4096]{1,0:T(8,128)(2,1)} %param.4, bf16[32768,128]{0,1:T(8,128)(2,1)} %all-gather.5.cloned.1.call-done, s32[]{:T(128)S(6)} %select_n.2), kind=kOutput, calls=%fused_computation.3 | convolution fusion | flops 2147483648 | bytes 18874372 | tf_op jit(solution)/shard_map/dot_general | solution.py:25
  112.8 0.0 all-gather.7.cloned.1.call-start
  112.8 0.1 copy.7
  112.9 72.7 %reduce-scatter.5.cloned.1.call-done = f32[256,128]{0,1:T(8,128)} async-done(((f32[2048,128]{0,1:T(8,128)}), f32[256,128]{0,1:T(8,128)}) %reduce-scatter.5.cloned.1.call-update) | async-done | bytes 131088 | tf_op jit(solution)/shard_map/reduce_scatter | solution.py:24
  185.6 1.0 clamp_convert_fusion.2
  186.7 37.0 %all_gather.26 = bf16[2048,128]{0,1:T(8,128)(2,1)} all-gather(bf16[256,128]{0,1:T(8,128)(2,1)S(1)} %get-tuple-element.6), channel_id=1, replica_groups=mesh['wide'=16,'narrow'=8] {'narrow'}, dimensions={0}, use_global_device_ids=true | all-gather | bytes 589824 | tf_op jit(solution)/shard_map/all_gather | solution.py:21
  223.7 0.0 reduce-scatter.7.cloned.1.call-start
  223.7 51.2 %all-gather.7.cloned.1.call-done = bf16[32768,128]{0,1:T(8,128)(2,1)} async-done(((bf16[2048,128]{0,1:T(8,128)(2,1)}), bf16[32768,128]{0,1:T(8,128)(2,1)}) %all-gather.7.cloned.1.call-update) | async-done | bytes 8388624 | tf_op jit(solution)/shard_map/all_gather | solution.py:22
  274.9 12.8 %convolution_bitcast_fusion.2 = f32[2048,128]{0,1:T(8,128)} fusion(bf16[2048,4096]{1,0:T(8,128)(2,1)} %param.4, bf16[32768,128]{0,1:T(8,128)(2,1)} %all-gather.7.cloned.1.call-done, s32[]{:T(128)S(6)} %select_n.2), kind=kOutput, calls=%fused_computation.2 | convolution fusion | flops 2147483648 | bytes 18874372 | tf_op jit(solution)/shard_map/dot_general | solution.py:25
  287.7 0.0 all-gather.9.cloned.1.call-start
  287.8 72.8 %reduce-scatter.7.cloned.1.call-done = f32[256,128]{0,1:T(8,128)} async-done(((f32[2048,128]{0,1:T(8,128)}), f32[256,128]{0,1:T(8,128)}) %reduce-scatter.7.cloned.1.call-update) | async-done | bytes 131088 | tf_op jit(solution)/shard_map/reduce_scatter | solution.py:24
  360.6 1.0 clamp_convert_fusion.1
  361.6 37.0 %all_gather.28 = bf16[2048,128]{0,1:T(8,128)(2,1)} all-gather(bf16[256,128]{0,1:T(8,128)(2,1)S(1)} %get-tuple-element.4), channel_id=1, replica_groups=mesh['wide'=16,'narrow'=8] {'narrow'}, dimensions={0}, use_global_device_ids=true | all-gather | bytes 589824 | tf_op jit(solution)/shard_map/all_gather | solution.py:21
  398.6 0.2 reduce-scatter.9.cloned.1.call-start
  398.8 50.9 %all-gather.9.cloned.1.call-done = bf16[32768,128]{0,1:T(8,128)(2,1)} async-done(((bf16[2048,128]{0,1:T(8,128)(2,1)}), bf16[32768,128]{0,1:T(8,128)(2,1)}) %all-gather.9.cloned.1.call-update) | async-done | bytes 8388624 | tf_op jit(solution)/shard_map/all_gather | solution.py:22
  449.8 12.8 %convolution_bitcast_fusion.1 = f32[2048,128]{0,1:T(8,128)} fusion(bf16[2048,4096]{1,0:T(8,128)(2,1)} %param.4, bf16[32768,128]{0,1:T(8,128)(2,1)} %all-gather.9.cloned.1.call-done, s32[]{:T(128)S(6)} %select_n.2), kind=kOutput, calls=%fused_computation.1 | convolution fusion | flops 2147483648 | bytes 18874372 | tf_op jit(solution)/shard_map/dot_general | solution.py:25
  462.6 0.0 all-gather.11.cloned.1.call-start
  462.6 72.8 %reduce-scatter.9.cloned.1.call-done = f32[256,128]{0,1:T(8,128)} async-done(((f32[2048,128]{0,1:T(8,128)}), f32[256,128]{0,1:T(8,128)}) %reduce-scatter.9.cloned.1.call-update) | async-done | bytes 131088 | tf_op jit(solution)/shard_map/reduce_scatter | solution.py:24
  535.5 1.1 clamp_convert_fusion
  536.5 37.0 %all_gather.30 = bf16[2048,128]{0,1:T(8,128)(2,1)} all-gather(bf16[256,128]{0,1:T(8,128)(2,1)S(1)} %clamp_convert_fusion), channel_id=1, replica_groups=mesh['wide'=16,'narrow'=8] {'narrow'}, dimensions={0}, use_global_device_ids=true | all-gather | bytes 589824 | tf_op jit(solution)/shard_map/all_gather | solution.py:21
  573.5 0.0 reduce-scatter.11.cloned.1.call-start
  573.6 51.1 %all-gather.11.cloned.1.call-done = bf16[32768,128]{0,1:T(8,128)(2,1)} async-done(((bf16[2048,128]{0,1:T(8,128)(2,1)}), bf16[32768,128]{0,1:T(8,128)(2,1)}) %all-gather.11.cloned.1.call-update) | async-done | bytes 8388624 | tf_op jit(solution)/shard_map/all_gather | solution.py:22
  624.7 12.8 %convolution_bitcast_fusion = f32[2048,128]{0,1:T(8,128)} fusion(bf16[2048,4096]{1,0:T(8,128)(2,1)} %param.4, bf16[32768,128]{0,1:T(8,128)(2,1)} %all-gather.11.cloned.1.call-done, s32[]{:T(128)S(6)} %select_n.2), kind=kOutput, calls=%fused_computation | convolution fusion | flops 2147483648 | bytes 18874372 | tf_op jit(solution)/shard_map/dot_general | solution.py:25
  637.6 73.0 %reduce-scatter.11.cloned.1.call-done = f32[256,128]{0,1:T(8,128)} async-done(((f32[2048,128]{0,1:T(8,128)}), f32[256,128]{0,1:T(8,128)}) %reduce-scatter.11.cloned.1.call-update) | async-done | bytes 131088 | tf_op jit(solution)/shard_map/reduce_scatter | solution.py:24
  710.5 1.0 multiply_subtract_fusion
  711.6 0.8 copy.9
  712.3 0.8 copy.8
  (17 shorter events, 0.2 us)
Async XLA Ops:
  7.2 105.6 %copy-start.2 = (f32[256,128]{1,0:T(8,128)S(1)}, f32[256,128]{1,0:T(8,128)}, u32[]{:S(2)}) copy-start(f32[256,128]{1,0:T(8,128)} %param.6) | copy-start | bytes 393220
  7.2 178.4 %copy-start.3 = (f32[256]{0:T(256)S(1)}, f32[256]{0:T(256)}, u32[]{:S(2)}) copy-start(f32[256]{0:T(256)} %param.7) | copy-start | bytes 3076
  7.2 92.7 %all-gather.5.cloned.1.call-start = ((), (), s32[]{:S(2)}) async-start(), calls=%async_computation.4 | async-start | bytes 8912896 | tf_op jit(solution)/shard_map/all_gather | solution.py:22
  46.5 139.1 %reduce-scatter.5.cloned.1.call-start = ((), (), s32[]{:S(2)}) async-start(), calls=%async_computation.5 | async-start | bytes 1179648 | tf_op jit(solution)/shard_map/reduce_scatter | solution.py:24
  112.8 162.1 %all-gather.7.cloned.1.call-start = ((), (), s32[]{:S(2)}) async-start(), calls=%async_computation.6 | async-start | bytes 8912896 | tf_op jit(solution)/shard_map/all_gather | solution.py:22
  185.6 175.0 %copy-start.1 = (f32[256,128]{0,1:T(8,128)S(1)}, f32[256,128]{0,1:T(8,128)}, u32[]{:S(2)}) copy-start(f32[256,128]{0,1:T(8,128)} %reduce-scatter.5.cloned.1.call-done) | copy-start | bytes 393220
  223.7 136.9 %reduce-scatter.7.cloned.1.call-start = ((), (), s32[]{:S(2)}) async-start(), calls=%async_computation.7 | async-start | bytes 1179648 | tf_op jit(solution)/shard_map/reduce_scatter | solution.py:24
  287.7 162.0 %all-gather.9.cloned.1.call-start = ((), (), s32[]{:S(2)}) async-start(), calls=%async_computation.8 | async-start | bytes 8912896 | tf_op jit(solution)/shard_map/all_gather | solution.py:22
  398.6 136.9 %reduce-scatter.9.cloned.1.call-start = ((), (), s32[]{:S(2)}) async-start(), calls=%async_computation.9 | async-start | bytes 1179648 | tf_op jit(solution)/shard_map/reduce_scatter | solution.py:24
  462.6 162.1 %all-gather.11.cloned.1.call-start = ((), (), s32[]{:S(2)}) async-start(), calls=%async_computation.10 | async-start | bytes 8912896 | tf_op jit(solution)/shard_map/all_gather | solution.py:22
  535.5 175.0 %copy-start = (f32[256,128]{0,1:T(8,128)S(1)}, f32[256,128]{0,1:T(8,128)}, u32[]{:S(2)}) copy-start(f32[256,128]{0,1:T(8,128)} %reduce-scatter.9.cloned.1.call-done) | copy-start | bytes 393220
  573.5 137.0 %reduce-scatter.11.cloned.1.call-start = ((), (), s32[]{:S(2)}) async-start(), calls=%async_computation.11 | async-start | bytes 1179648 | tf_op jit(solution)/shard_map/reduce_scatter | solution.py:24
Sparse Core Ops, SparseCore 0:
  46.6 53.2 all-gather.4
  112.9 72.6 reduce-scatter.4
  223.8 51.0 all-gather.6
  287.9 72.6 reduce-scatter.6
  398.7 50.9 all-gather.8
  462.7 72.7 reduce-scatter.8
  573.7 51.0 all-gather.10
  637.7 72.7 reduce-scatter.10
where the time goes:
time: 720 us
  waiting for transfers between devices  498 us (69%)
  blocking collectives  149 us (21%)
  matrix products  51.3 us (7%)
  between operations  14.2 us (2%)
    reduce_scatter x4, waiting for transfers between devices, on_device(): lax.psum_scatter(jnp.dot(coupling, column_block, preferred_element_type=j...  291 us
    all_gather x4, waiting for transfers between devices, on_device(): everything = lax.all_gather(row_block, 'wide', axis=0, tiled=True)  207 us
    all_gather x4, blocking collectives, on_device(): row_block = lax.all_gather(lowered, 'narrow', axis=0, tiled=True)  149 us
    dot_general x4, matrix products, on_device(): jnp.dot(coupling, column_block, preferred_element_type=jnp.float32)  51.3 us
  transfers between devices with their start and end apart: 8, of which 8 were waited for; matrix products, arithmetic and copies ran while one was open for 0% of the time, Pallas kernels for 0%

commit v1 on v0

v1 whole, which is shorter than its diff:
```python
import functools

import jax
import jax.numpy as jnp
from jax import lax
from jax.experimental import pallas as pl
from jax.experimental.pallas import tpu as pltpu
from jax.sharding import PartitionSpec as P

STEPS = 4
AXES = ("wide", "narrow")

time_step = 1.25
coupling_scale = 0.5


def shifted(block, shift):
    return (block // 4 ^ shift // 4) * 4 + (block % 4 + shift % 4) % 4


def permuted(array, place, wide, narrow):
    pairs = []
    for w in range(wide):
        for n in range(narrow):
            to_w, to_n = place(w, n)
            pairs.append((w * narrow + n, to_w * narrow + to_n))
    return lax.ppermute(array, AXES, pairs)


def other_core(w, n):
    return w ^ 1, n


def to_column(turn):
    def place(w, n):
        core = w % 2
        return shifted(n, turn + 4 * core) * 2 + core, w // 2

    return place


def multiply(columns_ref, coupling_ref, *refs, add):
    *pieces, out_ref = refs
    rows = coupling_ref.shape[0]
    tile = 512

    @pl.loop(0, rows // tile)
    def _(index):
        span = pl.ds(pl.multiple_of(index * tile, tile), tile)
        if add:
            total = pieces[-1][span, :]
        else:
            total = jnp.zeros((tile, 128), jnp.float32)
        for turn in range(4):
            for half in range(2):
                first = pl.multiple_of(columns_ref[turn * 2 + half], 128)
                total += jnp.dot(
                    coupling_ref[span, pl.ds(first, 256)],
                    pieces[turn][half * 256 : half * 256 + 256, :],
                    preferred_element_type=jnp.float32,
                )
        out_ref[span, :] = total.astype(out_ref.dtype)


def product(columns, coupling, pieces, total=None):
    operands = [coupling, *pieces] + ([] if total is None else [total])
    return pl.pallas_call(
        functools.partial(multiply, add=total is not None),
        out_shape=jax.ShapeDtypeStruct((coupling.shape[0], 128), jnp.float32),
        in_specs=[pl.BlockSpec(memory_space=pltpu.SMEM)] + [pl.BlockSpec(memory_space=pltpu.VMEM)] * len(operands),
        out_specs=pl.BlockSpec(memory_space=pltpu.VMEM),
        compiler_params=pltpu.CompilerParams(vmem_limit_bytes=8 << 20),
        cost_estimate=pl.CostEstimate(flops=2 * 2048 * 2048 * 128, bytes_accessed=10 << 20, transcendentals=0),
    )(columns, *[pltpu.with_memory_space_constraint(o, pltpu.VMEM) for o in operands])


def on_device(wide, narrow, coupling, hashes, momentum, linear):
    own_w, own_n = lax.axis_index("wide"), lax.axis_index("narrow")
    block, core = own_w // 2, own_w % 2

    def columns_of(from_core):
        columns = []
        for turn in range(4):
            piece = (block // 4 ^ from_core) * 4 + (block % 4 + 4 - turn) % 4
            for half in (from_core, 1 - from_core):
                columns.append(half * 2048 + piece * 256)
        return jnp.stack(columns).astype(jnp.int32)

    own_columns, other_columns = columns_of(core), columns_of(1 - core)
    positions = (hashes.astype(jnp.float32) - 32768.0) / 65536.0
    velocity = momentum
    linear_term = linear[:, None]
    for step_index in range(STEPS):
        lowered = positions.astype(jnp.bfloat16)
        chip = jnp.concatenate([lowered, permuted(lowered, other_core, wide, narrow)])
        own = [permuted(chip, to_column(turn), wide, narrow) for turn in range(4)]
        other = [permuted(piece, other_core, wide, narrow) for piece in own]
        total = product(own_columns, coupling, own)
        partial = product(other_columns, coupling, other, total)
        sent = (partial * 256.0).astype(jnp.float16)
        parts = lax.all_to_all(sent.reshape(narrow, -1, 128), "narrow", 0, 0)
        local_field = jnp.sum(parts.astype(jnp.float32), axis=0) / 256.0
        pump_level = (step_index + 1.0) / (STEPS + 1.0)
        velocity = velocity + time_step * (
            -(1.0 - pump_level) * positions + coupling_scale * (local_field + linear_term)
        )
        moved = positions + time_step * velocity
        clamped = jnp.clip(moved, -1.0, 1.0)
        velocity = velocity - (moved - clamped) / time_step
        positions = clamped
    return (positions, velocity)


def solution(mesh):
    return jax.shard_map(
        functools.partial(on_device, mesh.shape["wide"], mesh.shape["narrow"]),
        mesh=mesh,
        in_specs=(
            P("wide", "narrow"),
            P(("wide", "narrow"), None),
            P(("wide", "narrow"), None),
            P(("wide", "narrow")),
        ),
        out_specs=(P(("wide", "narrow"), None), P(("wide", "narrow"), None)),
        check_vma=False,
    )
```

time: 720 us -> 192 us (0.27)
  waiting for transfers between devices: 498 us -> 25.7 us
  blocking collectives: 149 us -> 92.5 us
  matrix products: 51.3 us -> 0 us
  starting transfers between devices: 0.51 us -> 33.7 us
  Pallas kernels: 0 us -> 27.1 us
  between operations: 14.2 us -> 1.01 us
    reduce_scatter x4 -> x0, waiting for transfers between devices: 291 us -> none  [on_device(): lax.psum_scatter(jnp.dot(coupling, column_block, preferred_element_type=j...]
    all_gather x4 -> x0, waiting for transfers between devices: 207 us -> none  [on_device(): everything = lax.all_gather(row_block, 'wide', axis=0, tiled=True)]
    all_gather x4 -> x0, blocking collectives: 149 us -> none  [on_device(): row_block = lax.all_gather(lowered, 'narrow', axis=0, tiled=True)]
    all_to_all x0 -> x4, blocking collectives: none -> 92.5 us  [on_device(): parts = lax.all_to_all(sent.reshape(narrow, -1, 128), 'narrow', 0, 0)]
    dot_general x4 -> x0, matrix products: 51.3 us -> none  [on_device(): jnp.dot(coupling, column_block, preferred_element_type=jnp.float32)]
    ppermute x0 -> x36, starting transfers between devices: none -> 33.7 us  [permuted(): return lax.ppermute(array, AXES, pairs)]
    pallas_call x0 -> x8, Pallas kernels: none -> 27.1 us  [product(): pl.pallas_call(functools.partial(multiply, add=total is not None), out_sh...]
    ppermute x0 -> x36, waiting for transfers between devices: none -> 25.7 us  [permuted(): return lax.ppermute(array, AXES, pairs)]
  transfers between devices with their start and end apart: 8 -> 36, of which waited for: 8 -> 13; matrix products, arithmetic and copies ran while one was open for 0% -> 0% of each run, Pallas kernels for 0% -> 7%
where the time goes in v1:
time: 192 us; the launch traced here: 191 us
  blocking collectives  92.5 us (48%)
  starting transfers between devices  33.7 us (18%)
  Pallas kernels  27.1 us (14%)
  waiting for transfers between devices  25.7 us (13%)
  local copies, waits for them, and re-layouts  8.29 us (4%)
  other arithmetic  2.98 us (2%)
    all_to_all x4, blocking collectives, on_device(): parts = lax.all_to_all(sent.reshape(narrow, -1, 128), 'narrow', 0, 0)  92.5 us
    ppermute x36, starting transfers between devices, permuted(): return lax.ppermute(array, AXES, pairs)  33.7 us
    pallas_call x8, Pallas kernels, product(): pl.pallas_call(functools.partial(multiply, add=total is not None), out_sh...  27.1 us
    ppermute x36, waiting for transfers between devices, permuted(): return lax.ppermute(array, AXES, pairs)  25.7 us
    unnamed x10, local copies, waits for them, and re-layouts  8.12 us
  transfers between devices with their start and end apart: 36, of which 13 were waited for; matrix products, arithmetic and copies ran while one was open for 0% of the time, Pallas kernels for 7%

profile of v1, /device:TPU:0, one launch (start us, length us, event | category | flops | bytes accessed | tf_op | source)
XLA Modules:
  0.0 191.3 jit_solution(337026001396555672)
XLA Ops:
  2.9 3.2 %collective-permute-start.7 = (bf16[512,128]{1,0:T(8,128)(2,1)S(1)}, bf16[512,128]{1,0:T(8,128)(2,1)S(1)}, u32[]{:S(2)}, u32[]{:S(2)}) collective-permute-start(bf16[512,128]{1,0:T(8,128)(2,1)S(1)} %pad_maximum_fusion), channel_id=1, source_target_pairs={{0,48},{1,0},{2,16},{3,32},{4,112},{5,64},{6,80},{7,96},{8,120},{9... | collective-permute-start | bytes 393224 | tf_op jit(solution)/shard_map/ppermute | solution.py:27
  6.1 4.8 %collective-permute-start.5 = (bf16[512,128]{1,0:T(8,128)(2,1)S(1)}, bf16[512,128]{1,0:T(8,128)(2,1)S(1)}, u32[]{:S(2)}, u32[]{:S(2)}) collective-permute-start(bf16[512,128]{1,0:T(8,128)(2,1)S(1)} %pad_maximum_fusion), channel_id=1, source_target_pairs={{0,32},{1,48},{2,0},{3,16},{4,96},{5,112},{6,64},{7,80},{8,104},{9... | collective-permute-start | bytes 393224 | tf_op jit(solution)/shard_map/ppermute | solution.py:27
  11.5 4.0 %collective-permute-start.8 = (bf16[512,128]{1,0:T(8,128)(2,1)S(1)}, bf16[512,128]{1,0:T(8,128)(2,1)S(1)}, u32[]{:S(2)}, u32[]{:S(2)}) collective-permute-start(bf16[512,128]{1,0:T(8,128)(2,1)S(1)} %collective-permute-done.7.refs_3_), channel_id=1, source_target_pairs={{0,8},{1,9},{2,10},{3,11},{4,12},{5,13},{6,14},{7,15},{8,0},{9,1},... | collective-permute-start | bytes 393224 | tf_op jit(solution)/shard_map/ppermute | solution.py:27
  15.6 2.4 %collective-permute-done.3.refs_1_ = bf16[512,128]{1,0:T(8,128)(2,1)S(1)} collective-permute-done((bf16[512,128]{1,0:T(8,128)(2,1)S(1)}, bf16[512,128]{1,0:T(8,128)(2,1)S(1)}, u32[]{:S(2)}, u32[]{:S(2)}) %collective-permute-start.3) | collective-permute-done | bytes 131104 | tf_op jit(solution)/shard_map/ppermute | solution.py:27
  17.9 2.4 %collective-permute-start.4 = (bf16[512,128]{1,0:T(8,128)(2,1)S(1)}, bf16[512,128]{1,0:T(8,128)(2,1)S(1)}, u32[]{:S(2)}, u32[]{:S(2)}) collective-permute-start(bf16[512,128]{1,0:T(8,128)(2,1)S(1)} %collective-permute-done.3.refs_1_), channel_id=1, source_target_pairs={{0,8},{1,9},{2,10},{3,11},{4,12},{5,13},{6,14},{7,15},{8,0},{9,1},... | collective-permute-start | bytes 393224 | tf_op jit(solution)/shard_map/ppermute | solution.py:27
  20.5 5.8 %copy-done = bf16[2048,4096]{1,0:T(8,128)(2,1)S(1)} copy-done((bf16[2048,4096]{1,0:T(8,128)(2,1)S(1)}, bf16[2048,4096]{1,0:T(8,128)(2,1)}, u32[]{:S(2)}) %copy-start) | copy-done | bytes 16777240
  26.3 3.4 %shard_map.59.refs_4_ = f32[2048,128]{1,0:T(8,128)S(1)} custom-call(s32[8]{0:T(128)S(1)} %stack.71.columns_ref, bf16[2048,4096]{1,0:T(8,128)(2,1)S(1)} %copy-done, bf16[512,128]{1,0:T(8,128)(2,1)S(1)} %collective-permute-done.1.refs_0_, bf16[512,128]{1,0:T(8,128)(2,1)S(1)} %collective-permute-done.3.refs_1_, ...), custom_call_target="tpu_custom_call" | custom-call | flops 1073741824 | bytes 10485760 | tf_op jit(solution)/shard_map/pallas_call | solution.py:67
  29.8 2.3 %copy-done.1 = bf16[2048,4096]{1,0:T(8,128)(2,1)S(1)} copy-done((bf16[2048,4096]{1,0:T(8,128)(2,1)S(1)}, bf16[2048,4096]{1,0:T(8,128)(2,1)}, u32[]{:S(2)}) %copy-start.1) | copy-done | bytes 16777240
  32.1 3.4 %shard_map.60 = f32[2048,128]{1,0:T(8,128)S(1)} custom-call(s32[8]{0:T(128)S(1)} %stack.62.columns_ref, bf16[2048,4096]{1,0:T(8,128)(2,1)S(1)} %copy-done.1, bf16[512,128]{1,0:T(8,128)(2,1)S(1)} %collective-permute-done.2.refs_0_, bf16[512,128]{1,0:T(8,128)(2,1)S(1)} %collective-permute-done.4.refs_1_, bf16[512,128]{1,0:T(8,128)(2,1)S(1)} %collective-permute-done.6.refs_2_, ...), custom_call_target="tpu_custom_call" | custom-call | flops 1073741824 | bytes 10485760 | tf_op jit(solution)/shard_map/pallas_call | solution.py:67
  35.6 25.5 %all_to_all.20 = f16[8,256,128]{2,1,0:T(8,128)(2,1)S(1)} all-to-all(f16[8,256,128]{2,1,0:T(8,128)(2,1)S(1)} %bitcast.20), channel_id=1, replica_groups=mesh['wide'=16,'narrow'=8] {'narrow'}, dimensions={0} | all-to-all | bytes 1048576 | tf_op jit(solution)/shard_map/all_to_all | solution.py:101
  63.0 3.2 %collective-permute-start.12 = (bf16[512,128]{1,0:T(8,128)(2,1)S(1)}, bf16[512,128]{1,0:T(8,128)(2,1)S(1)}, u32[]{:S(2)}, u32[]{:S(2)}) collective-permute-start(bf16[512,128]{1,0:T(8,128)(2,1)S(1)} %pad_maximum_fusion.1), channel_id=1, source_target_pairs={{0,16},{1,32},{2,48},{3,0},{4,80},{5,96},{6,112},{7,64},{8,88},{9,... | collective-permute-start | bytes 393224 | tf_op jit(solution)/shard_map/ppermute | solution.py:27
  66.8 1.3 collective-permute-done.16.refs_3_
  68.2 2.3 %collective-permute-start.17 = (bf16[512,128]{1,0:T(8,128)(2,1)S(1)}, bf16[512,128]{1,0:T(8,128)(2,1)S(1)}, u32[]{:S(2)}, u32[]{:S(2)}) collective-permute-start(bf16[512,128]{1,0:T(8,128)(2,1)S(1)} %collective-permute-done.16.refs_3_), channel_id=1, source_target_pairs={{0,8},{1,9},{2,10},{3,11},{4,12},{5,13},{6,14},{7,15},{8,0},{9,1},... | collective-permute-start | bytes 393224 | tf_op jit(solution)/shard_map/ppermute | solution.py:27
  70.4 2.0 %collective-permute-done.14.refs_2_ = bf16[512,128]{1,0:T(8,128)(2,1)S(1)} collective-permute-done((bf16[512,128]{1,0:T(8,128)(2,1)S(1)}, bf16[512,128]{1,0:T(8,128)(2,1)S(1)}, u32[]{:S(2)}, u32[]{:S(2)}) %collective-permute-start.14) | collective-permute-done | bytes 131104 | tf_op jit(solution)/shard_map/ppermute | solution.py:27
  73.9 3.4 %shard_map.61.refs_4_ = f32[2048,128]{1,0:T(8,128)S(1)} custom-call(s32[8]{0:T(128)S(1)} %stack.71.columns_ref, bf16[2048,4096]{1,0:T(8,128)(2,1)S(1)} %copy-done.1, bf16[512,128]{1,0:T(8,128)(2,1)S(1)} %collective-permute-done.10.refs_0_, bf16[512,128]{1,0:T(8,128)(2,1)S(1)} %collective-permute-done.12.refs_1_, ...), custom_call_target="tpu_custom_call" | custom-call | flops 1073741824 | bytes 10485760 | tf_op jit(solution)/shard_map/pallas_call | solution.py:67
  77.3 3.4 %shard_map.62 = f32[2048,128]{1,0:T(8,128)S(1)} custom-call(s32[8]{0:T(128)S(1)} %stack.62.columns_ref, bf16[2048,4096]{1,0:T(8,128)(2,1)S(1)} %copy-done.1, bf16[512,128]{1,0:T(8,128)(2,1)S(1)} %collective-permute-done.11.refs_0_, bf16[512,128]{1,0:T(8,128)(2,1)S(1)} %collective-permute-done.13.refs_1_, ...), custom_call_target="tpu_custom_call" | custom-call | flops 1073741824 | bytes 10485760 | tf_op jit(solution)/shard_map/pallas_call | solution.py:67
  80.8 22.3 %all_to_all.21 = f16[8,256,128]{2,1,0:T(8,128)(2,1)S(1)} all-to-all(f16[8,256,128]{2,1,0:T(8,128)(2,1)S(1)} %bitcast.21), channel_id=1, replica_groups=mesh['wide'=16,'narrow'=8] {'narrow'}, dimensions={0} | all-to-all | bytes 1048576 | tf_op jit(solution)/shard_map/all_to_all | solution.py:101
  105.9 2.0 %collective-permute-start.23 = (bf16[512,128]{1,0:T(8,128)(2,1)S(1)}, bf16[512,128]{1,0:T(8,128)(2,1)S(1)}, u32[]{:S(2)}, u32[]{:S(2)}) collective-permute-start(bf16[512,128]{1,0:T(8,128)(2,1)S(1)} %pad_maximum_fusion.2), channel_id=1, source_target_pairs={{0,32},{1,48},{2,0},{3,16},{4,96},{5,112},{6,64},{7,80},{8,104},{9... | collective-permute-start | bytes 393224 | tf_op jit(solution)/shard_map/ppermute | solution.py:27
  108.8 3.8 %collective-permute-done.25.refs_3_ = bf16[512,128]{1,0:T(8,128)(2,1)S(1)} collective-permute-done((bf16[512,128]{1,0:T(8,128)(2,1)S(1)}, bf16[512,128]{1,0:T(8,128)(2,1)S(1)}, u32[]{:S(2)}, u32[]{:S(2)}) %collective-permute-start.25) | collective-permute-done | bytes 131104 | tf_op jit(solution)/shard_map/ppermute | solution.py:27
  112.6 2.2 %collective-permute-start.24 = (bf16[512,128]{1,0:T(8,128)(2,1)S(1)}, bf16[512,128]{1,0:T(8,128)(2,1)S(1)}, u32[]{:S(2)}, u32[]{:S(2)}) collective-permute-start(bf16[512,128]{1,0:T(8,128)(2,1)S(1)} %collective-permute-done.23.refs_2_), channel_id=1, source_target_pairs={{0,8},{1,9},{2,10},{3,11},{4,12},{5,13},{6,14},{7,15},{8,0},{9,1},... | collective-permute-start | bytes 393224 | tf_op jit(solution)/shard_map/ppermute | solution.py:27
  114.8 2.0 %collective-permute-done.21.refs_1_ = bf16[512,128]{1,0:T(8,128)(2,1)S(1)} collective-permute-done((bf16[512,128]{1,0:T(8,128)(2,1)S(1)}, bf16[512,128]{1,0:T(8,128)(2,1)S(1)}, u32[]{:S(2)}, u32[]{:S(2)}) %collective-permute-start.21) | collective-permute-done | bytes 131104 | tf_op jit(solution)/shard_map/ppermute | solution.py:27
  117.3 3.4 %shard_map.63.refs_4_ = f32[2048,128]{1,0:T(8,128)S(1)} custom-call(s32[8]{0:T(128)S(1)} %stack.71.columns_ref, bf16[2048,4096]{1,0:T(8,128)(2,1)S(1)} %copy-done.1, bf16[512,128]{1,0:T(8,128)(2,1)S(1)} %collective-permute-done.19.refs_0_, bf16[512,128]{1,0:T(8,128)(2,1)S(1)} %collective-permute-done.21.refs_1_, ...), custom_call_target="tpu_custom_call" | custom-call | flops 1073741824 | bytes 10485760 | tf_op jit(solution)/shard_map/pallas_call | solution.py:67
  120.8 3.4 %shard_map.64 = f32[2048,128]{1,0:T(8,128)S(1)} custom-call(s32[8]{0:T(128)S(1)} %stack.62.columns_ref, bf16[2048,4096]{1,0:T(8,128)(2,1)S(1)} %copy-done.1, bf16[512,128]{1,0:T(8,128)(2,1)S(1)} %collective-permute-done.20.refs_0_, bf16[512,128]{1,0:T(8,128)(2,1)S(1)} %collective-permute-done.22.refs_1_, ...), custom_call_target="tpu_custom_call" | custom-call | flops 1073741824 | bytes 10485760 | tf_op jit(solution)/shard_map/pallas_call | solution.py:67
  124.3 22.9 %all_to_all.22 = f16[8,256,128]{2,1,0:T(8,128)(2,1)S(1)} all-to-all(f16[8,256,128]{2,1,0:T(8,128)(2,1)S(1)} %bitcast.22), channel_id=1, replica_groups=mesh['wide'=16,'narrow'=8] {'narrow'}, dimensions={0} | all-to-all | bytes 1048576 | tf_op jit(solution)/shard_map/all_to_all | solution.py:101
  148.8 1.5 collective-permute-start.34
  150.3 2.0 %collective-permute-start.32 = (bf16[512,128]{1,0:T(8,128)(2,1)S(1)}, bf16[512,128]{1,0:T(8,128)(2,1)S(1)}, u32[]{:S(2)}, u32[]{:S(2)}) collective-permute-start(bf16[512,128]{1,0:T(8,128)(2,1)S(1)} %pad_maximum_fusion.3), channel_id=1, source_target_pairs={{0,32},{1,48},{2,0},{3,16},{4,96},{5,112},{6,64},{7,80},{8,104},{9... | collective-permute-start | bytes 393224 | tf_op jit(solution)/shard_map/ppermute | solution.py:27
  152.9 4.1 %collective-permute-done.34.refs_3_ = bf16[512,128]{1,0:T(8,128)(2,1)S(1)} collective-permute-done((bf16[512,128]{1,0:T(8,128)(2,1)S(1)}, bf16[512,128]{1,0:T(8,128)(2,1)S(1)}, u32[]{:S(2)}, u32[]{:S(2)}) %collective-permute-start.34) | collective-permute-done | bytes 131104 | tf_op jit(solution)/shard_map/ppermute | solution.py:27
  157.0 1.9 collective-permute-done.32.refs_2_
  158.9 2.2 %collective-permute-done.30.refs_1_ = bf16[512,128]{1,0:T(8,128)(2,1)S(1)} collective-permute-done((bf16[512,128]{1,0:T(8,128)(2,1)S(1)}, bf16[512,128]{1,0:T(8,128)(2,1)S(1)}, u32[]{:S(2)}, u32[]{:S(2)}) %collective-permute-start.30) | collective-permute-done | bytes 131104 | tf_op jit(solution)/shard_map/ppermute | solution.py:27
  161.7 3.4 %shard_map.65.refs_4_ = f32[2048,128]{1,0:T(8,128)S(1)} custom-call(s32[8]{0:T(128)S(1)} %stack.71.columns_ref, bf16[2048,4096]{1,0:T(8,128)(2,1)S(1)} %copy-done.1, bf16[512,128]{1,0:T(8,128)(2,1)S(1)} %collective-permute-done.28.refs_0_, bf16[512,128]{1,0:T(8,128)(2,1)S(1)} %collective-permute-done.30.refs_1_, ...), custom_call_target="tpu_custom_call" | custom-call | flops 1073741824 | bytes 10485760 | tf_op jit(solution)/shard_map/pallas_call | solution.py:67
  165.1 3.4 %shard_map.66 = f32[2048,128]{1,0:T(8,128)S(1)} custom-call(s32[8]{0:T(128)S(1)} %stack.62.columns_ref, bf16[2048,4096]{1,0:T(8,128)(2,1)S(1)} %copy-done.1, bf16[512,128]{1,0:T(8,128)(2,1)S(1)} %collective-permute-done.29.refs_0_, bf16[512,128]{1,0:T(8,128)(2,1)S(1)} %collective-permute-done.31.refs_1_, ...), custom_call_target="tpu_custom_call" | custom-call | flops 1073741824 | bytes 10485760 | tf_op jit(solution)/shard_map/pallas_call | solution.py:67
  168.6 21.7 %all_to_all.23 = f16[8,256,128]{2,1,0:T(8,128)(2,1)S(1)} all-to-all(f16[8,256,128]{2,1,0:T(8,128)(2,1)S(1)} %bitcast.23), channel_id=1, replica_groups=mesh['wide'=16,'narrow'=8] {'narrow'}, dimensions={0} | all-to-all | bytes 1048576 | tf_op jit(solution)/shard_map/all_to_all | solution.py:101
  (81 shorter events, 15.4 us)
Async XLA Ops:
  2.9 8.6 %collective-permute-start.7 = (bf16[512,128]{1,0:T(8,128)(2,1)S(1)}, bf16[512,128]{1,0:T(8,128)(2,1)S(1)}, u32[]{:S(2)}, u32[]{:S(2)}) collective-permute-start(bf16[512,128]{1,0:T(8,128)(2,1)S(1)} %pad_maximum_fusion), channel_id=1, source_target_pairs={{0,48},{1,0},{2,16},{3,32},{4,112},{5,64},{6,80},{7,96},{8,120},{9... | collective-permute-start | bytes 393224 | tf_op jit(solution)/shard_map/ppermute | solution.py:27
  6.1 9.4 %collective-permute-start.5 = (bf16[512,128]{1,0:T(8,128)(2,1)S(1)}, bf16[512,128]{1,0:T(8,128)(2,1)S(1)}, u32[]{:S(2)}, u32[]{:S(2)}) collective-permute-start(bf16[512,128]{1,0:T(8,128)(2,1)S(1)} %pad_maximum_fusion), channel_id=1, source_target_pairs={{0,32},{1,48},{2,0},{3,16},{4,96},{5,112},{6,64},{7,80},{8,104},{9... | collective-permute-start | bytes 393224 | tf_op jit(solution)/shard_map/ppermute | solution.py:27
  10.8 7.1 %collective-permute-start.3 = (bf16[512,128]{1,0:T(8,128)(2,1)S(1)}, bf16[512,128]{1,0:T(8,128)(2,1)S(1)}, u32[]{:S(2)}, u32[]{:S(2)}) collective-permute-start(bf16[512,128]{1,0:T(8,128)(2,1)S(1)} %pad_maximum_fusion), channel_id=1, source_target_pairs={{0,16},{1,32},{2,48},{3,0},{4,80},{5,96},{6,112},{7,64},{8,88},{9,... | collective-permute-start | bytes 393224 | tf_op jit(solution)/shard_map/ppermute | solution.py:27
  10.9 9.5 %collective-permute-start.1 = (bf16[512,128]{1,0:T(8,128)(2,1)S(1)}, bf16[512,128]{1,0:T(8,128)(2,1)S(1)}, u32[]{:S(2)}, u32[]{:S(2)}) collective-permute-start(bf16[512,128]{1,0:T(8,128)(2,1)S(1)} %pad_maximum_fusion), channel_id=1, source_target_pairs={{0,0},{1,16},{2,32},{3,48},{4,64},{5,80},{6,96},{7,112},{8,72},{9,... | collective-permute-start | bytes 393224 | tf_op jit(solution)/shard_map/ppermute | solution.py:27
  11.5 18.2 %collective-permute-start.8 = (bf16[512,128]{1,0:T(8,128)(2,1)S(1)}, bf16[512,128]{1,0:T(8,128)(2,1)S(1)}, u32[]{:S(2)}, u32[]{:S(2)}) collective-permute-start(bf16[512,128]{1,0:T(8,128)(2,1)S(1)} %collective-permute-done.7.refs_3_), channel_id=1, source_target_pairs={{0,8},{1,9},{2,10},{3,11},{4,12},{5,13},{6,14},{7,15},{8,0},{9,1},... | collective-permute-start | bytes 393224 | tf_op jit(solution)/shard_map/ppermute | solution.py:27
  15.5 14.2 %collective-permute-start.6 = (bf16[512,128]{1,0:T(8,128)(2,1)S(1)}, bf16[512,128]{1,0:T(8,128)(2,1)S(1)}, u32[]{:S(2)}, u32[]{:S(2)}) collective-permute-start(bf16[512,128]{1,0:T(8,128)(2,1)S(1)} %collective-permute-done.5.refs_2_), channel_id=1, source_target_pairs={{0,8},{1,9},{2,10},{3,11},{4,12},{5,13},{6,14},{7,15},{8,0},{9,1},... | collective-permute-start | bytes 393224 | tf_op jit(solution)/shard_map/ppermute | solution.py:27
  17.9 11.8 %collective-permute-start.4 = (bf16[512,128]{1,0:T(8,128)(2,1)S(1)}, bf16[512,128]{1,0:T(8,128)(2,1)S(1)}, u32[]{:S(2)}, u32[]{:S(2)}) collective-permute-start(bf16[512,128]{1,0:T(8,128)(2,1)S(1)} %collective-permute-done.3.refs_1_), channel_id=1, source_target_pairs={{0,8},{1,9},{2,10},{3,11},{4,12},{5,13},{6,14},{7,15},{8,0},{9,1},... | collective-permute-start | bytes 393224 | tf_op jit(solution)/shard_map/ppermute | solution.py:27
  20.4 9.4 %collective-permute-start.2 = (bf16[512,128]{1,0:T(8,128)(2,1)S(1)}, bf16[512,128]{1,0:T(8,128)(2,1)S(1)}, u32[]{:S(2)}, u32[]{:S(2)}) collective-permute-start(bf16[512,128]{1,0:T(8,128)(2,1)S(1)} %collective-permute-done.1.refs_0_), channel_id=1, source_target_pairs={{0,8},{1,9},{2,10},{3,11},{4,12},{5,13},{6,14},{7,15},{8,0},{9,1},... | collective-permute-start | bytes 393224 | tf_op jit(solution)/shard_map/ppermute | solution.py:27
  62.7 5.5 %collective-permute-start.16 = (bf16[512,128]{1,0:T(8,128)(2,1)S(1)}, bf16[512,128]{1,0:T(8,128)(2,1)S(1)}, u32[]{:S(2)}, u32[]{:S(2)}) collective-permute-start(bf16[512,128]{1,0:T(8,128)(2,1)S(1)} %pad_maximum_fusion.1), channel_id=1, source_target_pairs={{0,48},{1,0},{2,16},{3,32},{4,112},{5,64},{6,80},{7,96},{8,120},{9... | collective-permute-start | bytes 393224 | tf_op jit(solution)/shard_map/ppermute | solution.py:27
  62.8 9.7 %collective-permute-start.14 = (bf16[512,128]{1,0:T(8,128)(2,1)S(1)}, bf16[512,128]{1,0:T(8,128)(2,1)S(1)}, u32[]{:S(2)}, u32[]{:S(2)}) collective-permute-start(bf16[512,128]{1,0:T(8,128)(2,1)S(1)} %pad_maximum_fusion.1), channel_id=1, source_target_pairs={{0,32},{1,48},{2,0},{3,16},{4,96},{5,112},{6,64},{7,80},{8,104},{9... | collective-permute-start | bytes 393224 | tf_op jit(solution)/shard_map/ppermute | solution.py:27
  63.0 10.4 %collective-permute-start.12 = (bf16[512,128]{1,0:T(8,128)(2,1)S(1)}, bf16[512,128]{1,0:T(8,128)(2,1)S(1)}, u32[]{:S(2)}, u32[]{:S(2)}) collective-permute-start(bf16[512,128]{1,0:T(8,128)(2,1)S(1)} %pad_maximum_fusion.1), channel_id=1, source_target_pairs={{0,16},{1,32},{2,48},{3,0},{4,80},{5,96},{6,112},{7,64},{8,88},{9,... | collective-permute-start | bytes 393224 | tf_op jit(solution)/shard_map/ppermute | solution.py:27
  66.1 7.2 %collective-permute-start.10 = (bf16[512,128]{1,0:T(8,128)(2,1)S(1)}, bf16[512,128]{1,0:T(8,128)(2,1)S(1)}, u32[]{:S(2)}, u32[]{:S(2)}) collective-permute-start(bf16[512,128]{1,0:T(8,128)(2,1)S(1)} %pad_maximum_fusion.1), channel_id=1, source_target_pairs={{0,0},{1,16},{2,32},{3,48},{4,64},{5,80},{6,96},{7,112},{8,72},{9,... | collective-permute-start | bytes 393224 | tf_op jit(solution)/shard_map/ppermute | solution.py:27
  68.2 9.1 %collective-permute-start.17 = (bf16[512,128]{1,0:T(8,128)(2,1)S(1)}, bf16[512,128]{1,0:T(8,128)(2,1)S(1)}, u32[]{:S(2)}, u32[]{:S(2)}) collective-permute-start(bf16[512,128]{1,0:T(8,128)(2,1)S(1)} %collective-permute-done.16.refs_3_), channel_id=1, source_target_pairs={{0,8},{1,9},{2,10},{3,11},{4,12},{5,13},{6,14},{7,15},{8,0},{9,1},... | collective-permute-start | bytes 393224 | tf_op jit(solution)/shard_map/ppermute | solution.py:27
  72.5 4.8 %collective-permute-start.15 = (bf16[512,128]{1,0:T(8,128)(2,1)S(1)}, bf16[512,128]{1,0:T(8,128)(2,1)S(1)}, u32[]{:S(2)}, u32[]{:S(2)}) collective-permute-start(bf16[512,128]{1,0:T(8,128)(2,1)S(1)} %collective-permute-done.14.refs_2_), channel_id=1, source_target_pairs={{0,8},{1,9},{2,10},{3,11},{4,12},{5,13},{6,14},{7,15},{8,0},{9,1},... | collective-permute-start | bytes 393224 | tf_op jit(solution)/shard_map/ppermute | solution.py:27
  73.4 3.9 %collective-permute-start.13 = (bf16[512,128]{1,0:T(8,128)(2,1)S(1)}, bf16[512,128]{1,0:T(8,128)(2,1)S(1)}, u32[]{:S(2)}, u32[]{:S(2)}) collective-permute-start(bf16[512,128]{1,0:T(8,128)(2,1)S(1)} %collective-permute-done.12.refs_1_), channel_id=1, source_target_pairs={{0,8},{1,9},{2,10},{3,11},{4,12},{5,13},{6,14},{7,15},{8,0},{9,1},... | collective-permute-start | bytes 393224 | tf_op jit(solution)/shard_map/ppermute | solution.py:27
  73.4 3.9 %collective-permute-start.11 = (bf16[512,128]{1,0:T(8,128)(2,1)S(1)}, bf16[512,128]{1,0:T(8,128)(2,1)S(1)}, u32[]{:S(2)}, u32[]{:S(2)}) collective-permute-start(bf16[512,128]{1,0:T(8,128)(2,1)S(1)} %collective-permute-done.10.refs_0_), channel_id=1, source_target_pairs={{0,8},{1,9},{2,10},{3,11},{4,12},{5,13},{6,14},{7,15},{8,0},{9,1},... | collective-permute-start | bytes 393224 | tf_op jit(solution)/shard_map/ppermute | solution.py:27
  104.7 7.9 %collective-permute-start.25 = (bf16[512,128]{1,0:T(8,128)(2,1)S(1)}, bf16[512,128]{1,0:T(8,128)(2,1)S(1)}, u32[]{:S(2)}, u32[]{:S(2)}) collective-permute-start(bf16[512,128]{1,0:T(8,128)(2,1)S(1)} %pad_maximum_fusion.2), channel_id=1, source_target_pairs={{0,48},{1,0},{2,16},{3,32},{4,112},{5,64},{6,80},{7,96},{8,120},{9... | collective-permute-start | bytes 393224 | tf_op jit(solution)/shard_map/ppermute | solution.py:27
  105.9 6.7 %collective-permute-start.23 = (bf16[512,128]{1,0:T(8,128)(2,1)S(1)}, bf16[512,128]{1,0:T(8,128)(2,1)S(1)}, u32[]{:S(2)}, u32[]{:S(2)}) collective-permute-start(bf16[512,128]{1,0:T(8,128)(2,1)S(1)} %pad_maximum_fusion.2), channel_id=1, source_target_pairs={{0,32},{1,48},{2,0},{3,16},{4,96},{5,112},{6,64},{7,80},{8,104},{9... | collective-permute-start | bytes 393224 | tf_op jit(solution)/shard_map/ppermute | solution.py:27
  107.8 9.0 %collective-permute-start.21 = (bf16[512,128]{1,0:T(8,128)(2,1)S(1)}, bf16[512,128]{1,0:T(8,128)(2,1)S(1)}, u32[]{:S(2)}, u32[]{:S(2)}) collective-permute-start(bf16[512,128]{1,0:T(8,128)(2,1)S(1)} %pad_maximum_fusion.2), channel_id=1, source_target_pairs={{0,16},{1,32},{2,48},{3,0},{4,80},{5,96},{6,112},{7,64},{8,88},{9,... | collective-permute-start | bytes 393224 | tf_op jit(solution)/shard_map/ppermute | solution.py:27
  108.2 8.7 %collective-permute-start.19 = (bf16[512,128]{1,0:T(8,128)(2,1)S(1)}, bf16[512,128]{1,0:T(8,128)(2,1)S(1)}, u32[]{:S(2)}, u32[]{:S(2)}) collective-permute-start(bf16[512,128]{1,0:T(8,128)(2,1)S(1)} %pad_maximum_fusion.2), channel_id=1, source_target_pairs={{0,0},{1,16},{2,32},{3,48},{4,64},{5,80},{6,96},{7,112},{8,72},{9,... | collective-permute-start | bytes 393224 | tf_op jit(solution)/shard_map/ppermute | solution.py:27
  112.6 8.1 %collective-permute-start.26 = (bf16[512,128]{1,0:T(8,128)(2,1)S(1)}, bf16[512,128]{1,0:T(8,128)(2,1)S(1)}, u32[]{:S(2)}, u32[]{:S(2)}) collective-permute-start(bf16[512,128]{1,0:T(8,128)(2,1)S(1)} %collective-permute-done.25.refs_3_), channel_id=1, source_target_pairs={{0,8},{1,9},{2,10},{3,11},{4,12},{5,13},{6,14},{7,15},{8,0},{9,1},... | collective-permute-start | bytes 393224 | tf_op jit(solution)/shard_map/ppermute | solution.py:27
  112.6 8.1 %collective-permute-start.24 = (bf16[512,128]{1,0:T(8,128)(2,1)S(1)}, bf16[512,128]{1,0:T(8,128)(2,1)S(1)}, u32[]{:S(2)}, u32[]{:S(2)}) collective-permute-start(bf16[512,128]{1,0:T(8,128)(2,1)S(1)} %collective-permute-done.23.refs_2_), channel_id=1, source_target_pairs={{0,8},{1,9},{2,10},{3,11},{4,12},{5,13},{6,14},{7,15},{8,0},{9,1},... | collective-permute-start | bytes 393224 | tf_op jit(solution)/shard_map/ppermute | solution.py:27
  116.8 3.9 %collective-permute-start.22 = (bf16[512,128]{1,0:T(8,128)(2,1)S(1)}, bf16[512,128]{1,0:T(8,128)(2,1)S(1)}, u32[]{:S(2)}, u32[]{:S(2)}) collective-permute-start(bf16[512,128]{1,0:T(8,128)(2,1)S(1)} %collective-permute-done.21.refs_1_), channel_id=1, source_target_pairs={{0,8},{1,9},{2,10},{3,11},{4,12},{5,13},{6,14},{7,15},{8,0},{9,1},... | collective-permute-start | bytes 393224 | tf_op jit(solution)/shard_map/ppermute | solution.py:27
  116.8 3.9 %collective-permute-start.20 = (bf16[512,128]{1,0:T(8,128)(2,1)S(1)}, bf16[512,128]{1,0:T(8,128)(2,1)S(1)}, u32[]{:S(2)}, u32[]{:S(2)}) collective-permute-start(bf16[512,128]{1,0:T(8,128)(2,1)S(1)} %collective-permute-done.19.refs_0_), channel_id=1, source_target_pairs={{0,8},{1,9},{2,10},{3,11},{4,12},{5,13},{6,14},{7,15},{8,0},{9,1},... | collective-permute-start | bytes 393224 | tf_op jit(solution)/shard_map/ppermute | solution.py:27
  148.8 8.2 %collective-permute-start.34 = (bf16[512,128]{1,0:T(8,128)(2,1)S(1)}, bf16[512,128]{1,0:T(8,128)(2,1)S(1)}, u32[]{:S(2)}, u32[]{:S(2)}) collective-permute-start(bf16[512,128]{1,0:T(8,128)(2,1)S(1)} %pad_maximum_fusion.3), channel_id=1, source_target_pairs={{0,48},{1,0},{2,16},{3,32},{4,112},{5,64},{6,80},{7,96},{8,120},{9... | collective-permute-start | bytes 393224 | tf_op jit(solution)/shard_map/ppermute | solution.py:27
  150.3 8.6 %collective-permute-start.32 = (bf16[512,128]{1,0:T(8,128)(2,1)S(1)}, bf16[512,128]{1,0:T(8,128)(2,1)S(1)}, u32[]{:S(2)}, u32[]{:S(2)}) collective-permute-start(bf16[512,128]{1,0:T(8,128)(2,1)S(1)} %pad_maximum_fusion.3), channel_id=1, source_target_pairs={{0,32},{1,48},{2,0},{3,16},{4,96},{5,112},{6,64},{7,80},{8,104},{9... | collective-permute-start | bytes 393224 | tf_op jit(solution)/shard_map/ppermute | solution.py:27
  152.2 8.9 %collective-permute-start.30 = (bf16[512,128]{1,0:T(8,128)(2,1)S(1)}, bf16[512,128]{1,0:T(8,128)(2,1)S(1)}, u32[]{:S(2)}, u32[]{:S(2)}) collective-permute-start(bf16[512,128]{1,0:T(8,128)(2,1)S(1)} %pad_maximum_fusion.3), channel_id=1, source_target_pairs={{0,16},{1,32},{2,48},{3,0},{4,80},{5,96},{6,112},{7,64},{8,88},{9,... | collective-permute-start | bytes 393224 | tf_op jit(solution)/shard_map/ppermute | solution.py:27
  152.2 8.9 %collective-permute-start.28 = (bf16[512,128]{1,0:T(8,128)(2,1)S(1)}, bf16[512,128]{1,0:T(8,128)(2,1)S(1)}, u32[]{:S(2)}, u32[]{:S(2)}) collective-permute-start(bf16[512,128]{1,0:T(8,128)(2,1)S(1)} %pad_maximum_fusion.3), channel_id=1, source_target_pairs={{0,0},{1,16},{2,32},{3,48},{4,64},{5,80},{6,96},{7,112},{8,72},{9,... | collective-permute-start | bytes 393224 | tf_op jit(solution)/shard_map/ppermute | solution.py:27
  157.0 8.1 %collective-permute-start.35 = (bf16[512,128]{1,0:T(8,128)(2,1)S(1)}, bf16[512,128]{1,0:T(8,128)(2,1)S(1)}, u32[]{:S(2)}, u32[]{:S(2)}) collective-permute-start(bf16[512,128]{1,0:T(8,128)(2,1)S(1)} %collective-permute-done.34.refs_3_), channel_id=1, source_target_pairs={{0,8},{1,9},{2,10},{3,11},{4,12},{5,13},{6,14},{7,15},{8,0},{9,1},... | collective-permute-start | bytes 393224 | tf_op jit(solution)/shard_map/ppermute | solution.py:27
  158.9 6.2 %collective-permute-start.33 = (bf16[512,128]{1,0:T(8,128)(2,1)S(1)}, bf16[512,128]{1,0:T(8,128)(2,1)S(1)}, u32[]{:S(2)}, u32[]{:S(2)}) collective-permute-start(bf16[512,128]{1,0:T(8,128)(2,1)S(1)} %collective-permute-done.32.refs_2_), channel_id=1, source_target_pairs={{0,8},{1,9},{2,10},{3,11},{4,12},{5,13},{6,14},{7,15},{8,0},{9,1},... | collective-permute-start | bytes 393224 | tf_op jit(solution)/shard_map/ppermute | solution.py:27
  161.1 3.9 %collective-permute-start.31 = (bf16[512,128]{1,0:T(8,128)(2,1)S(1)}, bf16[512,128]{1,0:T(8,128)(2,1)S(1)}, u32[]{:S(2)}, u32[]{:S(2)}) collective-permute-start(bf16[512,128]{1,0:T(8,128)(2,1)S(1)} %collective-permute-done.30.refs_1_), channel_id=1, source_target_pairs={{0,8},{1,9},{2,10},{3,11},{4,12},{5,13},{6,14},{7,15},{8,0},{9,1},... | collective-permute-start | bytes 393224 | tf_op jit(solution)/shard_map/ppermute | solution.py:27
  161.2 3.9 %collective-permute-start.29 = (bf16[512,128]{1,0:T(8,128)(2,1)S(1)}, bf16[512,128]{1,0:T(8,128)(2,1)S(1)}, u32[]{:S(2)}, u32[]{:S(2)}) collective-permute-start(bf16[512,128]{1,0:T(8,128)(2,1)S(1)} %collective-permute-done.28.refs_0_), channel_id=1, source_target_pairs={{0,8},{1,9},{2,10},{3,11},{4,12},{5,13},{6,14},{7,15},{8,0},{9,1},... | collective-permute-start | bytes 393224 | tf_op jit(solution)/shard_map/ppermute | solution.py:27
  (9 other events, 121.5 us)

commit v2 on v0

v2 whole, which is shorter than its diff:
```python
import functools

import jax
import jax.numpy as jnp
from jax import lax
from jax.experimental import pallas as pl
from jax.experimental.pallas import tpu as pltpu
from jax.sharding import PartitionSpec as P

STEPS = 4
AXES = ("wide", "narrow")
REPLICAS = 128
PIECE = 256
SCALE = 256.0

time_step = 1.25
coupling_scale = 0.5


def shifted(block, shift):
    return (block // 4 ^ shift // 4) * 4 + (block % 4 + shift % 4) % 4


def permuted(array, place):
    pairs = []
    for w in range(16):
        for n in range(8):
            to_w, to_n = place(w, n)
            pairs.append((w * 8 + n, to_w * 8 + to_n))
    return lax.ppermute(array, AXES, pairs)


def other_core(w, n):
    return w ^ 1, n


def to_users(turn):
    def place(w, n):
        core = w % 2
        return shifted(n, turn + 4 * core) * 2 + core, w // 2

    return place


def multiply(wide_ref, coupling_ref, *refs, terms, add, stream):
    refs = list(refs)
    if stream:
        arrived, held_ref = refs.pop(), refs.pop()
    out_ref = refs.pop()
    total_ref = refs.pop() if add else None
    rows = out_ref.shape[0]
    tile = 512
    chip, core = wide_ref[0] // 2, wide_ref[0] % 2
    spans = []
    for turn, crossed in terms:
        sender = 1 - core if crossed else core
        piece = (chip // 4 ^ sender) * 4 + (chip % 4 + 4 - turn) % 4
        for half in (sender, 1 - sender):
            spans.append(pl.ds(pl.multiple_of(half * 2048 + piece * PIECE, PIECE), PIECE))
    copies = []
    if stream:
        for index, columns in enumerate(spans):
            copies.append(
                pltpu.make_async_copy(coupling_ref.at[:, columns], held_ref.at[index], arrived.at[index])
            )
            copies[-1].start()
    for index, piece_ref in enumerate(refs):
        for copy in copies[2 * index : 2 * index + 2]:
            copy.wait()
        for first in range(0, rows, tile):
            span = pl.ds(first, tile)
            blocks = []
            for k in (2 * index, 2 * index + 1):
                blocks.append(held_ref[k, span, :] if stream else coupling_ref[span, spans[k]])
            term = jnp.dot(blocks[0], piece_ref[:PIECE, :], preferred_element_type=jnp.float32)
            term += jnp.dot(blocks[1], piece_ref[PIECE:, :], preferred_element_type=jnp.float32)
            if index > 0:
                term += out_ref[span, :]
            elif add:
                term += total_ref[span, :]
            out_ref[span, :] = term


def product(wide, coupling, terms, pieces, total=None, stream=False):
    operands = [*pieces] + ([] if total is None else [total])
    rows = coupling.shape[0]
    depth = 2 * PIECE * len(pieces)
    space = pltpu.HBM if stream else pltpu.VMEM
    scratch = []
    if stream:
        scratch = [
            pltpu.VMEM((depth // PIECE, rows, PIECE), coupling.dtype),
            pltpu.SemaphoreType.DMA((depth // PIECE,)),
        ]
    return pl.pallas_call(
        functools.partial(multiply, terms=terms, add=total is not None, stream=stream),
        out_shape=jax.ShapeDtypeStruct((rows, REPLICAS), jnp.float32),
        in_specs=[pl.BlockSpec(memory_space=pltpu.SMEM), pl.BlockSpec(memory_space=space)]
        + [pl.BlockSpec(memory_space=pltpu.VMEM)] * len(operands),
        out_specs=pl.BlockSpec(memory_space=pltpu.VMEM),
        scratch_shapes=scratch,
        compiler_params=pltpu.CompilerParams(vmem_limit_bytes=(16 if stream else 8) << 20),
        cost_estimate=pl.CostEstimate(
            flops=2 * rows * depth * REPLICAS, bytes_accessed=rows * depth * 2, transcendentals=0
        ),
    )(wide, pltpu.with_memory_space_constraint(coupling, space), *operands)


def on_device(coupling, hashes, momentum, linear):
    wide = lax.axis_index("wide").astype(jnp.int32).reshape(1)
    positions = (hashes.astype(jnp.float32) - 32768.0) / 65536.0
    lowered = positions.astype(jnp.bfloat16)
    velocity = momentum
    linear_term = linear[:, None]
    for step_index in range(STEPS):
        chip = jnp.concatenate([lowered, permuted(lowered, other_core)])
        turns = (1, 3, 2, 0)
        own = [permuted(chip, to_users(turn)) for turn in turns]
        stream = step_index == 0
        other = [permuted(piece, other_core) for piece in own[:3]]
        total = product(wide, coupling, [(turn, False) for turn in turns[:3]], own[:3], None, stream)
        last, total = lax.optimization_barrier((own[3], total))
        other.append(permuted(last, other_core))
        terms = [(turns[3], False)] + [(turn, True) for turn in turns[:3]]
        total = product(wide, coupling, terms, [last, *other[:3]], total, stream)
        total = product(wide, coupling, [(turns[3], True)], other[3:], total, stream)
        sent = (total * SCALE).astype(jnp.float16)
        parts = lax.all_to_all(sent.reshape(8, PIECE, REPLICAS), "narrow", 0, 0)
        local_field = jnp.sum(parts.astype(jnp.float32), axis=0) / SCALE
        pump_level = (step_index + 1.0) / (STEPS + 1.0)
        velocity = velocity + time_step * (
            -(1.0 - pump_level) * positions + coupling_scale * (local_field + linear_term)
        )
        moved = positions + time_step * velocity
        clamped = jnp.clip(moved, -1.0, 1.0)
        velocity = velocity - (moved - clamped) / time_step
        positions = clamped
        lowered = positions.astype(jnp.bfloat16)
    return (positions, velocity)


def solution(mesh):
    return jax.shard_map(
        on_device,
        mesh=mesh,
        in_specs=(
            P("wide", "narrow"),
            P(("wide", "narrow"), None),
            P(("wide", "narrow"), None),
            P(("wide", "narrow")),
        ),
        out_specs=(P(("wide", "narrow"), None), P(("wide", "narrow"), None)),
        check_vma=False,
    )
```

time: 720 us -> 175 us (0.24)
  waiting for transfers between devices: 498 us -> 21.8 us
  blocking collectives: 149 us -> 89.1 us
  matrix products: 51.3 us -> 0 us
  starting transfers between devices: 0.51 us -> 34.3 us
  Pallas kernels: 0 us -> 25.5 us
  between operations: 14.2 us -> 1.15 us
    reduce_scatter x4 -> x0, waiting for transfers between devices: 291 us -> none  [on_device(): lax.psum_scatter(jnp.dot(coupling, column_block, preferred_element_type=j...]
    all_gather x4 -> x0, waiting for transfers between devices: 207 us -> none  [on_device(): everything = lax.all_gather(row_block, 'wide', axis=0, tiled=True)]
    all_gather x4 -> x0, blocking collectives: 149 us -> none  [on_device(): row_block = lax.all_gather(lowered, 'narrow', axis=0, tiled=True)]
    all_to_all x0 -> x4, blocking collectives: none -> 89.1 us  [on_device(): parts = lax.all_to_all(sent.reshape(8, PIECE, REPLICAS), 'narrow', 0, 0)]
    dot_general x4 -> x0, matrix products: 51.3 us -> none  [on_device(): jnp.dot(coupling, column_block, preferred_element_type=jnp.float32)]
    ppermute x0 -> x36, starting transfers between devices: none -> 34.3 us  [permuted(): return lax.ppermute(array, AXES, pairs)]
    pallas_call x0 -> x12, Pallas kernels: none -> 25.5 us  [product(): pl.pallas_call(functools.partial(multiply, terms=terms, add=total is not...]
    ppermute x0 -> x36, waiting for transfers between devices: none -> 21.8 us  [permuted(): return lax.ppermute(array, AXES, pairs)]
  transfers between devices with their start and end apart: 8 -> 36, of which waited for: 8 -> 11; matrix products, arithmetic and copies ran while one was open for 0% -> 0% of each run, Pallas kernels for 0% -> 12%
where the time goes in v2:
time: 175 us
  blocking collectives  89.1 us (51%)
  starting transfers between devices  34.3 us (20%)
  Pallas kernels  25.5 us (15%)
  waiting for transfers between devices  21.8 us (12%)
  other arithmetic  2.98 us (2%)
    all_to_all x4, blocking collectives, on_device(): parts = lax.all_to_all(sent.reshape(8, PIECE, REPLICAS), 'narrow', 0, 0)  89.1 us
    ppermute x36, starting transfers between devices, permuted(): return lax.ppermute(array, AXES, pairs)  34.3 us
    pallas_call x12, Pallas kernels, product(): pl.pallas_call(functools.partial(multiply, terms=terms, add=total is not...  25.5 us
    ppermute x36, waiting for transfers between devices, permuted(): return lax.ppermute(array, AXES, pairs)  21.8 us
  transfers between devices with their start and end apart: 36, of which 11 were waited for; matrix products, arithmetic and copies ran while one was open for 0% of the time, Pallas kernels for 12%

profile of v2, /device:TPU:0, one launch (start us, length us, event | category | flops | bytes accessed | tf_op | source)
XLA Modules:
  0.0 174.9 jit_solution(14327687489849441373)
XLA Ops:
  1.7 1.2 collective-permute-done
  2.9 3.3 %collective-permute-start.4 = (bf16[512,128]{1,0:T(8,128)(2,1)S(1)}, bf16[512,128]{1,0:T(8,128)(2,1)S(1)}, u32[]{:S(2)}, u32[]{:S(2)}) collective-permute-start(bf16[512,128]{1,0:T(8,128)(2,1)S(1)} %pad_maximum_fusion), channel_id=1, source_target_pairs={{0,32},{1,48},{2,0},{3,16},{4,96},{5,112},{6,64},{7,80},{8,104},{9... | collective-permute-start | bytes 393224 | tf_op jit(solution)/shard_map/ppermute | solution.py:30
  6.3 4.0 %collective-permute-start.3 = (bf16[512,128]{1,0:T(8,128)(2,1)S(1)}, bf16[512,128]{1,0:T(8,128)(2,1)S(1)}, u32[]{:S(2)}, u32[]{:S(2)}) collective-permute-start(bf16[512,128]{1,0:T(8,128)(2,1)S(1)} %pad_maximum_fusion), channel_id=1, source_target_pairs={{0,48},{1,0},{2,16},{3,32},{4,112},{5,64},{6,80},{7,96},{8,120},{9... | collective-permute-start | bytes 393224 | tf_op jit(solution)/shard_map/ppermute | solution.py:30
  11.9 3.6 %collective-permute-start.8 = (bf16[512,128]{1,0:T(8,128)(2,1)S(1)}, bf16[512,128]{1,0:T(8,128)(2,1)S(1)}, u32[]{:S(2)}, u32[]{:S(2)}) collective-permute-start(bf16[512,128]{1,0:T(8,128)(2,1)S(1)} %collective-permute-done.4.refs_2_), channel_id=1, source_target_pairs={{0,8},{1,9},{2,10},{3,11},{4,12},{5,13},{6,14},{7,15},{8,0},{9,1},... | collective-permute-start | bytes 393224 | tf_op jit(solution)/shard_map/ppermute | solution.py:30
  15.6 1.5 collective-permute-done.3.refs_1_
  17.0 2.8 %collective-permute-start.6 = (bf16[512,128]{1,0:T(8,128)(2,1)S(1)}, bf16[512,128]{1,0:T(8,128)(2,1)S(1)}, u32[]{:S(2)}, u32[]{:S(2)}) collective-permute-start(bf16[512,128]{1,0:T(8,128)(2,1)S(1)} %collective-permute-done.2.refs_0_), channel_id=1, source_target_pairs={{0,8},{1,9},{2,10},{3,11},{4,12},{5,13},{6,14},{7,15},{8,0},{9,1},... | collective-permute-start | bytes 393224 | tf_op jit(solution)/shard_map/ppermute | solution.py:30
  19.8 3.6 %shard_map.59.refs_4_ = f32[2048,128]{1,0:T(8,128)S(1)} custom-call(s32[1]{0:T(128)} %bitcast.wide_ref, bf16[2048,4096]{1,0:T(8,128)(2,1)} %coupling_ref.23, bf16[512,128]{1,0:T(8,128)(2,1)S(1)} %collective-permute-done.2.refs_0_, bf16[512,128]{1,0:T(8,128)(2,1)S(1)} %collective-permute-done.3.refs_1_, bf16[512,128]{1,0:T(8,128)(2,1)S(1)} %collective-permute-done.4.refs_2_), custom_call_target="tpu_custom_call" | custom-call | flops 805306368 | bytes 6291456 | tf_op jit(solution)/shard_map/pallas_call | solution.py:95
  23.7 4.5 %shard_map.60.refs_1_ = f32[2048,128]{1,0:T(8,128)S(1)} custom-call(s32[1]{0:T(128)} %bitcast.wide_ref, bf16[2048,4096]{1,0:T(8,128)(2,1)} %coupling_ref.23, bf16[512,128]{1,0:T(8,128)(2,1)S(1)} %collective-permute-done.1.refs_0_, bf16[512,128]{1,0:T(8,128)(2,1)S(1)} %collective-permute-done.6.refs_1_, bf16[512,128]{1,0:T(8,128)(2,1)S(1)} %collective-permute-done.7.refs_2_, ...), custom_call_target="tpu_custom_call" | custom-call | flops 1073741824 | bytes 8388608 | tf_op jit(solution)/shard_map/pallas_call | solution.py:95
  28.2 2.8 %shard_map.61 = f32[2048,128]{1,0:T(8,128)S(1)} custom-call(s32[1]{0:T(128)} %bitcast.wide_ref, bf16[2048,4096]{1,0:T(8,128)(2,1)} %coupling_ref.23, bf16[512,128]{1,0:T(8,128)(2,1)S(1)} %collective-permute-done.5.refs_0_, f32[2048,128]{1,0:T(8,128)S(1)} %shard_map.60.refs_1_), custom_call_target="tpu_custom_call" | custom-call | flops 268435456 | bytes 2097152 | tf_op jit(solution)/shard_map/pallas_call | solution.py:95
  31.2 21.4 %all_to_all.20 = f16[8,256,128]{2,1,0:T(8,128)(2,1)S(1)} all-to-all(f16[8,256,128]{2,1,0:T(8,128)(2,1)S(1)} %bitcast.7), channel_id=1, replica_groups=mesh['wide'=16,'narrow'=8] {'narrow'}, dimensions={0} | all-to-all | bytes 1048576 | tf_op jit(solution)/shard_map/all_to_all | solution.py:128
  52.9 1.2 collective-permute-done.9
  56.7 4.1 %collective-permute-done.13.refs_2_ = bf16[512,128]{1,0:T(8,128)(2,1)S(1)} collective-permute-done((bf16[512,128]{1,0:T(8,128)(2,1)S(1)}, bf16[512,128]{1,0:T(8,128)(2,1)S(1)}, u32[]{:S(2)}, u32[]{:S(2)}) %collective-permute-start.13) | collective-permute-done | bytes 131104 | tf_op jit(solution)/shard_map/ppermute | solution.py:30
  60.8 2.0 %collective-permute-start.17 = (bf16[512,128]{1,0:T(8,128)(2,1)S(1)}, bf16[512,128]{1,0:T(8,128)(2,1)S(1)}, u32[]{:S(2)}, u32[]{:S(2)}) collective-permute-start(bf16[512,128]{1,0:T(8,128)(2,1)S(1)} %collective-permute-done.13.refs_2_), channel_id=1, source_target_pairs={{0,8},{1,9},{2,10},{3,11},{4,12},{5,13},{6,14},{7,15},{8,0},{9,1},... | collective-permute-start | bytes 393224 | tf_op jit(solution)/shard_map/ppermute | solution.py:30
  62.9 2.1 %collective-permute-done.11.refs_0_ = bf16[512,128]{1,0:T(8,128)(2,1)S(1)} collective-permute-done((bf16[512,128]{1,0:T(8,128)(2,1)S(1)}, bf16[512,128]{1,0:T(8,128)(2,1)S(1)}, u32[]{:S(2)}, u32[]{:S(2)}) %collective-permute-start.11) | collective-permute-done | bytes 131104 | tf_op jit(solution)/shard_map/ppermute | solution.py:30
  65.0 1.8 %shard_map.62.refs_4_ = f32[2048,128]{1,0:T(8,128)S(1)} custom-call(s32[1]{0:T(128)} %bitcast.wide_ref, bf16[2048,4096]{1,0:T(8,128)(2,1)S(1)} %bitcast.6, bf16[512,128]{1,0:T(8,128)(2,1)S(1)} %collective-permute-done.11.refs_0_, bf16[512,128]{1,0:T(8,128)(2,1)S(1)} %collective-permute-done.12.refs_1_, bf16[512,128]{1,0:T(8,128)(2,1)S(1)} %collective-permute-done.13.refs_2_), custom_call_target="tpu_custom_call" | custom-call | flops 805306368 | bytes 6291456 | tf_op jit(solution)/shard_map/pallas_call | solution.py:95
  67.5 2.3 %shard_map.63.refs_1_ = f32[2048,128]{1,0:T(8,128)S(1)} custom-call(s32[1]{0:T(128)} %bitcast.wide_ref, bf16[2048,4096]{1,0:T(8,128)(2,1)S(1)} %bitcast.6, bf16[512,128]{1,0:T(8,128)(2,1)S(1)} %collective-permute-done.10.refs_0_, bf16[512,128]{1,0:T(8,128)(2,1)S(1)} %collective-permute-done.15.refs_1_, bf16[512,128]{1,0:T(8,128)(2,1)S(1)} %collective-permute-done.16.refs_2_, ...), custom_call_target="tpu_custom_call" | custom-call | flops 1073741824 | bytes 8388608 | tf_op jit(solution)/shard_map/pallas_call | solution.py:95
  70.7 21.2 %all_to_all.21 = f16[8,256,128]{2,1,0:T(8,128)(2,1)S(1)} all-to-all(f16[8,256,128]{2,1,0:T(8,128)(2,1)S(1)} %bitcast.8), channel_id=1, replica_groups=mesh['wide'=16,'narrow'=8] {'narrow'}, dimensions={0} | all-to-all | bytes 1048576 | tf_op jit(solution)/shard_map/all_to_all | solution.py:128
  92.2 1.2 collective-permute-done.18
  94.7 1.6 collective-permute-start.20
  97.0 3.1 %collective-permute-done.22.refs_2_ = bf16[512,128]{1,0:T(8,128)(2,1)S(1)} collective-permute-done((bf16[512,128]{1,0:T(8,128)(2,1)S(1)}, bf16[512,128]{1,0:T(8,128)(2,1)S(1)}, u32[]{:S(2)}, u32[]{:S(2)}) %collective-permute-start.22) | collective-permute-done | bytes 131104 | tf_op jit(solution)/shard_map/ppermute | solution.py:30
  100.1 1.8 %collective-permute-start.26 = (bf16[512,128]{1,0:T(8,128)(2,1)S(1)}, bf16[512,128]{1,0:T(8,128)(2,1)S(1)}, u32[]{:S(2)}, u32[]{:S(2)}) collective-permute-start(bf16[512,128]{1,0:T(8,128)(2,1)S(1)} %collective-permute-done.22.refs_2_), channel_id=1, source_target_pairs={{0,8},{1,9},{2,10},{3,11},{4,12},{5,13},{6,14},{7,15},{8,0},{9,1},... | collective-permute-start | bytes 393224 | tf_op jit(solution)/shard_map/ppermute | solution.py:30
  102.8 1.8 %collective-permute-start.24 = (bf16[512,128]{1,0:T(8,128)(2,1)S(1)}, bf16[512,128]{1,0:T(8,128)(2,1)S(1)}, u32[]{:S(2)}, u32[]{:S(2)}) collective-permute-start(bf16[512,128]{1,0:T(8,128)(2,1)S(1)} %collective-permute-done.20.refs_0_), channel_id=1, source_target_pairs={{0,8},{1,9},{2,10},{3,11},{4,12},{5,13},{6,14},{7,15},{8,0},{9,1},... | collective-permute-start | bytes 393224 | tf_op jit(solution)/shard_map/ppermute | solution.py:30
  104.7 1.8 %shard_map.65.refs_4_ = f32[2048,128]{1,0:T(8,128)S(1)} custom-call(s32[1]{0:T(128)} %bitcast.wide_ref, bf16[2048,4096]{1,0:T(8,128)(2,1)S(1)} %bitcast.6, bf16[512,128]{1,0:T(8,128)(2,1)S(1)} %collective-permute-done.20.refs_0_, bf16[512,128]{1,0:T(8,128)(2,1)S(1)} %collective-permute-done.21.refs_1_, bf16[512,128]{1,0:T(8,128)(2,1)S(1)} %collective-permute-done.22.refs_2_), custom_call_target="tpu_custom_call" | custom-call | flops 805306368 | bytes 6291456 | tf_op jit(solution)/shard_map/pallas_call | solution.py:95
  106.6 2.3 %shard_map.66.refs_1_ = f32[2048,128]{1,0:T(8,128)S(1)} custom-call(s32[1]{0:T(128)} %bitcast.wide_ref, bf16[2048,4096]{1,0:T(8,128)(2,1)S(1)} %bitcast.6, bf16[512,128]{1,0:T(8,128)(2,1)S(1)} %collective-permute-done.19.refs_0_, bf16[512,128]{1,0:T(8,128)(2,1)S(1)} %collective-permute-done.24.refs_1_, bf16[512,128]{1,0:T(8,128)(2,1)S(1)} %collective-permute-done.25.refs_2_, ...), custom_call_target="tpu_custom_call" | custom-call | flops 1073741824 | bytes 8388608 | tf_op jit(solution)/shard_map/pallas_call | solution.py:95
  109.8 23.6 %all_to_all.22 = f16[8,256,128]{2,1,0:T(8,128)(2,1)S(1)} all-to-all(f16[8,256,128]{2,1,0:T(8,128)(2,1)S(1)} %bitcast.9), channel_id=1, replica_groups=mesh['wide'=16,'narrow'=8] {'narrow'}, dimensions={0} | all-to-all | bytes 1048576 | tf_op jit(solution)/shard_map/all_to_all | solution.py:128
  135.1 1.8 %collective-permute-start.29 = (bf16[512,128]{1,0:T(8,128)(2,1)S(1)}, bf16[512,128]{1,0:T(8,128)(2,1)S(1)}, u32[]{:S(2)}, u32[]{:S(2)}) collective-permute-start(bf16[512,128]{1,0:T(8,128)(2,1)S(1)} %pad_maximum_fusion.3), channel_id=1, source_target_pairs={{0,16},{1,32},{2,48},{3,0},{4,80},{5,96},{6,112},{7,64},{8,88},{9,... | collective-permute-start | bytes 393224 | tf_op jit(solution)/shard_map/ppermute | solution.py:30
  137.5 4.1 %collective-permute-done.31.refs_2_ = bf16[512,128]{1,0:T(8,128)(2,1)S(1)} collective-permute-done((bf16[512,128]{1,0:T(8,128)(2,1)S(1)}, bf16[512,128]{1,0:T(8,128)(2,1)S(1)}, u32[]{:S(2)}, u32[]{:S(2)}) %collective-permute-start.31) | collective-permute-done | bytes 131104 | tf_op jit(solution)/shard_map/ppermute | solution.py:30
  141.6 1.7 collective-permute-start.35
  144.2 1.7 collective-permute-start.33
  145.9 1.8 %shard_map.68.refs_4_ = f32[2048,128]{1,0:T(8,128)S(1)} custom-call(s32[1]{0:T(128)} %bitcast.wide_ref, bf16[2048,4096]{1,0:T(8,128)(2,1)S(1)} %bitcast.6, bf16[512,128]{1,0:T(8,128)(2,1)S(1)} %collective-permute-done.29.refs_0_, bf16[512,128]{1,0:T(8,128)(2,1)S(1)} %collective-permute-done.30.refs_1_, bf16[512,128]{1,0:T(8,128)(2,1)S(1)} %collective-permute-done.31.refs_2_), custom_call_target="tpu_custom_call" | custom-call | flops 805306368 | bytes 6291456 | tf_op jit(solution)/shard_map/pallas_call | solution.py:95
  147.8 2.3 %shard_map.69.refs_1_ = f32[2048,128]{1,0:T(8,128)S(1)} custom-call(s32[1]{0:T(128)} %bitcast.wide_ref, bf16[2048,4096]{1,0:T(8,128)(2,1)S(1)} %bitcast.6, bf16[512,128]{1,0:T(8,128)(2,1)S(1)} %collective-permute-done.28.refs_0_, bf16[512,128]{1,0:T(8,128)(2,1)S(1)} %collective-permute-done.33.refs_1_, bf16[512,128]{1,0:T(8,128)(2,1)S(1)} %collective-permute-done.34.refs_2_, ...), custom_call_target="tpu_custom_call" | custom-call | flops 1073741824 | bytes 8388608 | tf_op jit(solution)/shard_map/pallas_call | solution.py:95
  151.0 22.9 %all_to_all.23 = f16[8,256,128]{2,1,0:T(8,128)(2,1)S(1)} all-to-all(f16[8,256,128]{2,1,0:T(8,128)(2,1)S(1)} %bitcast.10), channel_id=1, replica_groups=mesh['wide'=16,'narrow'=8] {'narrow'}, dimensions={0} | all-to-all | bytes 1048576 | tf_op jit(solution)/shard_map/all_to_all | solution.py:128
  (88 shorter events, 16.5 us)
Async XLA Ops:
  2.9 9.0 %collective-permute-start.4 = (bf16[512,128]{1,0:T(8,128)(2,1)S(1)}, bf16[512,128]{1,0:T(8,128)(2,1)S(1)}, u32[]{:S(2)}, u32[]{:S(2)}) collective-permute-start(bf16[512,128]{1,0:T(8,128)(2,1)S(1)} %pad_maximum_fusion), channel_id=1, source_target_pairs={{0,32},{1,48},{2,0},{3,16},{4,96},{5,112},{6,64},{7,80},{8,104},{9... | collective-permute-start | bytes 393224 | tf_op jit(solution)/shard_map/ppermute | solution.py:30
  6.3 10.8 %collective-permute-start.3 = (bf16[512,128]{1,0:T(8,128)(2,1)S(1)}, bf16[512,128]{1,0:T(8,128)(2,1)S(1)}, u32[]{:S(2)}, u32[]{:S(2)}) collective-permute-start(bf16[512,128]{1,0:T(8,128)(2,1)S(1)} %pad_maximum_fusion), channel_id=1, source_target_pairs={{0,48},{1,0},{2,16},{3,32},{4,112},{5,64},{6,80},{7,96},{8,120},{9... | collective-permute-start | bytes 393224 | tf_op jit(solution)/shard_map/ppermute | solution.py:30
  10.3 6.7 %collective-permute-start.2 = (bf16[512,128]{1,0:T(8,128)(2,1)S(1)}, bf16[512,128]{1,0:T(8,128)(2,1)S(1)}, u32[]{:S(2)}, u32[]{:S(2)}) collective-permute-start(bf16[512,128]{1,0:T(8,128)(2,1)S(1)} %pad_maximum_fusion), channel_id=1, source_target_pairs={{0,16},{1,32},{2,48},{3,0},{4,80},{5,96},{6,112},{7,64},{8,88},{9,... | collective-permute-start | bytes 393224 | tf_op jit(solution)/shard_map/ppermute | solution.py:30
  11.3 12.3 %collective-permute-start.1 = (bf16[512,128]{1,0:T(8,128)(2,1)S(1)}, bf16[512,128]{1,0:T(8,128)(2,1)S(1)}, u32[]{:S(2)}, u32[]{:S(2)}) collective-permute-start(bf16[512,128]{1,0:T(8,128)(2,1)S(1)} %pad_maximum_fusion), channel_id=1, source_target_pairs={{0,0},{1,16},{2,32},{3,48},{4,64},{5,80},{6,96},{7,112},{8,72},{9,... | collective-permute-start | bytes 393224 | tf_op jit(solution)/shard_map/ppermute | solution.py:30
  11.9 11.7 %collective-permute-start.8 = (bf16[512,128]{1,0:T(8,128)(2,1)S(1)}, bf16[512,128]{1,0:T(8,128)(2,1)S(1)}, u32[]{:S(2)}, u32[]{:S(2)}) collective-permute-start(bf16[512,128]{1,0:T(8,128)(2,1)S(1)} %collective-permute-done.4.refs_2_), channel_id=1, source_target_pairs={{0,8},{1,9},{2,10},{3,11},{4,12},{5,13},{6,14},{7,15},{8,0},{9,1},... | collective-permute-start | bytes 393224 | tf_op jit(solution)/shard_map/ppermute | solution.py:30
  17.0 6.6 %collective-permute-start.7 = (bf16[512,128]{1,0:T(8,128)(2,1)S(1)}, bf16[512,128]{1,0:T(8,128)(2,1)S(1)}, u32[]{:S(2)}, u32[]{:S(2)}) collective-permute-start(bf16[512,128]{1,0:T(8,128)(2,1)S(1)} %collective-permute-done.3.refs_1_), channel_id=1, source_target_pairs={{0,8},{1,9},{2,10},{3,11},{4,12},{5,13},{6,14},{7,15},{8,0},{9,1},... | collective-permute-start | bytes 393224 | tf_op jit(solution)/shard_map/ppermute | solution.py:30
  17.0 6.6 %collective-permute-start.6 = (bf16[512,128]{1,0:T(8,128)(2,1)S(1)}, bf16[512,128]{1,0:T(8,128)(2,1)S(1)}, u32[]{:S(2)}, u32[]{:S(2)}) collective-permute-start(bf16[512,128]{1,0:T(8,128)(2,1)S(1)} %collective-permute-done.2.refs_0_), channel_id=1, source_target_pairs={{0,8},{1,9},{2,10},{3,11},{4,12},{5,13},{6,14},{7,15},{8,0},{9,1},... | collective-permute-start | bytes 393224 | tf_op jit(solution)/shard_map/ppermute | solution.py:30
  23.5 4.7 %collective-permute-start.5 = (bf16[512,128]{1,0:T(8,128)(2,1)S(1)}, bf16[512,128]{1,0:T(8,128)(2,1)S(1)}, u32[]{:S(2)}, u32[]{:S(2)}) collective-permute-start(bf16[512,128]{1,0:T(8,128)(2,1)S(1)} %collective-permute-done.1.refs_0_), channel_id=1, source_target_pairs={{0,8},{1,9},{2,10},{3,11},{4,12},{5,13},{6,14},{7,15},{8,0},{9,1},... | collective-permute-start | bytes 393224 | tf_op jit(solution)/shard_map/ppermute | solution.py:30
  54.2 6.6 %collective-permute-start.13 = (bf16[512,128]{1,0:T(8,128)(2,1)S(1)}, bf16[512,128]{1,0:T(8,128)(2,1)S(1)}, u32[]{:S(2)}, u32[]{:S(2)}) collective-permute-start(bf16[512,128]{1,0:T(8,128)(2,1)S(1)} %pad_maximum_fusion.1), channel_id=1, source_target_pairs={{0,32},{1,48},{2,0},{3,16},{4,96},{5,112},{6,64},{7,80},{8,104},{9... | collective-permute-start | bytes 393224 | tf_op jit(solution)/shard_map/ppermute | solution.py:30
  54.3 8.6 %collective-permute-start.12 = (bf16[512,128]{1,0:T(8,128)(2,1)S(1)}, bf16[512,128]{1,0:T(8,128)(2,1)S(1)}, u32[]{:S(2)}, u32[]{:S(2)}) collective-permute-start(bf16[512,128]{1,0:T(8,128)(2,1)S(1)} %pad_maximum_fusion.1), channel_id=1, source_target_pairs={{0,48},{1,0},{2,16},{3,32},{4,112},{5,64},{6,80},{7,96},{8,120},{9... | collective-permute-start | bytes 393224 | tf_op jit(solution)/shard_map/ppermute | solution.py:30
  55.0 9.9 %collective-permute-start.11 = (bf16[512,128]{1,0:T(8,128)(2,1)S(1)}, bf16[512,128]{1,0:T(8,128)(2,1)S(1)}, u32[]{:S(2)}, u32[]{:S(2)}) collective-permute-start(bf16[512,128]{1,0:T(8,128)(2,1)S(1)} %pad_maximum_fusion.1), channel_id=1, source_target_pairs={{0,16},{1,32},{2,48},{3,0},{4,80},{5,96},{6,112},{7,64},{8,88},{9,... | collective-permute-start | bytes 393224 | tf_op jit(solution)/shard_map/ppermute | solution.py:30
  56.0 10.7 %collective-permute-start.10 = (bf16[512,128]{1,0:T(8,128)(2,1)S(1)}, bf16[512,128]{1,0:T(8,128)(2,1)S(1)}, u32[]{:S(2)}, u32[]{:S(2)}) collective-permute-start(bf16[512,128]{1,0:T(8,128)(2,1)S(1)} %pad_maximum_fusion.1), channel_id=1, source_target_pairs={{0,0},{1,16},{2,32},{3,48},{4,64},{5,80},{6,96},{7,112},{8,72},{9,... | collective-permute-start | bytes 393224 | tf_op jit(solution)/shard_map/ppermute | solution.py:30
  60.8 6.7 %collective-permute-start.17 = (bf16[512,128]{1,0:T(8,128)(2,1)S(1)}, bf16[512,128]{1,0:T(8,128)(2,1)S(1)}, u32[]{:S(2)}, u32[]{:S(2)}) collective-permute-start(bf16[512,128]{1,0:T(8,128)(2,1)S(1)} %collective-permute-done.13.refs_2_), channel_id=1, source_target_pairs={{0,8},{1,9},{2,10},{3,11},{4,12},{5,13},{6,14},{7,15},{8,0},{9,1},... | collective-permute-start | bytes 393224 | tf_op jit(solution)/shard_map/ppermute | solution.py:30
  62.9 4.7 %collective-permute-start.16 = (bf16[512,128]{1,0:T(8,128)(2,1)S(1)}, bf16[512,128]{1,0:T(8,128)(2,1)S(1)}, u32[]{:S(2)}, u32[]{:S(2)}) collective-permute-start(bf16[512,128]{1,0:T(8,128)(2,1)S(1)} %collective-permute-done.12.refs_1_), channel_id=1, source_target_pairs={{0,8},{1,9},{2,10},{3,11},{4,12},{5,13},{6,14},{7,15},{8,0},{9,1},... | collective-permute-start | bytes 393224 | tf_op jit(solution)/shard_map/ppermute | solution.py:30
  64.9 2.6 %collective-permute-start.15 = (bf16[512,128]{1,0:T(8,128)(2,1)S(1)}, bf16[512,128]{1,0:T(8,128)(2,1)S(1)}, u32[]{:S(2)}, u32[]{:S(2)}) collective-permute-start(bf16[512,128]{1,0:T(8,128)(2,1)S(1)} %collective-permute-done.11.refs_0_), channel_id=1, source_target_pairs={{0,8},{1,9},{2,10},{3,11},{4,12},{5,13},{6,14},{7,15},{8,0},{9,1},... | collective-permute-start | bytes 393224 | tf_op jit(solution)/shard_map/ppermute | solution.py:30
  66.8 3.1 %collective-permute-start.14 = (bf16[512,128]{1,0:T(8,128)(2,1)S(1)}, bf16[512,128]{1,0:T(8,128)(2,1)S(1)}, u32[]{:S(2)}, u32[]{:S(2)}) collective-permute-start(bf16[512,128]{1,0:T(8,128)(2,1)S(1)} %collective-permute-done.10.refs_0_), channel_id=1, source_target_pairs={{0,8},{1,9},{2,10},{3,11},{4,12},{5,13},{6,14},{7,15},{8,0},{9,1},... | collective-permute-start | bytes 393224 | tf_op jit(solution)/shard_map/ppermute | solution.py:30
  93.5 6.6 %collective-permute-start.22 = (bf16[512,128]{1,0:T(8,128)(2,1)S(1)}, bf16[512,128]{1,0:T(8,128)(2,1)S(1)}, u32[]{:S(2)}, u32[]{:S(2)}) collective-permute-start(bf16[512,128]{1,0:T(8,128)(2,1)S(1)} %pad_maximum_fusion.2), channel_id=1, source_target_pairs={{0,32},{1,48},{2,0},{3,16},{4,96},{5,112},{6,64},{7,80},{8,104},{9... | collective-permute-start | bytes 393224 | tf_op jit(solution)/shard_map/ppermute | solution.py:30
  93.9 8.0 %collective-permute-start.21 = (bf16[512,128]{1,0:T(8,128)(2,1)S(1)}, bf16[512,128]{1,0:T(8,128)(2,1)S(1)}, u32[]{:S(2)}, u32[]{:S(2)}) collective-permute-start(bf16[512,128]{1,0:T(8,128)(2,1)S(1)} %pad_maximum_fusion.2), channel_id=1, source_target_pairs={{0,48},{1,0},{2,16},{3,32},{4,112},{5,64},{6,80},{7,96},{8,120},{9... | collective-permute-start | bytes 393224 | tf_op jit(solution)/shard_map/ppermute | solution.py:30
  94.7 8.2 %collective-permute-start.20 = (bf16[512,128]{1,0:T(8,128)(2,1)S(1)}, bf16[512,128]{1,0:T(8,128)(2,1)S(1)}, u32[]{:S(2)}, u32[]{:S(2)}) collective-permute-start(bf16[512,128]{1,0:T(8,128)(2,1)S(1)} %pad_maximum_fusion.2), channel_id=1, source_target_pairs={{0,16},{1,32},{2,48},{3,0},{4,80},{5,96},{6,112},{7,64},{8,88},{9,... | collective-permute-start | bytes 393224 | tf_op jit(solution)/shard_map/ppermute | solution.py:30
  96.3 10.2 %collective-permute-start.19 = (bf16[512,128]{1,0:T(8,128)(2,1)S(1)}, bf16[512,128]{1,0:T(8,128)(2,1)S(1)}, u32[]{:S(2)}, u32[]{:S(2)}) collective-permute-start(bf16[512,128]{1,0:T(8,128)(2,1)S(1)} %pad_maximum_fusion.2), channel_id=1, source_target_pairs={{0,0},{1,16},{2,32},{3,48},{4,64},{5,80},{6,96},{7,112},{8,72},{9,... | collective-permute-start | bytes 393224 | tf_op jit(solution)/shard_map/ppermute | solution.py:30
  100.1 6.5 %collective-permute-start.26 = (bf16[512,128]{1,0:T(8,128)(2,1)S(1)}, bf16[512,128]{1,0:T(8,128)(2,1)S(1)}, u32[]{:S(2)}, u32[]{:S(2)}) collective-permute-start(bf16[512,128]{1,0:T(8,128)(2,1)S(1)} %collective-permute-done.22.refs_2_), channel_id=1, source_target_pairs={{0,8},{1,9},{2,10},{3,11},{4,12},{5,13},{6,14},{7,15},{8,0},{9,1},... | collective-permute-start | bytes 393224 | tf_op jit(solution)/shard_map/ppermute | solution.py:30
  101.8 4.7 %collective-permute-start.25 = (bf16[512,128]{1,0:T(8,128)(2,1)S(1)}, bf16[512,128]{1,0:T(8,128)(2,1)S(1)}, u32[]{:S(2)}, u32[]{:S(2)}) collective-permute-start(bf16[512,128]{1,0:T(8,128)(2,1)S(1)} %collective-permute-done.21.refs_1_), channel_id=1, source_target_pairs={{0,8},{1,9},{2,10},{3,11},{4,12},{5,13},{6,14},{7,15},{8,0},{9,1},... | collective-permute-start | bytes 393224 | tf_op jit(solution)/shard_map/ppermute | solution.py:30
  102.8 3.8 %collective-permute-start.24 = (bf16[512,128]{1,0:T(8,128)(2,1)S(1)}, bf16[512,128]{1,0:T(8,128)(2,1)S(1)}, u32[]{:S(2)}, u32[]{:S(2)}) collective-permute-start(bf16[512,128]{1,0:T(8,128)(2,1)S(1)} %collective-permute-done.20.refs_0_), channel_id=1, source_target_pairs={{0,8},{1,9},{2,10},{3,11},{4,12},{5,13},{6,14},{7,15},{8,0},{9,1},... | collective-permute-start | bytes 393224 | tf_op jit(solution)/shard_map/ppermute | solution.py:30
  106.5 2.5 %collective-permute-start.23 = (bf16[512,128]{1,0:T(8,128)(2,1)S(1)}, bf16[512,128]{1,0:T(8,128)(2,1)S(1)}, u32[]{:S(2)}, u32[]{:S(2)}) collective-permute-start(bf16[512,128]{1,0:T(8,128)(2,1)S(1)} %collective-permute-done.19.refs_0_), channel_id=1, source_target_pairs={{0,8},{1,9},{2,10},{3,11},{4,12},{5,13},{6,14},{7,15},{8,0},{9,1},... | collective-permute-start | bytes 393224 | tf_op jit(solution)/shard_map/ppermute | solution.py:30
  135.0 6.7 %collective-permute-start.31 = (bf16[512,128]{1,0:T(8,128)(2,1)S(1)}, bf16[512,128]{1,0:T(8,128)(2,1)S(1)}, u32[]{:S(2)}, u32[]{:S(2)}) collective-permute-start(bf16[512,128]{1,0:T(8,128)(2,1)S(1)} %pad_maximum_fusion.3), channel_id=1, source_target_pairs={{0,32},{1,48},{2,0},{3,16},{4,96},{5,112},{6,64},{7,80},{8,104},{9... | collective-permute-start | bytes 393224 | tf_op jit(solution)/shard_map/ppermute | solution.py:30
  135.0 8.3 %collective-permute-start.30 = (bf16[512,128]{1,0:T(8,128)(2,1)S(1)}, bf16[512,128]{1,0:T(8,128)(2,1)S(1)}, u32[]{:S(2)}, u32[]{:S(2)}) collective-permute-start(bf16[512,128]{1,0:T(8,128)(2,1)S(1)} %pad_maximum_fusion.3), channel_id=1, source_target_pairs={{0,48},{1,0},{2,16},{3,32},{4,112},{5,64},{6,80},{7,96},{8,120},{9... | collective-permute-start | bytes 393224 | tf_op jit(solution)/shard_map/ppermute | solution.py:30
  135.1 9.1 %collective-permute-start.29 = (bf16[512,128]{1,0:T(8,128)(2,1)S(1)}, bf16[512,128]{1,0:T(8,128)(2,1)S(1)}, u32[]{:S(2)}, u32[]{:S(2)}) collective-permute-start(bf16[512,128]{1,0:T(8,128)(2,1)S(1)} %pad_maximum_fusion.3), channel_id=1, source_target_pairs={{0,16},{1,32},{2,48},{3,0},{4,80},{5,96},{6,112},{7,64},{8,88},{9,... | collective-permute-start | bytes 393224 | tf_op jit(solution)/shard_map/ppermute | solution.py:30
  136.9 10.8 %collective-permute-start.28 = (bf16[512,128]{1,0:T(8,128)(2,1)S(1)}, bf16[512,128]{1,0:T(8,128)(2,1)S(1)}, u32[]{:S(2)}, u32[]{:S(2)}) collective-permute-start(bf16[512,128]{1,0:T(8,128)(2,1)S(1)} %pad_maximum_fusion.3), channel_id=1, source_target_pairs={{0,0},{1,16},{2,32},{3,48},{4,64},{5,80},{6,96},{7,112},{8,72},{9,... | collective-permute-start | bytes 393224 | tf_op jit(solution)/shard_map/ppermute | solution.py:30
  141.6 6.2 %collective-permute-start.35 = (bf16[512,128]{1,0:T(8,128)(2,1)S(1)}, bf16[512,128]{1,0:T(8,128)(2,1)S(1)}, u32[]{:S(2)}, u32[]{:S(2)}) collective-permute-start(bf16[512,128]{1,0:T(8,128)(2,1)S(1)} %collective-permute-done.31.refs_2_), channel_id=1, source_target_pairs={{0,8},{1,9},{2,10},{3,11},{4,12},{5,13},{6,14},{7,15},{8,0},{9,1},... | collective-permute-start | bytes 393224 | tf_op jit(solution)/shard_map/ppermute | solution.py:30
  143.3 4.5 %collective-permute-start.34 = (bf16[512,128]{1,0:T(8,128)(2,1)S(1)}, bf16[512,128]{1,0:T(8,128)(2,1)S(1)}, u32[]{:S(2)}, u32[]{:S(2)}) collective-permute-start(bf16[512,128]{1,0:T(8,128)(2,1)S(1)} %collective-permute-done.30.refs_1_), channel_id=1, source_target_pairs={{0,8},{1,9},{2,10},{3,11},{4,12},{5,13},{6,14},{7,15},{8,0},{9,1},... | collective-permute-start | bytes 393224 | tf_op jit(solution)/shard_map/ppermute | solution.py:30
  144.2 3.6 %collective-permute-start.33 = (bf16[512,128]{1,0:T(8,128)(2,1)S(1)}, bf16[512,128]{1,0:T(8,128)(2,1)S(1)}, u32[]{:S(2)}, u32[]{:S(2)}) collective-permute-start(bf16[512,128]{1,0:T(8,128)(2,1)S(1)} %collective-permute-done.29.refs_0_), channel_id=1, source_target_pairs={{0,8},{1,9},{2,10},{3,11},{4,12},{5,13},{6,14},{7,15},{8,0},{9,1},... | collective-permute-start | bytes 393224 | tf_op jit(solution)/shard_map/ppermute | solution.py:30
  147.7 2.5 %collective-permute-start.32 = (bf16[512,128]{1,0:T(8,128)(2,1)S(1)}, bf16[512,128]{1,0:T(8,128)(2,1)S(1)}, u32[]{:S(2)}, u32[]{:S(2)}) collective-permute-start(bf16[512,128]{1,0:T(8,128)(2,1)S(1)} %collective-permute-done.28.refs_0_), channel_id=1, source_target_pairs={{0,8},{1,9},{2,10},{3,11},{4,12},{5,13},{6,14},{7,15},{8,0},{9,1},... | collective-permute-start | bytes 393224 | tf_op jit(solution)/shard_map/ppermute | solution.py:30
  (11 other events, 249.4 us)

commit v3 on v2

v3 whole, which is shorter than its diff:
```python
import functools

import jax
import jax.numpy as jnp
from jax import lax
from jax.experimental import pallas as pl
from jax.experimental.pallas import tpu as pltpu
from jax.sharding import PartitionSpec as P

STEPS = 4
AXES = ("wide", "narrow")
REPLICAS = 128
PIECE = 256
SCALE = 64.0

time_step = 1.25
coupling_scale = 0.5


def shifted(block, shift):
    return (block // 4 ^ shift // 4) * 4 + (block % 4 + shift % 4) % 4


def permuted(array, place):
    pairs = []
    for w in range(16):
        for n in range(8):
            to_w, to_n = place(w, n)
            pairs.append((w * 8 + n, to_w * 8 + to_n))
    return lax.ppermute(array, AXES, pairs)


def other_core(w, n):
    return w ^ 1, n


def to_users(turns):
    def place(w, n):
        core = w % 2
        return shifted(n, turns[core] + 4 * core) * 2 + core, w // 2

    return place


def to_owner(turn):
    def place(w, n):
        core = w % 2
        return w, n ^ turn ^ 4 * core

    return place


ALL, KEPT, GIVEN = range(3)


def multiply(device_ref, coupling_ref, *refs, terms, rows_of, add, stream):
    refs = list(refs)
    if stream:
        arrived, held_ref = refs.pop(), refs.pop()
    out_ref = refs.pop()
    total_ref = refs.pop() if add else None
    rows = out_ref.shape[0]
    tile = 512
    wide, narrow = device_ref[0] // 8, device_ref[0] % 8
    chip, core = wide // 2, wide % 2
    base = 0
    if rows_of != ALL:
        adder = core if rows_of == KEPT else 1 - core
        base = pl.multiple_of((narrow // 4 ^ adder) * 1024, 1024)
    spans = []
    for turns, crossed in terms:
        sender = 1 - core if crossed else core
        turn = turns[0] + (turns[1] - turns[0]) * sender
        piece = (chip // 4 ^ sender) * 4 + (chip % 4 + 4 - turn) % 4
        for half in (sender, 1 - sender):
            spans.append(pl.ds(pl.multiple_of(half * 2048 + piece * PIECE, PIECE), PIECE))
    copies = []
    if stream:
        for index, columns in enumerate(spans):
            copies.append(
                pltpu.make_async_copy(
                    coupling_ref.at[pl.ds(base, rows), columns], held_ref.at[index], arrived.at[index]
                )
            )
            copies[-1].start()
    for index, piece_ref in enumerate(refs):
        for copy in copies[2 * index : 2 * index + 2]:
            copy.wait()
        for first in range(0, rows, tile):
            blocks = []
            for k in (2 * index, 2 * index + 1):
                if stream:
                    blocks.append(held_ref[k, pl.ds(first, tile), :])
                else:
                    blocks.append(coupling_ref[pl.ds(base + first, tile), spans[k]])
            term = jnp.dot(blocks[0], piece_ref[:PIECE, :], preferred_element_type=jnp.float32)
            term += jnp.dot(blocks[1], piece_ref[PIECE:, :], preferred_element_type=jnp.float32)
            for begin in range(0, tile, PIECE):
                to = first + begin
                if rows_of != ALL:
                    to = pl.multiple_of((narrow % 4 ^ to // PIECE) * PIECE, PIECE)
                to = pl.ds(to, PIECE)
                here = term[begin : begin + PIECE, :]
                if index > 0:
                    here += out_ref[to, :]
                elif add and total_ref.shape[0] == rows:
                    here += total_ref[to, :]
                elif add:
                    here += total_ref[pl.ds(base + first + begin, PIECE), :]
                out_ref[to, :] = here


def product(device, coupling, terms, pieces, total=None, rows_of=ALL, stream=False):
    operands = [*pieces] + ([] if total is None else [total])
    rows = coupling.shape[0] if rows_of == ALL else 1024
    depth = 2 * PIECE * len(pieces)
    space = pltpu.HBM if stream else pltpu.VMEM
    scratch = []
    if stream:
        scratch = [
            pltpu.VMEM((depth // PIECE, rows, PIECE), coupling.dtype),
            pltpu.SemaphoreType.DMA((depth // PIECE,)),
        ]
    return pl.pallas_call(
        functools.partial(multiply, terms=terms, rows_of=rows_of, add=total is not None, stream=stream),
        out_shape=jax.ShapeDtypeStruct((rows, REPLICAS), jnp.float32),
        in_specs=[pl.BlockSpec(memory_space=pltpu.SMEM), pl.BlockSpec(memory_space=space)]
        + [pl.BlockSpec(memory_space=pltpu.VMEM)] * len(operands),
        out_specs=pl.BlockSpec(memory_space=pltpu.VMEM),
        scratch_shapes=scratch,
        compiler_params=pltpu.CompilerParams(vmem_limit_bytes=(16 if stream else 8) << 20),
        cost_estimate=pl.CostEstimate(
            flops=2 * rows * depth * REPLICAS, bytes_accessed=rows * depth * 2, transcendentals=0
        ),
    )(device, pltpu.with_memory_space_constraint(coupling, space), *operands)


def on_device(coupling, hashes, momentum, linear):
    device = (lax.axis_index("wide") * 8 + lax.axis_index("narrow")).astype(jnp.int32).reshape(1)
    positions = (hashes.astype(jnp.float32) - 32768.0) / 65536.0
    velocity, linear_term = momentum, linear[:, None]
    lowered = positions.astype(jnp.bfloat16)
    lowered = jnp.concatenate([lowered, permuted(lowered, other_core)])
    turns = ((0, 1), (1, 3), (3, 2), (2, 0))
    for step_index in range(STEPS):
        own = [permuted(lowered, to_users(turn)) for turn in turns]
        stream = step_index == 0
        if step_index == STEPS - 1:
            positions, velocity, linear_term = positions[:PIECE], velocity[:PIECE], linear_term[:PIECE]
        others = [permuted(piece, other_core) for piece in own[:3]]
        total = product(device, coupling, [(turn, False) for turn in turns[:3]], own[:3], None, ALL, stream)
        last, total = lax.optimization_barrier((own[3], total))
        late = permuted(last, other_core)
        terms = [(turns[3], False)] + [(turn, True) for turn in turns[:3]]
        end = [(turns[3], True)]
        if step_index == 0:
            total = product(device, coupling, terms, [last, *others], total, ALL, stream)
            total = product(device, coupling, end, [late], total, ALL, stream)
            sent = (total * SCALE).astype(jnp.float16)
            parts = lax.all_to_all(sent.reshape(8, PIECE, REPLICAS), "narrow", 0, 0)
            field = jnp.sum(parts.astype(jnp.float32), axis=0)
        else:
            given = product(device, coupling, terms, [last, *others], total, GIVEN)
            given = product(device, coupling, end, [late], given, GIVEN)
            given = permuted((given * SCALE).astype(jnp.float16), other_core)
            kept = product(device, coupling, terms + end, [last, *others, late], total, KEPT)
            kept = (kept * SCALE).astype(jnp.float16)
            sums = []
            for turn in (2, 1, 3, 0):
                rows = slice(turn * PIECE, turn * PIECE + PIECE)
                sums.append(permuted(jnp.concatenate([kept[rows], given[rows]]), to_owner(turn)))
            half_sum = lax.optimization_barrier(sum(part.astype(jnp.float32) for part in sums).astype(jnp.float16))
            if step_index == STEPS - 1:
                field = half_sum[:PIECE].astype(jnp.float32)
                field += permuted(half_sum[PIECE:], other_core).astype(jnp.float32)
            else:
                theirs = permuted(half_sum, other_core)
                theirs = jnp.concatenate([theirs[PIECE:], theirs[:PIECE]])
                field = half_sum.astype(jnp.float32) + theirs.astype(jnp.float32)
        local_field = field / SCALE
        pump_level = (step_index + 1.0) / (STEPS + 1.0)
        velocity = velocity + time_step * (
            -(1.0 - pump_level) * positions + coupling_scale * (local_field + linear_term)
        )
        moved = positions + time_step * velocity
        clamped = jnp.clip(moved, -1.0, 1.0)
        velocity = velocity - (moved - clamped) / time_step
        positions = clamped
        lowered = positions.astype(jnp.bfloat16)
        if step_index == 0:
            lowered = jnp.concatenate([lowered, permuted(lowered, other_core)])
            state = jnp.concatenate([positions, velocity, jnp.pad(linear.reshape(2, 128), ((0, 6), (0, 0)))])
            both = [state, permuted(state, other_core)]
            positions, velocity = (jnp.concatenate([s[k : k + PIECE] for s in both]) for k in (0, PIECE))
            linear_term = jnp.concatenate([s[2 * PIECE : 2 * PIECE + 2].reshape(PIECE) for s in both])[:, None]
    return (positions, velocity)


def solution(mesh):
    return jax.shard_map(
        on_device,
        mesh=mesh,
        in_specs=(
            P("wide", "narrow"),
            P(("wide", "narrow"), None),
            P(("wide", "narrow"), None),
            P(("wide", "narrow")),
        ),
        out_specs=(P(("wide", "narrow"), None), P(("wide", "narrow"), None)),
        check_vma=False,
    )
```

time: 175 us -> 171 us (0.977)
  blocking collectives: 89.1 us -> 16.4 us
  starting transfers between devices: 34.3 us -> 82.2 us
  waiting for transfers between devices: 21.8 us -> 38.9 us
    all_to_all x4 -> x1, blocking collectives: 89.1 us -> 16.4 us  [on_device(): parts = lax.all_to_all(sent.reshape(8, PIECE, REPLICAS), 'narrow', 0, 0)]
    ppermute x36 -> x53, starting transfers between devices: 34.3 us -> 82.2 us  [permuted(): return lax.ppermute(array, AXES, pairs)]
    ppermute x36 -> x53, waiting for transfers between devices: 21.8 us -> 38.9 us  [permuted(): return lax.ppermute(array, AXES, pairs)]
    pallas_call x12 -> x15, Pallas kernels: 25.5 us -> 26.2 us  [product(): pl.pallas_call(functools.partial(multiply, terms=terms, rows_of=rows_of,...]
  transfers between devices with their start and end apart: 36 -> 53, of which waited for: 11 -> 20; matrix products, arithmetic and copies ran while one was open for 0% -> 1% of each run, Pallas kernels for 12% -> 13%
where the time goes in v3:
time: 171 us; the launch traced here: 169 us
  starting transfers between devices  82.2 us (48%)
  waiting for transfers between devices  38.9 us (23%)
  Pallas kernels  26.2 us (15%)
  blocking collectives  16.4 us (10%)
  other arithmetic  3.75 us (2%)
    ppermute x53, starting transfers between devices, permuted(): return lax.ppermute(array, AXES, pairs)  82.2 us
    ppermute x53, waiting for transfers between devices, permuted(): return lax.ppermute(array, AXES, pairs)  38.9 us
    pallas_call x15, Pallas kernels, product(): pl.pallas_call(functools.partial(multiply, terms=terms, rows_of=rows_of,...  26.2 us
    all_to_all x1, blocking collectives, on_device(): parts = lax.all_to_all(sent.reshape(8, PIECE, REPLICAS), 'narrow', 0, 0)  16.4 us
  transfers between devices with their start and end apart: 53, of which 20 were waited for; matrix products, arithmetic and copies ran while one was open for 1% of the time, Pallas kernels for 13%

profile of v3, /device:TPU:0, one launch (start us, length us, event | category | flops | bytes accessed | tf_op | source)
XLA Modules:
  0.0 169.2 jit_solution(15162927525692619362)
XLA Ops:
  3.6 4.8 %collective-permute-start.3 = (bf16[512,128]{1,0:T(8,128)(2,1)S(1)}, bf16[512,128]{1,0:T(8,128)(2,1)S(1)}, u32[]{:S(2)}, u32[]{:S(2)}) collective-permute-start(bf16[512,128]{1,0:T(8,128)(2,1)S(1)} %pad_maximum_fusion.1), channel_id=1, source_target_pairs={{0,16},{1,32},{2,48},{3,0},{4,80},{5,96},{6,112},{7,64},{8,120},{9... | collective-permute-start | bytes 393224 | tf_op jit(solution)/shard_map/ppermute | solution.py:30
  8.4 6.6 %collective-permute-start.4 = (bf16[512,128]{1,0:T(8,128)(2,1)S(1)}, bf16[512,128]{1,0:T(8,128)(2,1)S(1)}, u32[]{:S(2)}, u32[]{:S(2)}) collective-permute-start(bf16[512,128]{1,0:T(8,128)(2,1)S(1)} %pad_maximum_fusion.1), channel_id=1, source_target_pairs={{0,48},{1,0},{2,16},{3,32},{4,112},{5,64},{6,80},{7,96},{8,104},{9... | collective-permute-start | bytes 393224 | tf_op jit(solution)/shard_map/ppermute | solution.py:30
  17.0 3.6 %collective-permute-done.4.refs_2_ = bf16[512,128]{1,0:T(8,128)(2,1)S(1)} collective-permute-done((bf16[512,128]{1,0:T(8,128)(2,1)S(1)}, bf16[512,128]{1,0:T(8,128)(2,1)S(1)}, u32[]{:S(2)}, u32[]{:S(2)}) %collective-permute-start.4) | collective-permute-done | bytes 131104 | tf_op jit(solution)/shard_map/ppermute | solution.py:30
  20.6 2.7 %collective-permute-start.8 = (bf16[512,128]{1,0:T(8,128)(2,1)S(1)}, bf16[512,128]{1,0:T(8,128)(2,1)S(1)}, u32[]{:S(2)}, u32[]{:S(2)}) collective-permute-start(bf16[512,128]{1,0:T(8,128)(2,1)S(1)} %collective-permute-done.4.refs_2_), channel_id=1, source_target_pairs={{0,8},{1,9},{2,10},{3,11},{4,12},{5,13},{6,14},{7,15},{8,0},{9,1},... | collective-permute-start | bytes 393224 | tf_op jit(solution)/shard_map/ppermute | solution.py:30
  23.3 3.6 %shard_map.59.refs_4_ = f32[2048,128]{1,0:T(8,128)S(1)} custom-call(s32[1]{0:T(128)} %bitcast.device_ref, bf16[2048,4096]{1,0:T(8,128)(2,1)} %coupling_ref.29, bf16[512,128]{1,0:T(8,128)(2,1)S(1)} %collective-permute-done.2.refs_0_, bf16[512,128]{1,0:T(8,128)(2,1)S(1)} %collective-permute-done.3.refs_1_, bf16[512,128]{1,0:T(8,128)(2,1)S(1)} %collective-permute-done.4.refs_2_), custom_call_target="tpu_custom_call" | custom-call | flops 805306368 | bytes 6291456 | tf_op jit(solution)/shard_map/pallas_call | solution.py:124
  27.1 4.5 %shard_map.60.refs_1_ = f32[2048,128]{1,0:T(8,128)S(1)} custom-call(s32[1]{0:T(128)} %bitcast.device_ref, bf16[2048,4096]{1,0:T(8,128)(2,1)} %coupling_ref.29, bf16[512,128]{1,0:T(8,128)(2,1)S(1)} %collective-permute-done.1.refs_0_, bf16[512,128]{1,0:T(8,128)(2,1)S(1)} %collective-permute-done.6.refs_1_, ...), custom_call_target="tpu_custom_call" | custom-call | flops 1073741824 | bytes 8388608 | tf_op jit(solution)/shard_map/pallas_call | solution.py:124
  31.7 2.8 %shard_map.61 = f32[2048,128]{1,0:T(8,128)S(1)} custom-call(s32[1]{0:T(128)} %bitcast.device_ref, bf16[2048,4096]{1,0:T(8,128)(2,1)} %coupling_ref.29, bf16[512,128]{1,0:T(8,128)(2,1)S(1)} %collective-permute-done.5.refs_0_, f32[2048,128]{1,0:T(8,128)S(1)} %shard_map.60.refs_1_), custom_call_target="tpu_custom_call" | custom-call | flops 268435456 | bytes 2097152 | tf_op jit(solution)/shard_map/pallas_call | solution.py:124
  34.6 16.4 %all_to_all.5 = f16[8,256,128]{2,1,0:T(8,128)(2,1)S(1)} all-to-all(f16[8,256,128]{2,1,0:T(8,128)(2,1)S(1)} %bitcast.7), channel_id=1, replica_groups=mesh['wide'=16,'narrow'=8] {'narrow'}, dimensions={0} | all-to-all | bytes 1048576 | tf_op jit(solution)/shard_map/all_to_all | solution.py:160
  53.3 3.0 %collective-permute-start.13 = (bf16[512,128]{1,0:T(8,128)(2,1)S(1)}, bf16[512,128]{1,0:T(8,128)(2,1)S(1)}, u32[]{:S(2)}, u32[]{:S(2)}) collective-permute-start(bf16[512,128]{1,0:T(8,128)(2,1)S(1)} %pad_maximum_fusion.2), channel_id=1, source_target_pairs={{0,16},{1,32},{2,48},{3,0},{4,80},{5,96},{6,112},{7,64},{8,120},{9... | collective-permute-start | bytes 393224 | tf_op jit(solution)/shard_map/ppermute | solution.py:30
  56.3 4.3 %collective-permute-start.14 = (bf16[512,128]{1,0:T(8,128)(2,1)S(1)}, bf16[512,128]{1,0:T(8,128)(2,1)S(1)}, u32[]{:S(2)}, u32[]{:S(2)}) collective-permute-start(bf16[512,128]{1,0:T(8,128)(2,1)S(1)} %pad_maximum_fusion.2), channel_id=1, source_target_pairs={{0,48},{1,0},{2,16},{3,32},{4,112},{5,64},{6,80},{7,96},{8,104},{9... | collective-permute-start | bytes 393224 | tf_op jit(solution)/shard_map/ppermute | solution.py:30
  62.5 3.8 %collective-permute-done.14.refs_2_ = bf16[512,128]{1,0:T(8,128)(2,1)S(1)} collective-permute-done((bf16[512,128]{1,0:T(8,128)(2,1)S(1)}, bf16[512,128]{1,0:T(8,128)(2,1)S(1)}, u32[]{:S(2)}, u32[]{:S(2)}) %collective-permute-start.14) | collective-permute-done | bytes 131104 | tf_op jit(solution)/shard_map/ppermute | solution.py:30
  66.3 1.8 %shard_map.62.refs_5_.refs_4_ = f32[2048,128]{1,0:T(8,128)S(1)} custom-call(s32[1]{0:T(128)} %bitcast.device_ref, bf16[2048,4096]{1,0:T(8,128)(2,1)S(1)} %bitcast.6, bf16[512,128]{1,0:T(8,128)(2,1)S(1)} %collective-permute-done.12.refs_0_, bf16[512,128]{1,0:T(8,128)(2,1)S(1)} %collective-permute-done.13.refs_1_, ...), custom_call_target="tpu_custom_call" | custom-call | flops 805306368 | bytes 6291456 | tf_op jit(solution)/shard_map/pallas_call | solution.py:124
  73.2 5.8 %collective-permute-start.20 = (f16[512,128]{1,0:T(8,128)(2,1)S(1)}, f16[512,128]{1,0:T(8,128)(2,1)S(1)}, u32[]{:S(2)}, u32[]{:S(2)}) collective-permute-start(f16[512,128]{1,0:T(8,128)(2,1)S(1)} %pad_maximum_fusion.3), channel_id=1, source_target_pairs={{0,2},{1,3},{2,0},{3,1},{4,6},{5,7},{6,4},{7,5},{8,14},{9,15},{10,... | collective-permute-start | bytes 393224 | tf_op jit(solution)/shard_map/ppermute | solution.py:30
  80.7 3.7 %collective-permute-done.20 = f16[512,128]{1,0:T(8,128)(2,1)S(1)} collective-permute-done((f16[512,128]{1,0:T(8,128)(2,1)S(1)}, f16[512,128]{1,0:T(8,128)(2,1)S(1)}, u32[]{:S(2)}, u32[]{:S(2)}) %collective-permute-start.20) | collective-permute-done | bytes 131104 | tf_op jit(solution)/shard_map/ppermute | solution.py:30
  85.9 3.8 %collective-permute-start.24 = (f16[512,128]{1,0:T(8,128)(2,1)S(1)}, f16[512,128]{1,0:T(8,128)(2,1)S(1)}, u32[]{:S(2)}, u32[]{:S(2)}) collective-permute-start(f16[512,128]{1,0:T(8,128)(2,1)S(1)} %add_convert_fusion.2), channel_id=1, source_target_pairs={{0,8},{1,9},{2,10},{3,11},{4,12},{5,13},{6,14},{7,15},{8,0},{9,1},... | collective-permute-start | bytes 393224 | tf_op jit(solution)/shard_map/ppermute | solution.py:30
  91.5 3.8 %collective-permute-start.27 = (bf16[512,128]{1,0:T(8,128)(2,1)S(1)}, bf16[512,128]{1,0:T(8,128)(2,1)S(1)}, u32[]{:S(2)}, u32[]{:S(2)}) collective-permute-start(bf16[512,128]{1,0:T(8,128)(2,1)S(1)} %clamp_convert_fusion), channel_id=1, source_target_pairs={{0,16},{1,32},{2,48},{3,0},{4,80},{5,96},{6,112},{7,64},{8,120},{9... | collective-permute-start | bytes 393224 | tf_op jit(solution)/shard_map/ppermute | solution.py:30
  95.3 4.4 %collective-permute-start.28 = (bf16[512,128]{1,0:T(8,128)(2,1)S(1)}, bf16[512,128]{1,0:T(8,128)(2,1)S(1)}, u32[]{:S(2)}, u32[]{:S(2)}) collective-permute-start(bf16[512,128]{1,0:T(8,128)(2,1)S(1)} %clamp_convert_fusion), channel_id=1, source_target_pairs={{0,48},{1,0},{2,16},{3,32},{4,112},{5,64},{6,80},{7,96},{8,104},{9... | collective-permute-start | bytes 393224 | tf_op jit(solution)/shard_map/ppermute | solution.py:30
  101.8 3.7 %collective-permute-done.28.refs_2_ = bf16[512,128]{1,0:T(8,128)(2,1)S(1)} collective-permute-done((bf16[512,128]{1,0:T(8,128)(2,1)S(1)}, bf16[512,128]{1,0:T(8,128)(2,1)S(1)}, u32[]{:S(2)}, u32[]{:S(2)}) %collective-permute-start.28) | collective-permute-done | bytes 131104 | tf_op jit(solution)/shard_map/ppermute | solution.py:30
  108.4 1.9 %collective-permute-done.25.refs_0_ = bf16[512,128]{1,0:T(8,128)(2,1)S(1)} collective-permute-done((bf16[512,128]{1,0:T(8,128)(2,1)S(1)}, bf16[512,128]{1,0:T(8,128)(2,1)S(1)}, u32[]{:S(2)}, u32[]{:S(2)}) %collective-permute-start.25) | collective-permute-done | bytes 131104 | tf_op jit(solution)/shard_map/ppermute | solution.py:30
  116.9 2.0 %collective-permute-start.36 = (f16[512,128]{1,0:T(8,128)(2,1)S(1)}, f16[512,128]{1,0:T(8,128)(2,1)S(1)}, u32[]{:S(2)}, u32[]{:S(2)}) collective-permute-start(f16[512,128]{1,0:T(8,128)(2,1)S(1)} %pad_maximum_fusion.9), channel_id=1, source_target_pairs={{0,3},{1,2},{2,1},{3,0},{4,7},{5,6},{6,5},{7,4},{8,15},{9,14},{10,... | collective-permute-start | bytes 393224 | tf_op jit(solution)/shard_map/ppermute | solution.py:30
  121.1 2.9 %collective-permute-done.35 = f16[512,128]{1,0:T(8,128)(2,1)S(1)} collective-permute-done((f16[512,128]{1,0:T(8,128)(2,1)S(1)}, f16[512,128]{1,0:T(8,128)(2,1)S(1)}, u32[]{:S(2)}, u32[]{:S(2)}) %collective-permute-start.35) | collective-permute-done | bytes 131104 | tf_op jit(solution)/shard_map/ppermute | solution.py:30
  124.2 4.0 %collective-permute-start.38 = (f16[512,128]{1,0:T(8,128)(2,1)S(1)}, f16[512,128]{1,0:T(8,128)(2,1)S(1)}, u32[]{:S(2)}, u32[]{:S(2)}) collective-permute-start(f16[512,128]{1,0:T(8,128)(2,1)S(1)} %add_convert_fusion.1), channel_id=1, source_target_pairs={{0,8},{1,9},{2,10},{3,11},{4,12},{5,13},{6,14},{7,15},{8,0},{9,1},... | collective-permute-start | bytes 393224 | tf_op jit(solution)/shard_map/ppermute | solution.py:30
  130.2 3.9 %collective-permute-start.41 = (bf16[512,128]{1,0:T(8,128)(2,1)S(1)}, bf16[512,128]{1,0:T(8,128)(2,1)S(1)}, u32[]{:S(2)}, u32[]{:S(2)}) collective-permute-start(bf16[512,128]{1,0:T(8,128)(2,1)S(1)} %fusion.11), channel_id=1, source_target_pairs={{0,16},{1,32},{2,48},{3,0},{4,80},{5,96},{6,112},{7,64},{8,120},{9... | collective-permute-start | bytes 393224 | tf_op jit(solution)/shard_map/ppermute | solution.py:30
  134.1 5.2 %collective-permute-start.42 = (bf16[512,128]{1,0:T(8,128)(2,1)S(1)}, bf16[512,128]{1,0:T(8,128)(2,1)S(1)}, u32[]{:S(2)}, u32[]{:S(2)}) collective-permute-start(bf16[512,128]{1,0:T(8,128)(2,1)S(1)} %fusion.11), channel_id=1, source_target_pairs={{0,48},{1,0},{2,16},{3,32},{4,112},{5,64},{6,80},{7,96},{8,104},{9... | collective-permute-start | bytes 393224 | tf_op jit(solution)/shard_map/ppermute | solution.py:30
  140.6 2.5 %collective-permute-start.44 = (bf16[512,128]{1,0:T(8,128)(2,1)S(1)}, bf16[512,128]{1,0:T(8,128)(2,1)S(1)}, u32[]{:S(2)}, u32[]{:S(2)}) collective-permute-start(bf16[512,128]{1,0:T(8,128)(2,1)S(1)} %collective-permute-done.41.refs_1_), channel_id=1, source_target_pairs={{0,8},{1,9},{2,10},{3,11},{4,12},{5,13},{6,14},{7,15},{8,0},{9,1},... | collective-permute-start | bytes 393224 | tf_op jit(solution)/shard_map/ppermute | solution.py:30
  143.0 2.6 %collective-permute-done.42.refs_2_ = bf16[512,128]{1,0:T(8,128)(2,1)S(1)} collective-permute-done((bf16[512,128]{1,0:T(8,128)(2,1)S(1)}, bf16[512,128]{1,0:T(8,128)(2,1)S(1)}, u32[]{:S(2)}, u32[]{:S(2)}) %collective-permute-start.42) | collective-permute-done | bytes 131104 | tf_op jit(solution)/shard_map/ppermute | solution.py:30
  145.7 1.8 %shard_map.70.refs_5_.refs_4_ = f32[2048,128]{1,0:T(8,128)S(1)} custom-call(s32[1]{0:T(128)} %bitcast.device_ref, bf16[2048,4096]{1,0:T(8,128)(2,1)S(1)} %bitcast.6, bf16[512,128]{1,0:T(8,128)(2,1)S(1)} %collective-permute-done.40.refs_0_, bf16[512,128]{1,0:T(8,128)(2,1)S(1)} %collective-permute-done.41.refs_1_, ...), custom_call_target="tpu_custom_call" | custom-call | flops 805306368 | bytes 6291456 | tf_op jit(solution)/shard_map/pallas_call | solution.py:124
  147.4 2.4 %collective-permute-done.39.refs_0_ = bf16[512,128]{1,0:T(8,128)(2,1)S(1)} collective-permute-done((bf16[512,128]{1,0:T(8,128)(2,1)S(1)}, bf16[512,128]{1,0:T(8,128)(2,1)S(1)}, u32[]{:S(2)}, u32[]{:S(2)}) %collective-permute-start.39) | collective-permute-done | bytes 131104 | tf_op jit(solution)/shard_map/ppermute | solution.py:30
  154.1 1.8 %collective-permute-start.48 = (f16[512,128]{1,0:T(8,128)(2,1)S(1)}, f16[512,128]{1,0:T(8,128)(2,1)S(1)}, u32[]{:S(2)}, u32[]{:S(2)}) collective-permute-start(f16[512,128]{1,0:T(8,128)(2,1)S(1)} %pad_maximum_fusion.11), channel_id=1, source_target_pairs={{0,2},{1,3},{2,0},{3,1},{4,6},{5,7},{6,4},{7,5},{8,14},{9,15},{10,... | collective-permute-start | bytes 393224 | tf_op jit(solution)/shard_map/ppermute | solution.py:30
  156.1 2.4 %collective-permute-start.50 = (f16[512,128]{1,0:T(8,128)(2,1)S(1)}, f16[512,128]{1,0:T(8,128)(2,1)S(1)}, u32[]{:S(2)}, u32[]{:S(2)}) collective-permute-start(f16[512,128]{1,0:T(8,128)(2,1)S(1)} %pad_maximum_fusion.13), channel_id=1, source_target_pairs={{0,3},{1,2},{2,1},{3,0},{4,7},{5,6},{6,5},{7,4},{8,15},{9,14},{10,... | collective-permute-start | bytes 393224 | tf_op jit(solution)/shard_map/ppermute | solution.py:30
  160.6 2.0 %collective-permute-done.49 = f16[512,128]{1,0:T(8,128)(2,1)S(1)} collective-permute-done((f16[512,128]{1,0:T(8,128)(2,1)S(1)}, f16[512,128]{1,0:T(8,128)(2,1)S(1)}, u32[]{:S(2)}, u32[]{:S(2)}) %collective-permute-start.49) | collective-permute-done | bytes 131104 | tf_op jit(solution)/shard_map/ppermute | solution.py:30
  163.7 3.8 %collective-permute-start.52 = (f16[256,128]{1,0:T(8,128)(2,1)S(1)}, f16[256,128]{1,0:T(8,128)(2,1)S(1)}, u32[]{:S(2)}, u32[]{:S(2)}) collective-permute-start(f16[256,128]{1,0:T(8,128)(2,1)S(1)} %slice.179), channel_id=1, source_target_pairs={{0,8},{1,9},{2,10},{3,11},{4,12},{5,13},{6,14},{7,15},{8,0},{9,1},... | collective-permute-start | bytes 196616 | tf_op jit(solution)/shard_map/ppermute | solution.py:30
  (150 shorter events, 45.4 us)
Async XLA Ops:
  2.9 12.1 %collective-permute-start.2 = (bf16[512,128]{1,0:T(8,128)(2,1)S(1)}, bf16[512,128]{1,0:T(8,128)(2,1)S(1)}, u32[]{:S(2)}, u32[]{:S(2)}) collective-permute-start(bf16[512,128]{1,0:T(8,128)(2,1)S(1)} %pad_maximum_fusion.1), channel_id=1, source_target_pairs={{0,0},{1,16},{2,32},{3,48},{4,64},{5,80},{6,96},{7,112},{8,88},{9,... | collective-permute-start | bytes 393224 | tf_op jit(solution)/shard_map/ppermute | solution.py:30
  3.6 13.1 %collective-permute-start.3 = (bf16[512,128]{1,0:T(8,128)(2,1)S(1)}, bf16[512,128]{1,0:T(8,128)(2,1)S(1)}, u32[]{:S(2)}, u32[]{:S(2)}) collective-permute-start(bf16[512,128]{1,0:T(8,128)(2,1)S(1)} %pad_maximum_fusion.1), channel_id=1, source_target_pairs={{0,16},{1,32},{2,48},{3,0},{4,80},{5,96},{6,112},{7,64},{8,120},{9... | collective-permute-start | bytes 393224 | tf_op jit(solution)/shard_map/ppermute | solution.py:30
  8.4 12.3 %collective-permute-start.4 = (bf16[512,128]{1,0:T(8,128)(2,1)S(1)}, bf16[512,128]{1,0:T(8,128)(2,1)S(1)}, u32[]{:S(2)}, u32[]{:S(2)}) collective-permute-start(bf16[512,128]{1,0:T(8,128)(2,1)S(1)} %pad_maximum_fusion.1), channel_id=1, source_target_pairs={{0,48},{1,0},{2,16},{3,32},{4,112},{5,64},{6,80},{7,96},{8,104},{9... | collective-permute-start | bytes 393224 | tf_op jit(solution)/shard_map/ppermute | solution.py:30
  15.0 12.0 %collective-permute-start.1 = (bf16[512,128]{1,0:T(8,128)(2,1)S(1)}, bf16[512,128]{1,0:T(8,128)(2,1)S(1)}, u32[]{:S(2)}, u32[]{:S(2)}) collective-permute-start(bf16[512,128]{1,0:T(8,128)(2,1)S(1)} %pad_maximum_fusion.1), channel_id=1, source_target_pairs={{0,32},{1,48},{2,0},{3,16},{4,96},{5,112},{6,64},{7,80},{8,72},{9,... | collective-permute-start | bytes 393224 | tf_op jit(solution)/shard_map/ppermute | solution.py:30
  15.0 12.1 %collective-permute-start.6 = (bf16[512,128]{1,0:T(8,128)(2,1)S(1)}, bf16[512,128]{1,0:T(8,128)(2,1)S(1)}, u32[]{:S(2)}, u32[]{:S(2)}) collective-permute-start(bf16[512,128]{1,0:T(8,128)(2,1)S(1)} %collective-permute-done.2.refs_0_), channel_id=1, source_target_pairs={{0,8},{1,9},{2,10},{3,11},{4,12},{5,13},{6,14},{7,15},{8,0},{9,1},... | collective-permute-start | bytes 393224 | tf_op jit(solution)/shard_map/ppermute | solution.py:30
  16.7 10.4 %collective-permute-start.7 = (bf16[512,128]{1,0:T(8,128)(2,1)S(1)}, bf16[512,128]{1,0:T(8,128)(2,1)S(1)}, u32[]{:S(2)}, u32[]{:S(2)}) collective-permute-start(bf16[512,128]{1,0:T(8,128)(2,1)S(1)} %collective-permute-done.3.refs_1_), channel_id=1, source_target_pairs={{0,8},{1,9},{2,10},{3,11},{4,12},{5,13},{6,14},{7,15},{8,0},{9,1},... | collective-permute-start | bytes 393224 | tf_op jit(solution)/shard_map/ppermute | solution.py:30
  52.6 8.1 %collective-permute-start.12 = (bf16[512,128]{1,0:T(8,128)(2,1)S(1)}, bf16[512,128]{1,0:T(8,128)(2,1)S(1)}, u32[]{:S(2)}, u32[]{:S(2)}) collective-permute-start(bf16[512,128]{1,0:T(8,128)(2,1)S(1)} %pad_maximum_fusion.2), channel_id=1, source_target_pairs={{0,0},{1,16},{2,32},{3,48},{4,64},{5,80},{6,96},{7,112},{8,88},{9,... | collective-permute-start | bytes 393224 | tf_op jit(solution)/shard_map/ppermute | solution.py:30
  53.3 8.8 %collective-permute-start.13 = (bf16[512,128]{1,0:T(8,128)(2,1)S(1)}, bf16[512,128]{1,0:T(8,128)(2,1)S(1)}, u32[]{:S(2)}, u32[]{:S(2)}) collective-permute-start(bf16[512,128]{1,0:T(8,128)(2,1)S(1)} %pad_maximum_fusion.2), channel_id=1, source_target_pairs={{0,16},{1,32},{2,48},{3,0},{4,80},{5,96},{6,112},{7,64},{8,120},{9... | collective-permute-start | bytes 393224 | tf_op jit(solution)/shard_map/ppermute | solution.py:30
  56.3 10.0 %collective-permute-start.14 = (bf16[512,128]{1,0:T(8,128)(2,1)S(1)}, bf16[512,128]{1,0:T(8,128)(2,1)S(1)}, u32[]{:S(2)}, u32[]{:S(2)}) collective-permute-start(bf16[512,128]{1,0:T(8,128)(2,1)S(1)} %pad_maximum_fusion.2), channel_id=1, source_target_pairs={{0,48},{1,0},{2,16},{3,32},{4,112},{5,64},{6,80},{7,96},{8,104},{9... | collective-permute-start | bytes 393224 | tf_op jit(solution)/shard_map/ppermute | solution.py:30
  60.6 7.6 %collective-permute-start.11 = (bf16[512,128]{1,0:T(8,128)(2,1)S(1)}, bf16[512,128]{1,0:T(8,128)(2,1)S(1)}, u32[]{:S(2)}, u32[]{:S(2)}) collective-permute-start(bf16[512,128]{1,0:T(8,128)(2,1)S(1)} %pad_maximum_fusion.2), channel_id=1, source_target_pairs={{0,32},{1,48},{2,0},{3,16},{4,96},{5,112},{6,64},{7,80},{8,72},{9,... | collective-permute-start | bytes 393224 | tf_op jit(solution)/shard_map/ppermute | solution.py:30
  60.7 8.1 %collective-permute-start.15 = (bf16[512,128]{1,0:T(8,128)(2,1)S(1)}, bf16[512,128]{1,0:T(8,128)(2,1)S(1)}, u32[]{:S(2)}, u32[]{:S(2)}) collective-permute-start(bf16[512,128]{1,0:T(8,128)(2,1)S(1)} %collective-permute-done.12.refs_0_), channel_id=1, source_target_pairs={{0,8},{1,9},{2,10},{3,11},{4,12},{5,13},{6,14},{7,15},{8,0},{9,1},... | collective-permute-start | bytes 393224 | tf_op jit(solution)/shard_map/ppermute | solution.py:30
  62.1 6.7 %collective-permute-start.16 = (bf16[512,128]{1,0:T(8,128)(2,1)S(1)}, bf16[512,128]{1,0:T(8,128)(2,1)S(1)}, u32[]{:S(2)}, u32[]{:S(2)}) collective-permute-start(bf16[512,128]{1,0:T(8,128)(2,1)S(1)} %collective-permute-done.13.refs_1_), channel_id=1, source_target_pairs={{0,8},{1,9},{2,10},{3,11},{4,12},{5,13},{6,14},{7,15},{8,0},{9,1},... | collective-permute-start | bytes 393224 | tf_op jit(solution)/shard_map/ppermute | solution.py:30
  68.7 11.9 %collective-permute-start.9 = (f32[520,128]{1,0:T(8,128)S(1)}, f32[520,128]{1,0:T(8,128)S(1)}, u32[]{:S(2)}, u32[]{:S(2)}) collective-permute-start(f32[520,128]{1,0:T(8,128)S(1)} %select_maximum_fusion), channel_id=1, source_target_pairs={{0,8},{1,9},{2,10},{3,11},{4,12},{5,13},{6,14},{7,15},{8,0},{9,1},... | collective-permute-start | bytes 798728 | tf_op jit(solution)/shard_map/ppermute | solution.py:30
  73.2 11.1 %collective-permute-start.20 = (f16[512,128]{1,0:T(8,128)(2,1)S(1)}, f16[512,128]{1,0:T(8,128)(2,1)S(1)}, u32[]{:S(2)}, u32[]{:S(2)}) collective-permute-start(f16[512,128]{1,0:T(8,128)(2,1)S(1)} %pad_maximum_fusion.3), channel_id=1, source_target_pairs={{0,2},{1,3},{2,0},{3,1},{4,6},{5,7},{6,4},{7,5},{8,14},{9,15},{10,... | collective-permute-start | bytes 393224 | tf_op jit(solution)/shard_map/ppermute | solution.py:30
  79.1 6.7 %collective-permute-start.21 = (f16[512,128]{1,0:T(8,128)(2,1)S(1)}, f16[512,128]{1,0:T(8,128)(2,1)S(1)}, u32[]{:S(2)}, u32[]{:S(2)}) collective-permute-start(f16[512,128]{1,0:T(8,128)(2,1)S(1)} %pad_maximum_fusion.4), channel_id=1, source_target_pairs={{0,1},{1,0},{2,3},{3,2},{4,5},{5,4},{6,7},{7,6},{8,13},{9,12},{10,... | collective-permute-start | bytes 393224 | tf_op jit(solution)/shard_map/ppermute | solution.py:30
  90.8 8.8 %collective-permute-start.26 = (bf16[512,128]{1,0:T(8,128)(2,1)S(1)}, bf16[512,128]{1,0:T(8,128)(2,1)S(1)}, u32[]{:S(2)}, u32[]{:S(2)}) collective-permute-start(bf16[512,128]{1,0:T(8,128)(2,1)S(1)} %clamp_convert_fusion), channel_id=1, source_target_pairs={{0,0},{1,16},{2,32},{3,48},{4,64},{5,80},{6,96},{7,112},{8,88},{9,... | collective-permute-start | bytes 393224 | tf_op jit(solution)/shard_map/ppermute | solution.py:30
  91.5 10.3 %collective-permute-start.27 = (bf16[512,128]{1,0:T(8,128)(2,1)S(1)}, bf16[512,128]{1,0:T(8,128)(2,1)S(1)}, u32[]{:S(2)}, u32[]{:S(2)}) collective-permute-start(bf16[512,128]{1,0:T(8,128)(2,1)S(1)} %clamp_convert_fusion), channel_id=1, source_target_pairs={{0,16},{1,32},{2,48},{3,0},{4,80},{5,96},{6,112},{7,64},{8,120},{9... | collective-permute-start | bytes 393224 | tf_op jit(solution)/shard_map/ppermute | solution.py:30
  95.3 10.3 %collective-permute-start.28 = (bf16[512,128]{1,0:T(8,128)(2,1)S(1)}, bf16[512,128]{1,0:T(8,128)(2,1)S(1)}, u32[]{:S(2)}, u32[]{:S(2)}) collective-permute-start(bf16[512,128]{1,0:T(8,128)(2,1)S(1)} %clamp_convert_fusion), channel_id=1, source_target_pairs={{0,48},{1,0},{2,16},{3,32},{4,112},{5,64},{6,80},{7,96},{8,104},{9... | collective-permute-start | bytes 393224 | tf_op jit(solution)/shard_map/ppermute | solution.py:30
  99.7 10.7 %collective-permute-start.25 = (bf16[512,128]{1,0:T(8,128)(2,1)S(1)}, bf16[512,128]{1,0:T(8,128)(2,1)S(1)}, u32[]{:S(2)}, u32[]{:S(2)}) collective-permute-start(bf16[512,128]{1,0:T(8,128)(2,1)S(1)} %clamp_convert_fusion), channel_id=1, source_target_pairs={{0,32},{1,48},{2,0},{3,16},{4,96},{5,112},{6,64},{7,80},{8,72},{9,... | collective-permute-start | bytes 393224 | tf_op jit(solution)/shard_map/ppermute | solution.py:30
  99.7 10.7 %collective-permute-start.29 = (bf16[512,128]{1,0:T(8,128)(2,1)S(1)}, bf16[512,128]{1,0:T(8,128)(2,1)S(1)}, u32[]{:S(2)}, u32[]{:S(2)}) collective-permute-start(bf16[512,128]{1,0:T(8,128)(2,1)S(1)} %collective-permute-done.26.refs_0_), channel_id=1, source_target_pairs={{0,8},{1,9},{2,10},{3,11},{4,12},{5,13},{6,14},{7,15},{8,0},{9,1},... | collective-permute-start | bytes 393224 | tf_op jit(solution)/shard_map/ppermute | solution.py:30
  101.8 8.6 %collective-permute-start.30 = (bf16[512,128]{1,0:T(8,128)(2,1)S(1)}, bf16[512,128]{1,0:T(8,128)(2,1)S(1)}, u32[]{:S(2)}, u32[]{:S(2)}) collective-permute-start(bf16[512,128]{1,0:T(8,128)(2,1)S(1)} %collective-permute-done.27.refs_1_), channel_id=1, source_target_pairs={{0,8},{1,9},{2,10},{3,11},{4,12},{5,13},{6,14},{7,15},{8,0},{9,1},... | collective-permute-start | bytes 393224 | tf_op jit(solution)/shard_map/ppermute | solution.py:30
  116.2 7.9 %collective-permute-start.35 = (f16[512,128]{1,0:T(8,128)(2,1)S(1)}, f16[512,128]{1,0:T(8,128)(2,1)S(1)}, u32[]{:S(2)}, u32[]{:S(2)}) collective-permute-start(f16[512,128]{1,0:T(8,128)(2,1)S(1)} %pad_maximum_fusion.8), channel_id=1, source_target_pairs={{0,1},{1,0},{2,3},{3,2},{4,5},{5,4},{6,7},{7,6},{8,13},{9,12},{10,... | collective-permute-start | bytes 393224 | tf_op jit(solution)/shard_map/ppermute | solution.py:30
  116.9 7.2 %collective-permute-start.36 = (f16[512,128]{1,0:T(8,128)(2,1)S(1)}, f16[512,128]{1,0:T(8,128)(2,1)S(1)}, u32[]{:S(2)}, u32[]{:S(2)}) collective-permute-start(f16[512,128]{1,0:T(8,128)(2,1)S(1)} %pad_maximum_fusion.9), channel_id=1, source_target_pairs={{0,3},{1,2},{2,1},{3,0},{4,7},{5,6},{6,5},{7,4},{8,15},{9,14},{10,... | collective-permute-start | bytes 393224 | tf_op jit(solution)/shard_map/ppermute | solution.py:30
  129.5 9.9 %collective-permute-start.40 = (bf16[512,128]{1,0:T(8,128)(2,1)S(1)}, bf16[512,128]{1,0:T(8,128)(2,1)S(1)}, u32[]{:S(2)}, u32[]{:S(2)}) collective-permute-start(bf16[512,128]{1,0:T(8,128)(2,1)S(1)} %fusion.11), channel_id=1, source_target_pairs={{0,0},{1,16},{2,32},{3,48},{4,64},{5,80},{6,96},{7,112},{8,88},{9,... | collective-permute-start | bytes 393224 | tf_op jit(solution)/shard_map/ppermute | solution.py:30
  130.2 10.4 %collective-permute-start.41 = (bf16[512,128]{1,0:T(8,128)(2,1)S(1)}, bf16[512,128]{1,0:T(8,128)(2,1)S(1)}, u32[]{:S(2)}, u32[]{:S(2)}) collective-permute-start(bf16[512,128]{1,0:T(8,128)(2,1)S(1)} %fusion.11), channel_id=1, source_target_pairs={{0,16},{1,32},{2,48},{3,0},{4,80},{5,96},{6,112},{7,64},{8,120},{9... | collective-permute-start | bytes 393224 | tf_op jit(solution)/shard_map/ppermute | solution.py:30
  134.1 11.5 %collective-permute-start.42 = (bf16[512,128]{1,0:T(8,128)(2,1)S(1)}, bf16[512,128]{1,0:T(8,128)(2,1)S(1)}, u32[]{:S(2)}, u32[]{:S(2)}) collective-permute-start(bf16[512,128]{1,0:T(8,128)(2,1)S(1)} %fusion.11), channel_id=1, source_target_pairs={{0,48},{1,0},{2,16},{3,32},{4,112},{5,64},{6,80},{7,96},{8,104},{9... | collective-permute-start | bytes 393224 | tf_op jit(solution)/shard_map/ppermute | solution.py:30
  139.3 10.5 %collective-permute-start.39 = (bf16[512,128]{1,0:T(8,128)(2,1)S(1)}, bf16[512,128]{1,0:T(8,128)(2,1)S(1)}, u32[]{:S(2)}, u32[]{:S(2)}) collective-permute-start(bf16[512,128]{1,0:T(8,128)(2,1)S(1)} %fusion.11), channel_id=1, source_target_pairs={{0,32},{1,48},{2,0},{3,16},{4,96},{5,112},{6,64},{7,80},{8,72},{9,... | collective-permute-start | bytes 393224 | tf_op jit(solution)/shard_map/ppermute | solution.py:30
  139.4 10.5 %collective-permute-start.43 = (bf16[512,128]{1,0:T(8,128)(2,1)S(1)}, bf16[512,128]{1,0:T(8,128)(2,1)S(1)}, u32[]{:S(2)}, u32[]{:S(2)}) collective-permute-start(bf16[512,128]{1,0:T(8,128)(2,1)S(1)} %collective-permute-done.40.refs_0_), channel_id=1, source_target_pairs={{0,8},{1,9},{2,10},{3,11},{4,12},{5,13},{6,14},{7,15},{8,0},{9,1},... | collective-permute-start | bytes 393224 | tf_op jit(solution)/shard_map/ppermute | solution.py:30
  140.6 9.3 %collective-permute-start.44 = (bf16[512,128]{1,0:T(8,128)(2,1)S(1)}, bf16[512,128]{1,0:T(8,128)(2,1)S(1)}, u32[]{:S(2)}, u32[]{:S(2)}) collective-permute-start(bf16[512,128]{1,0:T(8,128)(2,1)S(1)} %collective-permute-done.41.refs_1_), channel_id=1, source_target_pairs={{0,8},{1,9},{2,10},{3,11},{4,12},{5,13},{6,14},{7,15},{8,0},{9,1},... | collective-permute-start | bytes 393224 | tf_op jit(solution)/shard_map/ppermute | solution.py:30
  154.1 6.6 %collective-permute-start.48 = (f16[512,128]{1,0:T(8,128)(2,1)S(1)}, f16[512,128]{1,0:T(8,128)(2,1)S(1)}, u32[]{:S(2)}, u32[]{:S(2)}) collective-permute-start(f16[512,128]{1,0:T(8,128)(2,1)S(1)} %pad_maximum_fusion.11), channel_id=1, source_target_pairs={{0,2},{1,3},{2,0},{3,1},{4,6},{5,7},{6,4},{7,5},{8,14},{9,15},{10,... | collective-permute-start | bytes 393224 | tf_op jit(solution)/shard_map/ppermute | solution.py:30
  155.9 6.7 %collective-permute-start.49 = (f16[512,128]{1,0:T(8,128)(2,1)S(1)}, f16[512,128]{1,0:T(8,128)(2,1)S(1)}, u32[]{:S(2)}, u32[]{:S(2)}) collective-permute-start(f16[512,128]{1,0:T(8,128)(2,1)S(1)} %pad_maximum_fusion.12), channel_id=1, source_target_pairs={{0,1},{1,0},{2,3},{3,2},{4,5},{5,4},{6,7},{7,6},{8,13},{9,12},{10,... | collective-permute-start | bytes 393224 | tf_op jit(solution)/shard_map/ppermute | solution.py:30
  156.1 7.5 %collective-permute-start.50 = (f16[512,128]{1,0:T(8,128)(2,1)S(1)}, f16[512,128]{1,0:T(8,128)(2,1)S(1)}, u32[]{:S(2)}, u32[]{:S(2)}) collective-permute-start(f16[512,128]{1,0:T(8,128)(2,1)S(1)} %pad_maximum_fusion.13), channel_id=1, source_target_pairs={{0,3},{1,2},{2,1},{3,0},{4,7},{5,6},{6,5},{7,4},{8,15},{9,14},{10,... | collective-permute-start | bytes 393224 | tf_op jit(solution)/shard_map/ppermute | solution.py:30
  (28 other events, 301.0 us)

commit v4 on v3

--- a/solution.py
+++ b/solution.py
@@ -153,7 +153,7 @@
         late = permuted(last, other_core)
         terms = [(turns[3], False)] + [(turn, True) for turn in turns[:3]]
         end = [(turns[3], True)]
-        if step_index == 0:
+        if step_index in (0, STEPS - 1):
             total = product(device, coupling, terms, [last, *others], total, ALL, stream)
             total = product(device, coupling, end, [late], total, ALL, stream)
             sent = (total * SCALE).astype(jnp.float16)
@@ -170,13 +170,9 @@
                 rows = slice(turn * PIECE, turn * PIECE + PIECE)
                 sums.append(permuted(jnp.concatenate([kept[rows], given[rows]]), to_owner(turn)))
             half_sum = lax.optimization_barrier(sum(part.astype(jnp.float32) for part in sums).astype(jnp.float16))
-            if step_index == STEPS - 1:
-                field = half_sum[:PIECE].astype(jnp.float32)
-                field += permuted(half_sum[PIECE:], other_core).astype(jnp.float32)
-            else:
-                theirs = permuted(half_sum, other_core)
-                theirs = jnp.concatenate([theirs[PIECE:], theirs[:PIECE]])
-                field = half_sum.astype(jnp.float32) + theirs.astype(jnp.float32)
+            theirs = permuted(half_sum, other_core)
+            theirs = jnp.concatenate([theirs[PIECE:], theirs[:PIECE]])
+            field = half_sum.astype(jnp.float32) + theirs.astype(jnp.float32)
         local_field = field / SCALE
         pump_level = (step_index + 1.0) / (STEPS + 1.0)
         velocity = velocity + time_step * (

time: 171 us -> 170 us (level)
  blocking collectives: 16.4 us -> 32 us
  starting transfers between devices: 82.2 us -> 72.9 us
  waiting for transfers between devices: 38.9 us -> 33.5 us
    all_to_all x1 -> x2, blocking collectives: 16.4 us -> 32 us  [on_device(): parts = lax.all_to_all(sent.reshape(8, PIECE, REPLICAS), 'narrow', 0, 0)]
    ppermute x53 -> x47, starting transfers between devices: 82.2 us -> 72.9 us  [permuted(): return lax.ppermute(array, AXES, pairs)]
    ppermute x53 -> x47, waiting for transfers between devices: 38.9 us -> 33.5 us  [permuted(): return lax.ppermute(array, AXES, pairs)]
    pallas_call x15 -> x14, Pallas kernels: 26.2 us -> 25.9 us  [product(): pl.pallas_call(functools.partial(multiply, terms=terms, rows_of=rows_of,...]
  transfers between devices with their start and end apart: 53 -> 47, of which waited for: 20 -> 17; matrix products, arithmetic and copies ran while one was open for 1% -> 0% of each run, Pallas kernels for 13% -> 13%
where the time goes in v4:
time: 170 us
  starting transfers between devices  72.9 us (43%)
  waiting for transfers between devices  33.5 us (20%)
  blocking collectives  32 us (19%)
  Pallas kernels  25.9 us (15%)
  other arithmetic  3.6 us (2%)
    ppermute x47, starting transfers between devices, permuted(): return lax.ppermute(array, AXES, pairs)  72.9 us
    ppermute x47, waiting for transfers between devices, permuted(): return lax.ppermute(array, AXES, pairs)  33.5 us
    all_to_all x2, blocking collectives, on_device(): parts = lax.all_to_all(sent.reshape(8, PIECE, REPLICAS), 'narrow', 0, 0)  32 us
    pallas_call x14, Pallas kernels, product(): pl.pallas_call(functools.partial(multiply, terms=terms, rows_of=rows_of,...  25.9 us
  transfers between devices with their start and end apart: 47, of which 17 were waited for; matrix products, arithmetic and copies ran while one was open for 0% of the time, Pallas kernels for 13%

profile of v4, /device:TPU:0, one launch (start us, length us, event | category | flops | bytes accessed | tf_op | source)
XLA Modules:
  0.0 169.6 jit_solution(310921114902208844)
XLA Ops:
  3.6 4.8 %collective-permute-start.3 = (bf16[512,128]{1,0:T(8,128)(2,1)S(1)}, bf16[512,128]{1,0:T(8,128)(2,1)S(1)}, u32[]{:S(2)}, u32[]{:S(2)}) collective-permute-start(bf16[512,128]{1,0:T(8,128)(2,1)S(1)} %pad_maximum_fusion.1), channel_id=1, source_target_pairs={{0,16},{1,32},{2,48},{3,0},{4,80},{5,96},{6,112},{7,64},{8,120},{9... | collective-permute-start | bytes 393224 | tf_op jit(solution)/shard_map/ppermute | solution.py:30
  8.4 6.6 %collective-permute-start.4 = (bf16[512,128]{1,0:T(8,128)(2,1)S(1)}, bf16[512,128]{1,0:T(8,128)(2,1)S(1)}, u32[]{:S(2)}, u32[]{:S(2)}) collective-permute-start(bf16[512,128]{1,0:T(8,128)(2,1)S(1)} %pad_maximum_fusion.1), channel_id=1, source_target_pairs={{0,48},{1,0},{2,16},{3,32},{4,112},{5,64},{6,80},{7,96},{8,104},{9... | collective-permute-start | bytes 393224 | tf_op jit(solution)/shard_map/ppermute | solution.py:30
  15.0 1.7 %collective-permute-start.6 = (bf16[512,128]{1,0:T(8,128)(2,1)S(1)}, bf16[512,128]{1,0:T(8,128)(2,1)S(1)}, u32[]{:S(2)}, u32[]{:S(2)}) collective-permute-start(bf16[512,128]{1,0:T(8,128)(2,1)S(1)} %collective-permute-done.2.refs_0_), channel_id=1, source_target_pairs={{0,8},{1,9},{2,10},{3,11},{4,12},{5,13},{6,14},{7,15},{8,0},{9,1},... | collective-permute-start | bytes 393224 | tf_op jit(solution)/shard_map/ppermute | solution.py:30
  17.0 3.6 %collective-permute-done.4.refs_2_ = bf16[512,128]{1,0:T(8,128)(2,1)S(1)} collective-permute-done((bf16[512,128]{1,0:T(8,128)(2,1)S(1)}, bf16[512,128]{1,0:T(8,128)(2,1)S(1)}, u32[]{:S(2)}, u32[]{:S(2)}) %collective-permute-start.4) | collective-permute-done | bytes 131104 | tf_op jit(solution)/shard_map/ppermute | solution.py:30
  20.6 2.7 %collective-permute-start.8 = (bf16[512,128]{1,0:T(8,128)(2,1)S(1)}, bf16[512,128]{1,0:T(8,128)(2,1)S(1)}, u32[]{:S(2)}, u32[]{:S(2)}) collective-permute-start(bf16[512,128]{1,0:T(8,128)(2,1)S(1)} %collective-permute-done.4.refs_2_), channel_id=1, source_target_pairs={{0,8},{1,9},{2,10},{3,11},{4,12},{5,13},{6,14},{7,15},{8,0},{9,1},... | collective-permute-start | bytes 393224 | tf_op jit(solution)/shard_map/ppermute | solution.py:30
  23.3 3.6 %shard_map.59.refs_4_ = f32[2048,128]{1,0:T(8,128)S(1)} custom-call(s32[1]{0:T(128)} %bitcast.device_ref, bf16[2048,4096]{1,0:T(8,128)(2,1)} %coupling_ref.27, bf16[512,128]{1,0:T(8,128)(2,1)S(1)} %collective-permute-done.2.refs_0_, bf16[512,128]{1,0:T(8,128)(2,1)S(1)} %collective-permute-done.3.refs_1_, bf16[512,128]{1,0:T(8,128)(2,1)S(1)} %collective-permute-done.4.refs_2_), custom_call_target="tpu_custom_call" | custom-call | flops 805306368 | bytes 6291456 | tf_op jit(solution)/shard_map/pallas_call | solution.py:124
  27.1 4.5 %shard_map.60.refs_1_ = f32[2048,128]{1,0:T(8,128)S(1)} custom-call(s32[1]{0:T(128)} %bitcast.device_ref, bf16[2048,4096]{1,0:T(8,128)(2,1)} %coupling_ref.27, bf16[512,128]{1,0:T(8,128)(2,1)S(1)} %collective-permute-done.1.refs_0_, bf16[512,128]{1,0:T(8,128)(2,1)S(1)} %collective-permute-done.6.refs_1_, ...), custom_call_target="tpu_custom_call" | custom-call | flops 1073741824 | bytes 8388608 | tf_op jit(solution)/shard_map/pallas_call | solution.py:124
  31.7 2.8 %shard_map.61 = f32[2048,128]{1,0:T(8,128)S(1)} custom-call(s32[1]{0:T(128)} %bitcast.device_ref, bf16[2048,4096]{1,0:T(8,128)(2,1)} %coupling_ref.27, bf16[512,128]{1,0:T(8,128)(2,1)S(1)} %collective-permute-done.5.refs_0_, f32[2048,128]{1,0:T(8,128)S(1)} %shard_map.60.refs_1_), custom_call_target="tpu_custom_call" | custom-call | flops 268435456 | bytes 2097152 | tf_op jit(solution)/shard_map/pallas_call | solution.py:124
  34.6 16.4 %all_to_all.10 = f16[8,256,128]{2,1,0:T(8,128)(2,1)S(1)} all-to-all(f16[8,256,128]{2,1,0:T(8,128)(2,1)S(1)} %bitcast.8), channel_id=1, replica_groups=mesh['wide'=16,'narrow'=8] {'narrow'}, dimensions={0} | all-to-all | bytes 1048576 | tf_op jit(solution)/shard_map/all_to_all | solution.py:160
  53.3 3.0 %collective-permute-start.13 = (bf16[512,128]{1,0:T(8,128)(2,1)S(1)}, bf16[512,128]{1,0:T(8,128)(2,1)S(1)}, u32[]{:S(2)}, u32[]{:S(2)}) collective-permute-start(bf16[512,128]{1,0:T(8,128)(2,1)S(1)} %pad_maximum_fusion.2), channel_id=1, source_target_pairs={{0,16},{1,32},{2,48},{3,0},{4,80},{5,96},{6,112},{7,64},{8,120},{9... | collective-permute-start | bytes 393224 | tf_op jit(solution)/shard_map/ppermute | solution.py:30
  56.3 4.3 %collective-permute-start.14 = (bf16[512,128]{1,0:T(8,128)(2,1)S(1)}, bf16[512,128]{1,0:T(8,128)(2,1)S(1)}, u32[]{:S(2)}, u32[]{:S(2)}) collective-permute-start(bf16[512,128]{1,0:T(8,128)(2,1)S(1)} %pad_maximum_fusion.2), channel_id=1, source_target_pairs={{0,48},{1,0},{2,16},{3,32},{4,112},{5,64},{6,80},{7,96},{8,104},{9... | collective-permute-start | bytes 393224 | tf_op jit(solution)/shard_map/ppermute | solution.py:30
  62.5 3.8 %collective-permute-done.14.refs_2_ = bf16[512,128]{1,0:T(8,128)(2,1)S(1)} collective-permute-done((bf16[512,128]{1,0:T(8,128)(2,1)S(1)}, bf16[512,128]{1,0:T(8,128)(2,1)S(1)}, u32[]{:S(2)}, u32[]{:S(2)}) %collective-permute-start.14) | collective-permute-done | bytes 131104 | tf_op jit(solution)/shard_map/ppermute | solution.py:30
  66.3 1.8 %shard_map.62.refs_5_.refs_4_ = f32[2048,128]{1,0:T(8,128)S(1)} custom-call(s32[1]{0:T(128)} %bitcast.device_ref, bf16[2048,4096]{1,0:T(8,128)(2,1)S(1)} %bitcast.7, bf16[512,128]{1,0:T(8,128)(2,1)S(1)} %collective-permute-done.12.refs_0_, bf16[512,128]{1,0:T(8,128)(2,1)S(1)} %collective-permute-done.13.refs_1_, ...), custom_call_target="tpu_custom_call" | custom-call | flops 805306368 | bytes 6291456 | tf_op jit(solution)/shard_map/pallas_call | solution.py:124
  73.2 5.8 %collective-permute-start.20 = (f16[512,128]{1,0:T(8,128)(2,1)S(1)}, f16[512,128]{1,0:T(8,128)(2,1)S(1)}, u32[]{:S(2)}, u32[]{:S(2)}) collective-permute-start(f16[512,128]{1,0:T(8,128)(2,1)S(1)} %pad_maximum_fusion.3), channel_id=1, source_target_pairs={{0,2},{1,3},{2,0},{3,1},{4,6},{5,7},{6,4},{7,5},{8,14},{9,15},{10,... | collective-permute-start | bytes 393224 | tf_op jit(solution)/shard_map/ppermute | solution.py:30
  80.7 3.7 %collective-permute-done.20 = f16[512,128]{1,0:T(8,128)(2,1)S(1)} collective-permute-done((f16[512,128]{1,0:T(8,128)(2,1)S(1)}, f16[512,128]{1,0:T(8,128)(2,1)S(1)}, u32[]{:S(2)}, u32[]{:S(2)}) %collective-permute-start.20) | collective-permute-done | bytes 131104 | tf_op jit(solution)/shard_map/ppermute | solution.py:30
  85.9 3.8 %collective-permute-start.24 = (f16[512,128]{1,0:T(8,128)(2,1)S(1)}, f16[512,128]{1,0:T(8,128)(2,1)S(1)}, u32[]{:S(2)}, u32[]{:S(2)}) collective-permute-start(f16[512,128]{1,0:T(8,128)(2,1)S(1)} %add_convert_fusion.1), channel_id=1, source_target_pairs={{0,8},{1,9},{2,10},{3,11},{4,12},{5,13},{6,14},{7,15},{8,0},{9,1},... | collective-permute-start | bytes 393224 | tf_op jit(solution)/shard_map/ppermute | solution.py:30
  91.5 3.8 %collective-permute-start.27 = (bf16[512,128]{1,0:T(8,128)(2,1)S(1)}, bf16[512,128]{1,0:T(8,128)(2,1)S(1)}, u32[]{:S(2)}, u32[]{:S(2)}) collective-permute-start(bf16[512,128]{1,0:T(8,128)(2,1)S(1)} %clamp_convert_fusion), channel_id=1, source_target_pairs={{0,16},{1,32},{2,48},{3,0},{4,80},{5,96},{6,112},{7,64},{8,120},{9... | collective-permute-start | bytes 393224 | tf_op jit(solution)/shard_map/ppermute | solution.py:30
  95.3 4.4 %collective-permute-start.28 = (bf16[512,128]{1,0:T(8,128)(2,1)S(1)}, bf16[512,128]{1,0:T(8,128)(2,1)S(1)}, u32[]{:S(2)}, u32[]{:S(2)}) collective-permute-start(bf16[512,128]{1,0:T(8,128)(2,1)S(1)} %clamp_convert_fusion), channel_id=1, source_target_pairs={{0,48},{1,0},{2,16},{3,32},{4,112},{5,64},{6,80},{7,96},{8,104},{9... | collective-permute-start | bytes 393224 | tf_op jit(solution)/shard_map/ppermute | solution.py:30
  101.8 3.7 %collective-permute-done.28.refs_2_ = bf16[512,128]{1,0:T(8,128)(2,1)S(1)} collective-permute-done((bf16[512,128]{1,0:T(8,128)(2,1)S(1)}, bf16[512,128]{1,0:T(8,128)(2,1)S(1)}, u32[]{:S(2)}, u32[]{:S(2)}) %collective-permute-start.28) | collective-permute-done | bytes 131104 | tf_op jit(solution)/shard_map/ppermute | solution.py:30
  106.7 1.8 %shard_map.66.refs_5_.refs_4_ = f32[2048,128]{1,0:T(8,128)S(1)} custom-call(s32[1]{0:T(128)} %bitcast.device_ref, bf16[2048,4096]{1,0:T(8,128)(2,1)S(1)} %bitcast.7, bf16[512,128]{1,0:T(8,128)(2,1)S(1)} %collective-permute-done.26.refs_0_, bf16[512,128]{1,0:T(8,128)(2,1)S(1)} %collective-permute-done.27.refs_1_, ...), custom_call_target="tpu_custom_call" | custom-call | flops 805306368 | bytes 6291456 | tf_op jit(solution)/shard_map/pallas_call | solution.py:124
  108.4 1.9 %collective-permute-done.25.refs_0_ = bf16[512,128]{1,0:T(8,128)(2,1)S(1)} collective-permute-done((bf16[512,128]{1,0:T(8,128)(2,1)S(1)}, bf16[512,128]{1,0:T(8,128)(2,1)S(1)}, u32[]{:S(2)}, u32[]{:S(2)}) %collective-permute-start.25) | collective-permute-done | bytes 131104 | tf_op jit(solution)/shard_map/ppermute | solution.py:30
  116.9 2.0 %collective-permute-start.36 = (f16[512,128]{1,0:T(8,128)(2,1)S(1)}, f16[512,128]{1,0:T(8,128)(2,1)S(1)}, u32[]{:S(2)}, u32[]{:S(2)}) collective-permute-start(f16[512,128]{1,0:T(8,128)(2,1)S(1)} %pad_maximum_fusion.9), channel_id=1, source_target_pairs={{0,3},{1,2},{2,1},{3,0},{4,7},{5,6},{6,5},{7,4},{8,15},{9,14},{10,... | collective-permute-start | bytes 393224 | tf_op jit(solution)/shard_map/ppermute | solution.py:30
  121.1 2.9 %collective-permute-done.35 = f16[512,128]{1,0:T(8,128)(2,1)S(1)} collective-permute-done((f16[512,128]{1,0:T(8,128)(2,1)S(1)}, f16[512,128]{1,0:T(8,128)(2,1)S(1)}, u32[]{:S(2)}, u32[]{:S(2)}) %collective-permute-start.35) | collective-permute-done | bytes 131104 | tf_op jit(solution)/shard_map/ppermute | solution.py:30
  124.2 4.0 %collective-permute-start.38 = (f16[512,128]{1,0:T(8,128)(2,1)S(1)}, f16[512,128]{1,0:T(8,128)(2,1)S(1)}, u32[]{:S(2)}, u32[]{:S(2)}) collective-permute-start(f16[512,128]{1,0:T(8,128)(2,1)S(1)} %add_convert_fusion), channel_id=1, source_target_pairs={{0,8},{1,9},{2,10},{3,11},{4,12},{5,13},{6,14},{7,15},{8,0},{9,1},... | collective-permute-start | bytes 393224 | tf_op jit(solution)/shard_map/ppermute | solution.py:30
  130.2 3.9 %collective-permute-start.41 = (bf16[512,128]{1,0:T(8,128)(2,1)S(1)}, bf16[512,128]{1,0:T(8,128)(2,1)S(1)}, u32[]{:S(2)}, u32[]{:S(2)}) collective-permute-start(bf16[512,128]{1,0:T(8,128)(2,1)S(1)} %fusion.11), channel_id=1, source_target_pairs={{0,16},{1,32},{2,48},{3,0},{4,80},{5,96},{6,112},{7,64},{8,120},{9... | collective-permute-start | bytes 393224 | tf_op jit(solution)/shard_map/ppermute | solution.py:30
  134.1 5.2 %collective-permute-start.42 = (bf16[512,128]{1,0:T(8,128)(2,1)S(1)}, bf16[512,128]{1,0:T(8,128)(2,1)S(1)}, u32[]{:S(2)}, u32[]{:S(2)}) collective-permute-start(bf16[512,128]{1,0:T(8,128)(2,1)S(1)} %fusion.11), channel_id=1, source_target_pairs={{0,48},{1,0},{2,16},{3,32},{4,112},{5,64},{6,80},{7,96},{8,104},{9... | collective-permute-start | bytes 393224 | tf_op jit(solution)/shard_map/ppermute | solution.py:30
  140.6 2.5 %collective-permute-start.45 = (bf16[512,128]{1,0:T(8,128)(2,1)S(1)}, bf16[512,128]{1,0:T(8,128)(2,1)S(1)}, u32[]{:S(2)}, u32[]{:S(2)}) collective-permute-start(bf16[512,128]{1,0:T(8,128)(2,1)S(1)} %collective-permute-done.41.refs_1_), channel_id=1, source_target_pairs={{0,8},{1,9},{2,10},{3,11},{4,12},{5,13},{6,14},{7,15},{8,0},{9,1},... | collective-permute-start | bytes 393224 | tf_op jit(solution)/shard_map/ppermute | solution.py:30
  143.1 2.6 %collective-permute-done.42.refs_2_ = bf16[512,128]{1,0:T(8,128)(2,1)S(1)} collective-permute-done((bf16[512,128]{1,0:T(8,128)(2,1)S(1)}, bf16[512,128]{1,0:T(8,128)(2,1)S(1)}, u32[]{:S(2)}, u32[]{:S(2)}) %collective-permute-start.42) | collective-permute-done | bytes 131104 | tf_op jit(solution)/shard_map/ppermute | solution.py:30
  145.7 1.8 %shard_map.70.refs_4_ = f32[2048,128]{1,0:T(8,128)S(1)} custom-call(s32[1]{0:T(128)} %bitcast.device_ref, bf16[2048,4096]{1,0:T(8,128)(2,1)S(1)} %bitcast.7, bf16[512,128]{1,0:T(8,128)(2,1)S(1)} %collective-permute-done.40.refs_0_, bf16[512,128]{1,0:T(8,128)(2,1)S(1)} %collective-permute-done.41.refs_1_, bf16[512,128]{1,0:T(8,128)(2,1)S(1)} %collective-permute-done.42.refs_2_), custom_call_target="tpu_custom_call" | custom-call | flops 805306368 | bytes 6291456 | tf_op jit(solution)/shard_map/pallas_call | solution.py:124
  147.5 2.4 %collective-permute-done.39.refs_0_ = bf16[512,128]{1,0:T(8,128)(2,1)S(1)} collective-permute-done((bf16[512,128]{1,0:T(8,128)(2,1)S(1)}, bf16[512,128]{1,0:T(8,128)(2,1)S(1)}, u32[]{:S(2)}, u32[]{:S(2)}) %collective-permute-start.39) | collective-permute-done | bytes 131104 | tf_op jit(solution)/shard_map/ppermute | solution.py:30
  149.9 2.3 %shard_map.71.refs_1_ = f32[2048,128]{1,0:T(8,128)S(1)} custom-call(s32[1]{0:T(128)} %bitcast.device_ref, bf16[2048,4096]{1,0:T(8,128)(2,1)S(1)} %bitcast.7, bf16[512,128]{1,0:T(8,128)(2,1)S(1)} %collective-permute-done.39.refs_0_, bf16[512,128]{1,0:T(8,128)(2,1)S(1)} %collective-permute-done.44.refs_1_, ...), custom_call_target="tpu_custom_call" | custom-call | flops 1073741824 | bytes 8388608 | tf_op jit(solution)/shard_map/pallas_call | solution.py:124
  153.1 15.6 %all_to_all.11 = f16[8,256,128]{2,1,0:T(8,128)(2,1)S(1)} all-to-all(f16[8,256,128]{2,1,0:T(8,128)(2,1)S(1)} %bitcast.9), channel_id=1, replica_groups=mesh['wide'=16,'narrow'=8] {'narrow'}, dimensions={0} | all-to-all | bytes 1048576 | tf_op jit(solution)/shard_map/all_to_all | solution.py:160
  (130 shorter events, 34.5 us)
Async XLA Ops:
  2.9 12.1 %collective-permute-start.2 = (bf16[512,128]{1,0:T(8,128)(2,1)S(1)}, bf16[512,128]{1,0:T(8,128)(2,1)S(1)}, u32[]{:S(2)}, u32[]{:S(2)}) collective-permute-start(bf16[512,128]{1,0:T(8,128)(2,1)S(1)} %pad_maximum_fusion.1), channel_id=1, source_target_pairs={{0,0},{1,16},{2,32},{3,48},{4,64},{5,80},{6,96},{7,112},{8,88},{9,... | collective-permute-start | bytes 393224 | tf_op jit(solution)/shard_map/ppermute | solution.py:30
  3.6 13.1 %collective-permute-start.3 = (bf16[512,128]{1,0:T(8,128)(2,1)S(1)}, bf16[512,128]{1,0:T(8,128)(2,1)S(1)}, u32[]{:S(2)}, u32[]{:S(2)}) collective-permute-start(bf16[512,128]{1,0:T(8,128)(2,1)S(1)} %pad_maximum_fusion.1), channel_id=1, source_target_pairs={{0,16},{1,32},{2,48},{3,0},{4,80},{5,96},{6,112},{7,64},{8,120},{9... | collective-permute-start | bytes 393224 | tf_op jit(solution)/shard_map/ppermute | solution.py:30
  8.4 12.3 %collective-permute-start.4 = (bf16[512,128]{1,0:T(8,128)(2,1)S(1)}, bf16[512,128]{1,0:T(8,128)(2,1)S(1)}, u32[]{:S(2)}, u32[]{:S(2)}) collective-permute-start(bf16[512,128]{1,0:T(8,128)(2,1)S(1)} %pad_maximum_fusion.1), channel_id=1, source_target_pairs={{0,48},{1,0},{2,16},{3,32},{4,112},{5,64},{6,80},{7,96},{8,104},{9... | collective-permute-start | bytes 393224 | tf_op jit(solution)/shard_map/ppermute | solution.py:30
  15.0 12.0 %collective-permute-start.1 = (bf16[512,128]{1,0:T(8,128)(2,1)S(1)}, bf16[512,128]{1,0:T(8,128)(2,1)S(1)}, u32[]{:S(2)}, u32[]{:S(2)}) collective-permute-start(bf16[512,128]{1,0:T(8,128)(2,1)S(1)} %pad_maximum_fusion.1), channel_id=1, source_target_pairs={{0,32},{1,48},{2,0},{3,16},{4,96},{5,112},{6,64},{7,80},{8,72},{9,... | collective-permute-start | bytes 393224 | tf_op jit(solution)/shard_map/ppermute | solution.py:30
  15.0 12.1 %collective-permute-start.6 = (bf16[512,128]{1,0:T(8,128)(2,1)S(1)}, bf16[512,128]{1,0:T(8,128)(2,1)S(1)}, u32[]{:S(2)}, u32[]{:S(2)}) collective-permute-start(bf16[512,128]{1,0:T(8,128)(2,1)S(1)} %collective-permute-done.2.refs_0_), channel_id=1, source_target_pairs={{0,8},{1,9},{2,10},{3,11},{4,12},{5,13},{6,14},{7,15},{8,0},{9,1},... | collective-permute-start | bytes 393224 | tf_op jit(solution)/shard_map/ppermute | solution.py:30
  16.7 10.4 %collective-permute-start.7 = (bf16[512,128]{1,0:T(8,128)(2,1)S(1)}, bf16[512,128]{1,0:T(8,128)(2,1)S(1)}, u32[]{:S(2)}, u32[]{:S(2)}) collective-permute-start(bf16[512,128]{1,0:T(8,128)(2,1)S(1)} %collective-permute-done.3.refs_1_), channel_id=1, source_target_pairs={{0,8},{1,9},{2,10},{3,11},{4,12},{5,13},{6,14},{7,15},{8,0},{9,1},... | collective-permute-start | bytes 393224 | tf_op jit(solution)/shard_map/ppermute | solution.py:30
  20.6 6.5 %collective-permute-start.8 = (bf16[512,128]{1,0:T(8,128)(2,1)S(1)}, bf16[512,128]{1,0:T(8,128)(2,1)S(1)}, u32[]{:S(2)}, u32[]{:S(2)}) collective-permute-start(bf16[512,128]{1,0:T(8,128)(2,1)S(1)} %collective-permute-done.4.refs_2_), channel_id=1, source_target_pairs={{0,8},{1,9},{2,10},{3,11},{4,12},{5,13},{6,14},{7,15},{8,0},{9,1},... | collective-permute-start | bytes 393224 | tf_op jit(solution)/shard_map/ppermute | solution.py:30
  52.6 8.1 %collective-permute-start.12 = (bf16[512,128]{1,0:T(8,128)(2,1)S(1)}, bf16[512,128]{1,0:T(8,128)(2,1)S(1)}, u32[]{:S(2)}, u32[]{:S(2)}) collective-permute-start(bf16[512,128]{1,0:T(8,128)(2,1)S(1)} %pad_maximum_fusion.2), channel_id=1, source_target_pairs={{0,0},{1,16},{2,32},{3,48},{4,64},{5,80},{6,96},{7,112},{8,88},{9,... | collective-permute-start | bytes 393224 | tf_op jit(solution)/shard_map/ppermute | solution.py:30
  53.3 8.8 %collective-permute-start.13 = (bf16[512,128]{1,0:T(8,128)(2,1)S(1)}, bf16[512,128]{1,0:T(8,128)(2,1)S(1)}, u32[]{:S(2)}, u32[]{:S(2)}) collective-permute-start(bf16[512,128]{1,0:T(8,128)(2,1)S(1)} %pad_maximum_fusion.2), channel_id=1, source_target_pairs={{0,16},{1,32},{2,48},{3,0},{4,80},{5,96},{6,112},{7,64},{8,120},{9... | collective-permute-start | bytes 393224 | tf_op jit(solution)/shard_map/ppermute | solution.py:30
  56.3 10.0 %collective-permute-start.14 = (bf16[512,128]{1,0:T(8,128)(2,1)S(1)}, bf16[512,128]{1,0:T(8,128)(2,1)S(1)}, u32[]{:S(2)}, u32[]{:S(2)}) collective-permute-start(bf16[512,128]{1,0:T(8,128)(2,1)S(1)} %pad_maximum_fusion.2), channel_id=1, source_target_pairs={{0,48},{1,0},{2,16},{3,32},{4,112},{5,64},{6,80},{7,96},{8,104},{9... | collective-permute-start | bytes 393224 | tf_op jit(solution)/shard_map/ppermute | solution.py:30
  60.6 7.6 %collective-permute-start.11 = (bf16[512,128]{1,0:T(8,128)(2,1)S(1)}, bf16[512,128]{1,0:T(8,128)(2,1)S(1)}, u32[]{:S(2)}, u32[]{:S(2)}) collective-permute-start(bf16[512,128]{1,0:T(8,128)(2,1)S(1)} %pad_maximum_fusion.2), channel_id=1, source_target_pairs={{0,32},{1,48},{2,0},{3,16},{4,96},{5,112},{6,64},{7,80},{8,72},{9,... | collective-permute-start | bytes 393224 | tf_op jit(solution)/shard_map/ppermute | solution.py:30
  60.7 8.1 %collective-permute-start.15 = (bf16[512,128]{1,0:T(8,128)(2,1)S(1)}, bf16[512,128]{1,0:T(8,128)(2,1)S(1)}, u32[]{:S(2)}, u32[]{:S(2)}) collective-permute-start(bf16[512,128]{1,0:T(8,128)(2,1)S(1)} %collective-permute-done.12.refs_0_), channel_id=1, source_target_pairs={{0,8},{1,9},{2,10},{3,11},{4,12},{5,13},{6,14},{7,15},{8,0},{9,1},... | collective-permute-start | bytes 393224 | tf_op jit(solution)/shard_map/ppermute | solution.py:30
  62.1 6.7 %collective-permute-start.16 = (bf16[512,128]{1,0:T(8,128)(2,1)S(1)}, bf16[512,128]{1,0:T(8,128)(2,1)S(1)}, u32[]{:S(2)}, u32[]{:S(2)}) collective-permute-start(bf16[512,128]{1,0:T(8,128)(2,1)S(1)} %collective-permute-done.13.refs_1_), channel_id=1, source_target_pairs={{0,8},{1,9},{2,10},{3,11},{4,12},{5,13},{6,14},{7,15},{8,0},{9,1},... | collective-permute-start | bytes 393224 | tf_op jit(solution)/shard_map/ppermute | solution.py:30
  68.7 11.9 %collective-permute-start.9 = (f32[520,128]{1,0:T(8,128)S(1)}, f32[520,128]{1,0:T(8,128)S(1)}, u32[]{:S(2)}, u32[]{:S(2)}) collective-permute-start(f32[520,128]{1,0:T(8,128)S(1)} %select_maximum_fusion), channel_id=1, source_target_pairs={{0,8},{1,9},{2,10},{3,11},{4,12},{5,13},{6,14},{7,15},{8,0},{9,1},... | collective-permute-start | bytes 798728 | tf_op jit(solution)/shard_map/ppermute | solution.py:30
  73.2 11.1 %collective-permute-start.20 = (f16[512,128]{1,0:T(8,128)(2,1)S(1)}, f16[512,128]{1,0:T(8,128)(2,1)S(1)}, u32[]{:S(2)}, u32[]{:S(2)}) collective-permute-start(f16[512,128]{1,0:T(8,128)(2,1)S(1)} %pad_maximum_fusion.3), channel_id=1, source_target_pairs={{0,2},{1,3},{2,0},{3,1},{4,6},{5,7},{6,4},{7,5},{8,14},{9,15},{10,... | collective-permute-start | bytes 393224 | tf_op jit(solution)/shard_map/ppermute | solution.py:30
  79.1 6.7 %collective-permute-start.21 = (f16[512,128]{1,0:T(8,128)(2,1)S(1)}, f16[512,128]{1,0:T(8,128)(2,1)S(1)}, u32[]{:S(2)}, u32[]{:S(2)}) collective-permute-start(f16[512,128]{1,0:T(8,128)(2,1)S(1)} %pad_maximum_fusion.4), channel_id=1, source_target_pairs={{0,1},{1,0},{2,3},{3,2},{4,5},{5,4},{6,7},{7,6},{8,13},{9,12},{10,... | collective-permute-start | bytes 393224 | tf_op jit(solution)/shard_map/ppermute | solution.py:30
  79.3 6.5 %collective-permute-start.22 = (f16[512,128]{1,0:T(8,128)(2,1)S(1)}, f16[512,128]{1,0:T(8,128)(2,1)S(1)}, u32[]{:S(2)}, u32[]{:S(2)}) collective-permute-start(f16[512,128]{1,0:T(8,128)(2,1)S(1)} %pad_maximum_fusion.5), channel_id=1, source_target_pairs={{0,3},{1,2},{2,1},{3,0},{4,7},{5,6},{6,5},{7,4},{8,15},{9,14},{10,... | collective-permute-start | bytes 393224 | tf_op jit(solution)/shard_map/ppermute | solution.py:30
  90.9 8.8 %collective-permute-start.26 = (bf16[512,128]{1,0:T(8,128)(2,1)S(1)}, bf16[512,128]{1,0:T(8,128)(2,1)S(1)}, u32[]{:S(2)}, u32[]{:S(2)}) collective-permute-start(bf16[512,128]{1,0:T(8,128)(2,1)S(1)} %clamp_convert_fusion), channel_id=1, source_target_pairs={{0,0},{1,16},{2,32},{3,48},{4,64},{5,80},{6,96},{7,112},{8,88},{9,... | collective-permute-start | bytes 393224 | tf_op jit(solution)/shard_map/ppermute | solution.py:30
  91.5 10.3 %collective-permute-start.27 = (bf16[512,128]{1,0:T(8,128)(2,1)S(1)}, bf16[512,128]{1,0:T(8,128)(2,1)S(1)}, u32[]{:S(2)}, u32[]{:S(2)}) collective-permute-start(bf16[512,128]{1,0:T(8,128)(2,1)S(1)} %clamp_convert_fusion), channel_id=1, source_target_pairs={{0,16},{1,32},{2,48},{3,0},{4,80},{5,96},{6,112},{7,64},{8,120},{9... | collective-permute-start | bytes 393224 | tf_op jit(solution)/shard_map/ppermute | solution.py:30
  95.3 10.3 %collective-permute-start.28 = (bf16[512,128]{1,0:T(8,128)(2,1)S(1)}, bf16[512,128]{1,0:T(8,128)(2,1)S(1)}, u32[]{:S(2)}, u32[]{:S(2)}) collective-permute-start(bf16[512,128]{1,0:T(8,128)(2,1)S(1)} %clamp_convert_fusion), channel_id=1, source_target_pairs={{0,48},{1,0},{2,16},{3,32},{4,112},{5,64},{6,80},{7,96},{8,104},{9... | collective-permute-start | bytes 393224 | tf_op jit(solution)/shard_map/ppermute | solution.py:30
  99.7 10.7 %collective-permute-start.25 = (bf16[512,128]{1,0:T(8,128)(2,1)S(1)}, bf16[512,128]{1,0:T(8,128)(2,1)S(1)}, u32[]{:S(2)}, u32[]{:S(2)}) collective-permute-start(bf16[512,128]{1,0:T(8,128)(2,1)S(1)} %clamp_convert_fusion), channel_id=1, source_target_pairs={{0,32},{1,48},{2,0},{3,16},{4,96},{5,112},{6,64},{7,80},{8,72},{9,... | collective-permute-start | bytes 393224 | tf_op jit(solution)/shard_map/ppermute | solution.py:30
  99.7 10.7 %collective-permute-start.29 = (bf16[512,128]{1,0:T(8,128)(2,1)S(1)}, bf16[512,128]{1,0:T(8,128)(2,1)S(1)}, u32[]{:S(2)}, u32[]{:S(2)}) collective-permute-start(bf16[512,128]{1,0:T(8,128)(2,1)S(1)} %collective-permute-done.26.refs_0_), channel_id=1, source_target_pairs={{0,8},{1,9},{2,10},{3,11},{4,12},{5,13},{6,14},{7,15},{8,0},{9,1},... | collective-permute-start | bytes 393224 | tf_op jit(solution)/shard_map/ppermute | solution.py:30
  101.8 8.6 %collective-permute-start.30 = (bf16[512,128]{1,0:T(8,128)(2,1)S(1)}, bf16[512,128]{1,0:T(8,128)(2,1)S(1)}, u32[]{:S(2)}, u32[]{:S(2)}) collective-permute-start(bf16[512,128]{1,0:T(8,128)(2,1)S(1)} %collective-permute-done.27.refs_1_), channel_id=1, source_target_pairs={{0,8},{1,9},{2,10},{3,11},{4,12},{5,13},{6,14},{7,15},{8,0},{9,1},... | collective-permute-start | bytes 393224 | tf_op jit(solution)/shard_map/ppermute | solution.py:30
  114.6 6.6 %collective-permute-start.34 = (f16[512,128]{1,0:T(8,128)(2,1)S(1)}, f16[512,128]{1,0:T(8,128)(2,1)S(1)}, u32[]{:S(2)}, u32[]{:S(2)}) collective-permute-start(f16[512,128]{1,0:T(8,128)(2,1)S(1)} %pad_maximum_fusion.7), channel_id=1, source_target_pairs={{0,2},{1,3},{2,0},{3,1},{4,6},{5,7},{6,4},{7,5},{8,14},{9,15},{10,... | collective-permute-start | bytes 393224 | tf_op jit(solution)/shard_map/ppermute | solution.py:30
  116.2 7.9 %collective-permute-start.35 = (f16[512,128]{1,0:T(8,128)(2,1)S(1)}, f16[512,128]{1,0:T(8,128)(2,1)S(1)}, u32[]{:S(2)}, u32[]{:S(2)}) collective-permute-start(f16[512,128]{1,0:T(8,128)(2,1)S(1)} %pad_maximum_fusion.8), channel_id=1, source_target_pairs={{0,1},{1,0},{2,3},{3,2},{4,5},{5,4},{6,7},{7,6},{8,13},{9,12},{10,... | collective-permute-start | bytes 393224 | tf_op jit(solution)/shard_map/ppermute | solution.py:30
  116.9 7.1 %collective-permute-start.36 = (f16[512,128]{1,0:T(8,128)(2,1)S(1)}, f16[512,128]{1,0:T(8,128)(2,1)S(1)}, u32[]{:S(2)}, u32[]{:S(2)}) collective-permute-start(f16[512,128]{1,0:T(8,128)(2,1)S(1)} %pad_maximum_fusion.9), channel_id=1, source_target_pairs={{0,3},{1,2},{2,1},{3,0},{4,7},{5,6},{6,5},{7,4},{8,15},{9,14},{10,... | collective-permute-start | bytes 393224 | tf_op jit(solution)/shard_map/ppermute | solution.py:30
  129.5 9.9 %collective-permute-start.40 = (bf16[512,128]{1,0:T(8,128)(2,1)S(1)}, bf16[512,128]{1,0:T(8,128)(2,1)S(1)}, u32[]{:S(2)}, u32[]{:S(2)}) collective-permute-start(bf16[512,128]{1,0:T(8,128)(2,1)S(1)} %fusion.11), channel_id=1, source_target_pairs={{0,0},{1,16},{2,32},{3,48},{4,64},{5,80},{6,96},{7,112},{8,88},{9,... | collective-permute-start | bytes 393224 | tf_op jit(solution)/shard_map/ppermute | solution.py:30
  130.2 10.4 %collective-permute-start.41 = (bf16[512,128]{1,0:T(8,128)(2,1)S(1)}, bf16[512,128]{1,0:T(8,128)(2,1)S(1)}, u32[]{:S(2)}, u32[]{:S(2)}) collective-permute-start(bf16[512,128]{1,0:T(8,128)(2,1)S(1)} %fusion.11), channel_id=1, source_target_pairs={{0,16},{1,32},{2,48},{3,0},{4,80},{5,96},{6,112},{7,64},{8,120},{9... | collective-permute-start | bytes 393224 | tf_op jit(solution)/shard_map/ppermute | solution.py:30
  134.1 11.6 %collective-permute-start.42 = (bf16[512,128]{1,0:T(8,128)(2,1)S(1)}, bf16[512,128]{1,0:T(8,128)(2,1)S(1)}, u32[]{:S(2)}, u32[]{:S(2)}) collective-permute-start(bf16[512,128]{1,0:T(8,128)(2,1)S(1)} %fusion.11), channel_id=1, source_target_pairs={{0,48},{1,0},{2,16},{3,32},{4,112},{5,64},{6,80},{7,96},{8,104},{9... | collective-permute-start | bytes 393224 | tf_op jit(solution)/shard_map/ppermute | solution.py:30
  139.4 10.5 %collective-permute-start.39 = (bf16[512,128]{1,0:T(8,128)(2,1)S(1)}, bf16[512,128]{1,0:T(8,128)(2,1)S(1)}, u32[]{:S(2)}, u32[]{:S(2)}) collective-permute-start(bf16[512,128]{1,0:T(8,128)(2,1)S(1)} %fusion.11), channel_id=1, source_target_pairs={{0,32},{1,48},{2,0},{3,16},{4,96},{5,112},{6,64},{7,80},{8,72},{9,... | collective-permute-start | bytes 393224 | tf_op jit(solution)/shard_map/ppermute | solution.py:30
  139.4 10.5 %collective-permute-start.44 = (bf16[512,128]{1,0:T(8,128)(2,1)S(1)}, bf16[512,128]{1,0:T(8,128)(2,1)S(1)}, u32[]{:S(2)}, u32[]{:S(2)}) collective-permute-start(bf16[512,128]{1,0:T(8,128)(2,1)S(1)} %collective-permute-done.40.refs_0_), channel_id=1, source_target_pairs={{0,8},{1,9},{2,10},{3,11},{4,12},{5,13},{6,14},{7,15},{8,0},{9,1},... | collective-permute-start | bytes 393224 | tf_op jit(solution)/shard_map/ppermute | solution.py:30
  140.6 9.3 %collective-permute-start.45 = (bf16[512,128]{1,0:T(8,128)(2,1)S(1)}, bf16[512,128]{1,0:T(8,128)(2,1)S(1)}, u32[]{:S(2)}, u32[]{:S(2)}) collective-permute-start(bf16[512,128]{1,0:T(8,128)(2,1)S(1)} %collective-permute-done.41.refs_1_), channel_id=1, source_target_pairs={{0,8},{1,9},{2,10},{3,11},{4,12},{5,13},{6,14},{7,15},{8,0},{9,1},... | collective-permute-start | bytes 393224 | tf_op jit(solution)/shard_map/ppermute | solution.py:30
  (22 other events, 270.5 us)

commit v5 on v4

--- a/solution.py
+++ b/solution.py
@@ -137,10 +137,10 @@
 
 def on_device(coupling, hashes, momentum, linear):
     device = (lax.axis_index("wide") * 8 + lax.axis_index("narrow")).astype(jnp.int32).reshape(1)
-    positions = (hashes.astype(jnp.float32) - 32768.0) / 65536.0
+    theirs = permuted(hashes, other_core)
+    positions, other_positions = ((h.astype(jnp.float32) - 32768.0) / 65536.0 for h in (hashes, theirs))
     velocity, linear_term = momentum, linear[:, None]
-    lowered = positions.astype(jnp.bfloat16)
-    lowered = jnp.concatenate([lowered, permuted(lowered, other_core)])
+    lowered = jnp.concatenate([positions.astype(jnp.bfloat16), other_positions.astype(jnp.bfloat16)])
     turns = ((0, 1), (1, 3), (3, 2), (2, 0))
     for step_index in range(STEPS):
         own = [permuted(lowered, to_users(turn)) for turn in turns]

time: 170 us -> 170 us (level)
  transfers between devices with their start and end apart: 47 -> 47, of which waited for: 17 -> 17; matrix products, arithmetic and copies ran while one was open for 0% -> 1% of each run, Pallas kernels for 13% -> 13%
where the time goes in v5:
time: 170 us; the launch traced here: 169 us
  starting transfers between devices  72.9 us (43%)
  waiting for transfers between devices  33.1 us (19%)
  blocking collectives  32.1 us (19%)
  Pallas kernels  25.9 us (15%)
  other arithmetic  3.62 us (2%)
    ppermute x47, starting transfers between devices, permuted(): return lax.ppermute(array, AXES, pairs)  72.9 us
    ppermute x47, waiting for transfers between devices, permuted(): return lax.ppermute(array, AXES, pairs)  33.1 us
    all_to_all x2, blocking collectives, on_device(): parts = lax.all_to_all(sent.reshape(8, PIECE, REPLICAS), 'narrow', 0, 0)  32.1 us
    pallas_call x14, Pallas kernels, product(): pl.pallas_call(functools.partial(multiply, terms=terms, rows_of=rows_of,...  25.9 us
  transfers between devices with their start and end apart: 47, of which 17 were waited for; matrix products, arithmetic and copies ran while one was open for 1% of the time, Pallas kernels for 13%

profile of v5, /device:TPU:0, one launch (start us, length us, event | category | flops | bytes accessed | tf_op | source)
XLA Modules:
  0.0 169.2 jit_solution(15766919350454725477)
XLA Ops:
  3.0 4.8 %collective-permute-start.3 = (bf16[512,128]{1,0:T(8,128)(2,1)S(1)}, bf16[512,128]{1,0:T(8,128)(2,1)S(1)}, u32[]{:S(2)}, u32[]{:S(2)}) collective-permute-start(bf16[512,128]{1,0:T(8,128)(2,1)S(1)} %pad_maximum_fusion.1), channel_id=1, source_target_pairs={{0,16},{1,32},{2,48},{3,0},{4,80},{5,96},{6,112},{7,64},{8,120},{9... | collective-permute-start | bytes 393224 | tf_op jit(solution)/shard_map/ppermute | solution.py:30
  7.8 6.6 %collective-permute-start.4 = (bf16[512,128]{1,0:T(8,128)(2,1)S(1)}, bf16[512,128]{1,0:T(8,128)(2,1)S(1)}, u32[]{:S(2)}, u32[]{:S(2)}) collective-permute-start(bf16[512,128]{1,0:T(8,128)(2,1)S(1)} %pad_maximum_fusion.1), channel_id=1, source_target_pairs={{0,48},{1,0},{2,16},{3,32},{4,112},{5,64},{6,80},{7,96},{8,104},{9... | collective-permute-start | bytes 393224 | tf_op jit(solution)/shard_map/ppermute | solution.py:30
  14.4 1.7 %collective-permute-start.6 = (bf16[512,128]{1,0:T(8,128)(2,1)S(1)}, bf16[512,128]{1,0:T(8,128)(2,1)S(1)}, u32[]{:S(2)}, u32[]{:S(2)}) collective-permute-start(bf16[512,128]{1,0:T(8,128)(2,1)S(1)} %collective-permute-done.2.refs_0_), channel_id=1, source_target_pairs={{0,8},{1,9},{2,10},{3,11},{4,12},{5,13},{6,14},{7,15},{8,0},{9,1},... | collective-permute-start | bytes 393224 | tf_op jit(solution)/shard_map/ppermute | solution.py:30
  16.4 3.6 %collective-permute-done.4.refs_2_ = bf16[512,128]{1,0:T(8,128)(2,1)S(1)} collective-permute-done((bf16[512,128]{1,0:T(8,128)(2,1)S(1)}, bf16[512,128]{1,0:T(8,128)(2,1)S(1)}, u32[]{:S(2)}, u32[]{:S(2)}) %collective-permute-start.4) | collective-permute-done | bytes 131104 | tf_op jit(solution)/shard_map/ppermute | solution.py:30
  20.0 2.7 %collective-permute-start.8 = (bf16[512,128]{1,0:T(8,128)(2,1)S(1)}, bf16[512,128]{1,0:T(8,128)(2,1)S(1)}, u32[]{:S(2)}, u32[]{:S(2)}) collective-permute-start(bf16[512,128]{1,0:T(8,128)(2,1)S(1)} %collective-permute-done.4.refs_2_), channel_id=1, source_target_pairs={{0,8},{1,9},{2,10},{3,11},{4,12},{5,13},{6,14},{7,15},{8,0},{9,1},... | collective-permute-start | bytes 393224 | tf_op jit(solution)/shard_map/ppermute | solution.py:30
  22.7 3.6 %shard_map.59.refs_4_ = f32[2048,128]{1,0:T(8,128)S(1)} custom-call(s32[1]{0:T(128)} %bitcast.device_ref, bf16[2048,4096]{1,0:T(8,128)(2,1)} %coupling_ref.27, bf16[512,128]{1,0:T(8,128)(2,1)S(1)} %collective-permute-done.2.refs_0_, bf16[512,128]{1,0:T(8,128)(2,1)S(1)} %collective-permute-done.3.refs_1_, bf16[512,128]{1,0:T(8,128)(2,1)S(1)} %collective-permute-done.4.refs_2_), custom_call_target="tpu_custom_call" | custom-call | flops 805306368 | bytes 6291456 | tf_op jit(solution)/shard_map/pallas_call | solution.py:124
  26.5 4.5 %shard_map.60.refs_1_ = f32[2048,128]{1,0:T(8,128)S(1)} custom-call(s32[1]{0:T(128)} %bitcast.device_ref, bf16[2048,4096]{1,0:T(8,128)(2,1)} %coupling_ref.27, bf16[512,128]{1,0:T(8,128)(2,1)S(1)} %collective-permute-done.1.refs_0_, bf16[512,128]{1,0:T(8,128)(2,1)S(1)} %collective-permute-done.6.refs_1_, ...), custom_call_target="tpu_custom_call" | custom-call | flops 1073741824 | bytes 8388608 | tf_op jit(solution)/shard_map/pallas_call | solution.py:124
  31.1 2.8 %shard_map.61 = f32[2048,128]{1,0:T(8,128)S(1)} custom-call(s32[1]{0:T(128)} %bitcast.device_ref, bf16[2048,4096]{1,0:T(8,128)(2,1)} %coupling_ref.27, bf16[512,128]{1,0:T(8,128)(2,1)S(1)} %collective-permute-done.5.refs_0_, f32[2048,128]{1,0:T(8,128)S(1)} %shard_map.60.refs_1_), custom_call_target="tpu_custom_call" | custom-call | flops 268435456 | bytes 2097152 | tf_op jit(solution)/shard_map/pallas_call | solution.py:124
  34.0 16.4 %all_to_all.10 = f16[8,256,128]{2,1,0:T(8,128)(2,1)S(1)} all-to-all(f16[8,256,128]{2,1,0:T(8,128)(2,1)S(1)} %bitcast.8), channel_id=1, replica_groups=mesh['wide'=16,'narrow'=8] {'narrow'}, dimensions={0} | all-to-all | bytes 1048576 | tf_op jit(solution)/shard_map/all_to_all | solution.py:160
  52.7 3.0 %collective-permute-start.13 = (bf16[512,128]{1,0:T(8,128)(2,1)S(1)}, bf16[512,128]{1,0:T(8,128)(2,1)S(1)}, u32[]{:S(2)}, u32[]{:S(2)}) collective-permute-start(bf16[512,128]{1,0:T(8,128)(2,1)S(1)} %pad_maximum_fusion.2), channel_id=1, source_target_pairs={{0,16},{1,32},{2,48},{3,0},{4,80},{5,96},{6,112},{7,64},{8,120},{9... | collective-permute-start | bytes 393224 | tf_op jit(solution)/shard_map/ppermute | solution.py:30
  55.7 4.3 %collective-permute-start.14 = (bf16[512,128]{1,0:T(8,128)(2,1)S(1)}, bf16[512,128]{1,0:T(8,128)(2,1)S(1)}, u32[]{:S(2)}, u32[]{:S(2)}) collective-permute-start(bf16[512,128]{1,0:T(8,128)(2,1)S(1)} %pad_maximum_fusion.2), channel_id=1, source_target_pairs={{0,48},{1,0},{2,16},{3,32},{4,112},{5,64},{6,80},{7,96},{8,104},{9... | collective-permute-start | bytes 393224 | tf_op jit(solution)/shard_map/ppermute | solution.py:30
  61.9 3.8 %collective-permute-done.14.refs_2_ = bf16[512,128]{1,0:T(8,128)(2,1)S(1)} collective-permute-done((bf16[512,128]{1,0:T(8,128)(2,1)S(1)}, bf16[512,128]{1,0:T(8,128)(2,1)S(1)}, u32[]{:S(2)}, u32[]{:S(2)}) %collective-permute-start.14) | collective-permute-done | bytes 131104 | tf_op jit(solution)/shard_map/ppermute | solution.py:30
  65.7 1.8 %shard_map.62.refs_5_.refs_4_ = f32[2048,128]{1,0:T(8,128)S(1)} custom-call(s32[1]{0:T(128)} %bitcast.device_ref, bf16[2048,4096]{1,0:T(8,128)(2,1)S(1)} %bitcast.7, bf16[512,128]{1,0:T(8,128)(2,1)S(1)} %collective-permute-done.12.refs_0_, bf16[512,128]{1,0:T(8,128)(2,1)S(1)} %collective-permute-done.13.refs_1_, ...), custom_call_target="tpu_custom_call" | custom-call | flops 805306368 | bytes 6291456 | tf_op jit(solution)/shard_map/pallas_call | solution.py:124
  72.6 5.9 %collective-permute-start.20 = (f16[512,128]{1,0:T(8,128)(2,1)S(1)}, f16[512,128]{1,0:T(8,128)(2,1)S(1)}, u32[]{:S(2)}, u32[]{:S(2)}) collective-permute-start(f16[512,128]{1,0:T(8,128)(2,1)S(1)} %pad_maximum_fusion.3), channel_id=1, source_target_pairs={{0,2},{1,3},{2,0},{3,1},{4,6},{5,7},{6,4},{7,5},{8,14},{9,15},{10,... | collective-permute-start | bytes 393224 | tf_op jit(solution)/shard_map/ppermute | solution.py:30
  80.1 3.6 %collective-permute-done.20 = f16[512,128]{1,0:T(8,128)(2,1)S(1)} collective-permute-done((f16[512,128]{1,0:T(8,128)(2,1)S(1)}, f16[512,128]{1,0:T(8,128)(2,1)S(1)}, u32[]{:S(2)}, u32[]{:S(2)}) %collective-permute-start.20) | collective-permute-done | bytes 131104 | tf_op jit(solution)/shard_map/ppermute | solution.py:30
  85.3 3.8 %collective-permute-start.24 = (f16[512,128]{1,0:T(8,128)(2,1)S(1)}, f16[512,128]{1,0:T(8,128)(2,1)S(1)}, u32[]{:S(2)}, u32[]{:S(2)}) collective-permute-start(f16[512,128]{1,0:T(8,128)(2,1)S(1)} %add_convert_fusion.1), channel_id=1, source_target_pairs={{0,8},{1,9},{2,10},{3,11},{4,12},{5,13},{6,14},{7,15},{8,0},{9,1},... | collective-permute-start | bytes 393224 | tf_op jit(solution)/shard_map/ppermute | solution.py:30
  90.9 3.8 %collective-permute-start.27 = (bf16[512,128]{1,0:T(8,128)(2,1)S(1)}, bf16[512,128]{1,0:T(8,128)(2,1)S(1)}, u32[]{:S(2)}, u32[]{:S(2)}) collective-permute-start(bf16[512,128]{1,0:T(8,128)(2,1)S(1)} %clamp_convert_fusion), channel_id=1, source_target_pairs={{0,16},{1,32},{2,48},{3,0},{4,80},{5,96},{6,112},{7,64},{8,120},{9... | collective-permute-start | bytes 393224 | tf_op jit(solution)/shard_map/ppermute | solution.py:30
  94.7 4.4 %collective-permute-start.28 = (bf16[512,128]{1,0:T(8,128)(2,1)S(1)}, bf16[512,128]{1,0:T(8,128)(2,1)S(1)}, u32[]{:S(2)}, u32[]{:S(2)}) collective-permute-start(bf16[512,128]{1,0:T(8,128)(2,1)S(1)} %clamp_convert_fusion), channel_id=1, source_target_pairs={{0,48},{1,0},{2,16},{3,32},{4,112},{5,64},{6,80},{7,96},{8,104},{9... | collective-permute-start | bytes 393224 | tf_op jit(solution)/shard_map/ppermute | solution.py:30
  101.2 3.7 %collective-permute-done.28.refs_2_ = bf16[512,128]{1,0:T(8,128)(2,1)S(1)} collective-permute-done((bf16[512,128]{1,0:T(8,128)(2,1)S(1)}, bf16[512,128]{1,0:T(8,128)(2,1)S(1)}, u32[]{:S(2)}, u32[]{:S(2)}) %collective-permute-start.28) | collective-permute-done | bytes 131104 | tf_op jit(solution)/shard_map/ppermute | solution.py:30
  106.1 1.8 %shard_map.66.refs_5_.refs_4_ = f32[2048,128]{1,0:T(8,128)S(1)} custom-call(s32[1]{0:T(128)} %bitcast.device_ref, bf16[2048,4096]{1,0:T(8,128)(2,1)S(1)} %bitcast.7, bf16[512,128]{1,0:T(8,128)(2,1)S(1)} %collective-permute-done.26.refs_0_, bf16[512,128]{1,0:T(8,128)(2,1)S(1)} %collective-permute-done.27.refs_1_, ...), custom_call_target="tpu_custom_call" | custom-call | flops 805306368 | bytes 6291456 | tf_op jit(solution)/shard_map/pallas_call | solution.py:124
  107.8 1.9 %collective-permute-done.25.refs_0_ = bf16[512,128]{1,0:T(8,128)(2,1)S(1)} collective-permute-done((bf16[512,128]{1,0:T(8,128)(2,1)S(1)}, bf16[512,128]{1,0:T(8,128)(2,1)S(1)}, u32[]{:S(2)}, u32[]{:S(2)}) %collective-permute-start.25) | collective-permute-done | bytes 131104 | tf_op jit(solution)/shard_map/ppermute | solution.py:30
  116.6 2.0 %collective-permute-start.36 = (f16[512,128]{1,0:T(8,128)(2,1)S(1)}, f16[512,128]{1,0:T(8,128)(2,1)S(1)}, u32[]{:S(2)}, u32[]{:S(2)}) collective-permute-start(f16[512,128]{1,0:T(8,128)(2,1)S(1)} %pad_maximum_fusion.9), channel_id=1, source_target_pairs={{0,3},{1,2},{2,1},{3,0},{4,7},{5,6},{6,5},{7,4},{8,15},{9,14},{10,... | collective-permute-start | bytes 393224 | tf_op jit(solution)/shard_map/ppermute | solution.py:30
  120.8 2.9 %collective-permute-done.35 = f16[512,128]{1,0:T(8,128)(2,1)S(1)} collective-permute-done((f16[512,128]{1,0:T(8,128)(2,1)S(1)}, f16[512,128]{1,0:T(8,128)(2,1)S(1)}, u32[]{:S(2)}, u32[]{:S(2)}) %collective-permute-start.35) | collective-permute-done | bytes 131104 | tf_op jit(solution)/shard_map/ppermute | solution.py:30
  123.8 4.0 %collective-permute-start.38 = (f16[512,128]{1,0:T(8,128)(2,1)S(1)}, f16[512,128]{1,0:T(8,128)(2,1)S(1)}, u32[]{:S(2)}, u32[]{:S(2)}) collective-permute-start(f16[512,128]{1,0:T(8,128)(2,1)S(1)} %add_convert_fusion), channel_id=1, source_target_pairs={{0,8},{1,9},{2,10},{3,11},{4,12},{5,13},{6,14},{7,15},{8,0},{9,1},... | collective-permute-start | bytes 393224 | tf_op jit(solution)/shard_map/ppermute | solution.py:30
  129.8 3.9 %collective-permute-start.41 = (bf16[512,128]{1,0:T(8,128)(2,1)S(1)}, bf16[512,128]{1,0:T(8,128)(2,1)S(1)}, u32[]{:S(2)}, u32[]{:S(2)}) collective-permute-start(bf16[512,128]{1,0:T(8,128)(2,1)S(1)} %fusion.11), channel_id=1, source_target_pairs={{0,16},{1,32},{2,48},{3,0},{4,80},{5,96},{6,112},{7,64},{8,120},{9... | collective-permute-start | bytes 393224 | tf_op jit(solution)/shard_map/ppermute | solution.py:30
  133.7 5.3 %collective-permute-start.42 = (bf16[512,128]{1,0:T(8,128)(2,1)S(1)}, bf16[512,128]{1,0:T(8,128)(2,1)S(1)}, u32[]{:S(2)}, u32[]{:S(2)}) collective-permute-start(bf16[512,128]{1,0:T(8,128)(2,1)S(1)} %fusion.11), channel_id=1, source_target_pairs={{0,48},{1,0},{2,16},{3,32},{4,112},{5,64},{6,80},{7,96},{8,104},{9... | collective-permute-start | bytes 393224 | tf_op jit(solution)/shard_map/ppermute | solution.py:30
  140.2 2.5 %collective-permute-start.45 = (bf16[512,128]{1,0:T(8,128)(2,1)S(1)}, bf16[512,128]{1,0:T(8,128)(2,1)S(1)}, u32[]{:S(2)}, u32[]{:S(2)}) collective-permute-start(bf16[512,128]{1,0:T(8,128)(2,1)S(1)} %collective-permute-done.41.refs_1_), channel_id=1, source_target_pairs={{0,8},{1,9},{2,10},{3,11},{4,12},{5,13},{6,14},{7,15},{8,0},{9,1},... | collective-permute-start | bytes 393224 | tf_op jit(solution)/shard_map/ppermute | solution.py:30
  142.7 2.6 %collective-permute-done.42.refs_2_ = bf16[512,128]{1,0:T(8,128)(2,1)S(1)} collective-permute-done((bf16[512,128]{1,0:T(8,128)(2,1)S(1)}, bf16[512,128]{1,0:T(8,128)(2,1)S(1)}, u32[]{:S(2)}, u32[]{:S(2)}) %collective-permute-start.42) | collective-permute-done | bytes 131104 | tf_op jit(solution)/shard_map/ppermute | solution.py:30
  145.3 1.8 %shard_map.70.refs_4_ = f32[2048,128]{1,0:T(8,128)S(1)} custom-call(s32[1]{0:T(128)} %bitcast.device_ref, bf16[2048,4096]{1,0:T(8,128)(2,1)S(1)} %bitcast.7, bf16[512,128]{1,0:T(8,128)(2,1)S(1)} %collective-permute-done.40.refs_0_, bf16[512,128]{1,0:T(8,128)(2,1)S(1)} %collective-permute-done.41.refs_1_, bf16[512,128]{1,0:T(8,128)(2,1)S(1)} %collective-permute-done.42.refs_2_), custom_call_target="tpu_custom_call" | custom-call | flops 805306368 | bytes 6291456 | tf_op jit(solution)/shard_map/pallas_call | solution.py:124
  147.1 2.4 %collective-permute-done.39.refs_0_ = bf16[512,128]{1,0:T(8,128)(2,1)S(1)} collective-permute-done((bf16[512,128]{1,0:T(8,128)(2,1)S(1)}, bf16[512,128]{1,0:T(8,128)(2,1)S(1)}, u32[]{:S(2)}, u32[]{:S(2)}) %collective-permute-start.39) | collective-permute-done | bytes 131104 | tf_op jit(solution)/shard_map/ppermute | solution.py:30
  149.5 2.3 %shard_map.71.refs_1_ = f32[2048,128]{1,0:T(8,128)S(1)} custom-call(s32[1]{0:T(128)} %bitcast.device_ref, bf16[2048,4096]{1,0:T(8,128)(2,1)S(1)} %bitcast.7, bf16[512,128]{1,0:T(8,128)(2,1)S(1)} %collective-permute-done.39.refs_0_, bf16[512,128]{1,0:T(8,128)(2,1)S(1)} %collective-permute-done.44.refs_1_, ...), custom_call_target="tpu_custom_call" | custom-call | flops 1073741824 | bytes 8388608 | tf_op jit(solution)/shard_map/pallas_call | solution.py:124
  152.7 15.6 %all_to_all.11 = f16[8,256,128]{2,1,0:T(8,128)(2,1)S(1)} all-to-all(f16[8,256,128]{2,1,0:T(8,128)(2,1)S(1)} %bitcast.9), channel_id=1, replica_groups=mesh['wide'=16,'narrow'=8] {'narrow'}, dimensions={0} | all-to-all | bytes 1048576 | tf_op jit(solution)/shard_map/all_to_all | solution.py:160
  (131 shorter events, 34.1 us)
Async XLA Ops:
  2.3 12.1 %collective-permute-start.2 = (bf16[512,128]{1,0:T(8,128)(2,1)S(1)}, bf16[512,128]{1,0:T(8,128)(2,1)S(1)}, u32[]{:S(2)}, u32[]{:S(2)}) collective-permute-start(bf16[512,128]{1,0:T(8,128)(2,1)S(1)} %pad_maximum_fusion.1), channel_id=1, source_target_pairs={{0,0},{1,16},{2,32},{3,48},{4,64},{5,80},{6,96},{7,112},{8,88},{9,... | collective-permute-start | bytes 393224 | tf_op jit(solution)/shard_map/ppermute | solution.py:30
  3.0 13.1 %collective-permute-start.3 = (bf16[512,128]{1,0:T(8,128)(2,1)S(1)}, bf16[512,128]{1,0:T(8,128)(2,1)S(1)}, u32[]{:S(2)}, u32[]{:S(2)}) collective-permute-start(bf16[512,128]{1,0:T(8,128)(2,1)S(1)} %pad_maximum_fusion.1), channel_id=1, source_target_pairs={{0,16},{1,32},{2,48},{3,0},{4,80},{5,96},{6,112},{7,64},{8,120},{9... | collective-permute-start | bytes 393224 | tf_op jit(solution)/shard_map/ppermute | solution.py:30
  7.8 12.3 %collective-permute-start.4 = (bf16[512,128]{1,0:T(8,128)(2,1)S(1)}, bf16[512,128]{1,0:T(8,128)(2,1)S(1)}, u32[]{:S(2)}, u32[]{:S(2)}) collective-permute-start(bf16[512,128]{1,0:T(8,128)(2,1)S(1)} %pad_maximum_fusion.1), channel_id=1, source_target_pairs={{0,48},{1,0},{2,16},{3,32},{4,112},{5,64},{6,80},{7,96},{8,104},{9... | collective-permute-start | bytes 393224 | tf_op jit(solution)/shard_map/ppermute | solution.py:30
  14.4 12.0 %collective-permute-start.1 = (bf16[512,128]{1,0:T(8,128)(2,1)S(1)}, bf16[512,128]{1,0:T(8,128)(2,1)S(1)}, u32[]{:S(2)}, u32[]{:S(2)}) collective-permute-start(bf16[512,128]{1,0:T(8,128)(2,1)S(1)} %pad_maximum_fusion.1), channel_id=1, source_target_pairs={{0,32},{1,48},{2,0},{3,16},{4,96},{5,112},{6,64},{7,80},{8,72},{9,... | collective-permute-start | bytes 393224 | tf_op jit(solution)/shard_map/ppermute | solution.py:30
  14.4 12.1 %collective-permute-start.6 = (bf16[512,128]{1,0:T(8,128)(2,1)S(1)}, bf16[512,128]{1,0:T(8,128)(2,1)S(1)}, u32[]{:S(2)}, u32[]{:S(2)}) collective-permute-start(bf16[512,128]{1,0:T(8,128)(2,1)S(1)} %collective-permute-done.2.refs_0_), channel_id=1, source_target_pairs={{0,8},{1,9},{2,10},{3,11},{4,12},{5,13},{6,14},{7,15},{8,0},{9,1},... | collective-permute-start | bytes 393224 | tf_op jit(solution)/shard_map/ppermute | solution.py:30
  16.1 10.4 %collective-permute-start.7 = (bf16[512,128]{1,0:T(8,128)(2,1)S(1)}, bf16[512,128]{1,0:T(8,128)(2,1)S(1)}, u32[]{:S(2)}, u32[]{:S(2)}) collective-permute-start(bf16[512,128]{1,0:T(8,128)(2,1)S(1)} %collective-permute-done.3.refs_1_), channel_id=1, source_target_pairs={{0,8},{1,9},{2,10},{3,11},{4,12},{5,13},{6,14},{7,15},{8,0},{9,1},... | collective-permute-start | bytes 393224 | tf_op jit(solution)/shard_map/ppermute | solution.py:30
  20.0 6.5 %collective-permute-start.8 = (bf16[512,128]{1,0:T(8,128)(2,1)S(1)}, bf16[512,128]{1,0:T(8,128)(2,1)S(1)}, u32[]{:S(2)}, u32[]{:S(2)}) collective-permute-start(bf16[512,128]{1,0:T(8,128)(2,1)S(1)} %collective-permute-done.4.refs_2_), channel_id=1, source_target_pairs={{0,8},{1,9},{2,10},{3,11},{4,12},{5,13},{6,14},{7,15},{8,0},{9,1},... | collective-permute-start | bytes 393224 | tf_op jit(solution)/shard_map/ppermute | solution.py:30
  52.0 8.1 %collective-permute-start.12 = (bf16[512,128]{1,0:T(8,128)(2,1)S(1)}, bf16[512,128]{1,0:T(8,128)(2,1)S(1)}, u32[]{:S(2)}, u32[]{:S(2)}) collective-permute-start(bf16[512,128]{1,0:T(8,128)(2,1)S(1)} %pad_maximum_fusion.2), channel_id=1, source_target_pairs={{0,0},{1,16},{2,32},{3,48},{4,64},{5,80},{6,96},{7,112},{8,88},{9,... | collective-permute-start | bytes 393224 | tf_op jit(solution)/shard_map/ppermute | solution.py:30
  52.7 8.8 %collective-permute-start.13 = (bf16[512,128]{1,0:T(8,128)(2,1)S(1)}, bf16[512,128]{1,0:T(8,128)(2,1)S(1)}, u32[]{:S(2)}, u32[]{:S(2)}) collective-permute-start(bf16[512,128]{1,0:T(8,128)(2,1)S(1)} %pad_maximum_fusion.2), channel_id=1, source_target_pairs={{0,16},{1,32},{2,48},{3,0},{4,80},{5,96},{6,112},{7,64},{8,120},{9... | collective-permute-start | bytes 393224 | tf_op jit(solution)/shard_map/ppermute | solution.py:30
  55.7 10.0 %collective-permute-start.14 = (bf16[512,128]{1,0:T(8,128)(2,1)S(1)}, bf16[512,128]{1,0:T(8,128)(2,1)S(1)}, u32[]{:S(2)}, u32[]{:S(2)}) collective-permute-start(bf16[512,128]{1,0:T(8,128)(2,1)S(1)} %pad_maximum_fusion.2), channel_id=1, source_target_pairs={{0,48},{1,0},{2,16},{3,32},{4,112},{5,64},{6,80},{7,96},{8,104},{9... | collective-permute-start | bytes 393224 | tf_op jit(solution)/shard_map/ppermute | solution.py:30
  60.0 7.6 %collective-permute-start.11 = (bf16[512,128]{1,0:T(8,128)(2,1)S(1)}, bf16[512,128]{1,0:T(8,128)(2,1)S(1)}, u32[]{:S(2)}, u32[]{:S(2)}) collective-permute-start(bf16[512,128]{1,0:T(8,128)(2,1)S(1)} %pad_maximum_fusion.2), channel_id=1, source_target_pairs={{0,32},{1,48},{2,0},{3,16},{4,96},{5,112},{6,64},{7,80},{8,72},{9,... | collective-permute-start | bytes 393224 | tf_op jit(solution)/shard_map/ppermute | solution.py:30
  60.1 8.3 %collective-permute-start.15 = (bf16[512,128]{1,0:T(8,128)(2,1)S(1)}, bf16[512,128]{1,0:T(8,128)(2,1)S(1)}, u32[]{:S(2)}, u32[]{:S(2)}) collective-permute-start(bf16[512,128]{1,0:T(8,128)(2,1)S(1)} %collective-permute-done.12.refs_0_), channel_id=1, source_target_pairs={{0,8},{1,9},{2,10},{3,11},{4,12},{5,13},{6,14},{7,15},{8,0},{9,1},... | collective-permute-start | bytes 393224 | tf_op jit(solution)/shard_map/ppermute | solution.py:30
  61.5 6.9 %collective-permute-start.16 = (bf16[512,128]{1,0:T(8,128)(2,1)S(1)}, bf16[512,128]{1,0:T(8,128)(2,1)S(1)}, u32[]{:S(2)}, u32[]{:S(2)}) collective-permute-start(bf16[512,128]{1,0:T(8,128)(2,1)S(1)} %collective-permute-done.13.refs_1_), channel_id=1, source_target_pairs={{0,8},{1,9},{2,10},{3,11},{4,12},{5,13},{6,14},{7,15},{8,0},{9,1},... | collective-permute-start | bytes 393224 | tf_op jit(solution)/shard_map/ppermute | solution.py:30
  68.1 11.9 %collective-permute-start.9 = (f32[520,128]{1,0:T(8,128)S(1)}, f32[520,128]{1,0:T(8,128)S(1)}, u32[]{:S(2)}, u32[]{:S(2)}) collective-permute-start(f32[520,128]{1,0:T(8,128)S(1)} %select_maximum_fusion), channel_id=1, source_target_pairs={{0,8},{1,9},{2,10},{3,11},{4,12},{5,13},{6,14},{7,15},{8,0},{9,1},... | collective-permute-start | bytes 798728 | tf_op jit(solution)/shard_map/ppermute | solution.py:30
  72.6 11.1 %collective-permute-start.20 = (f16[512,128]{1,0:T(8,128)(2,1)S(1)}, f16[512,128]{1,0:T(8,128)(2,1)S(1)}, u32[]{:S(2)}, u32[]{:S(2)}) collective-permute-start(f16[512,128]{1,0:T(8,128)(2,1)S(1)} %pad_maximum_fusion.3), channel_id=1, source_target_pairs={{0,2},{1,3},{2,0},{3,1},{4,6},{5,7},{6,4},{7,5},{8,14},{9,15},{10,... | collective-permute-start | bytes 393224 | tf_op jit(solution)/shard_map/ppermute | solution.py:30
  78.5 6.7 %collective-permute-start.21 = (f16[512,128]{1,0:T(8,128)(2,1)S(1)}, f16[512,128]{1,0:T(8,128)(2,1)S(1)}, u32[]{:S(2)}, u32[]{:S(2)}) collective-permute-start(f16[512,128]{1,0:T(8,128)(2,1)S(1)} %pad_maximum_fusion.4), channel_id=1, source_target_pairs={{0,1},{1,0},{2,3},{3,2},{4,5},{5,4},{6,7},{7,6},{8,13},{9,12},{10,... | collective-permute-start | bytes 393224 | tf_op jit(solution)/shard_map/ppermute | solution.py:30
  78.7 6.5 %collective-permute-start.22 = (f16[512,128]{1,0:T(8,128)(2,1)S(1)}, f16[512,128]{1,0:T(8,128)(2,1)S(1)}, u32[]{:S(2)}, u32[]{:S(2)}) collective-permute-start(f16[512,128]{1,0:T(8,128)(2,1)S(1)} %pad_maximum_fusion.5), channel_id=1, source_target_pairs={{0,3},{1,2},{2,1},{3,0},{4,7},{5,6},{6,5},{7,4},{8,15},{9,14},{10,... | collective-permute-start | bytes 393224 | tf_op jit(solution)/shard_map/ppermute | solution.py:30
  90.3 8.8 %collective-permute-start.26 = (bf16[512,128]{1,0:T(8,128)(2,1)S(1)}, bf16[512,128]{1,0:T(8,128)(2,1)S(1)}, u32[]{:S(2)}, u32[]{:S(2)}) collective-permute-start(bf16[512,128]{1,0:T(8,128)(2,1)S(1)} %clamp_convert_fusion), channel_id=1, source_target_pairs={{0,0},{1,16},{2,32},{3,48},{4,64},{5,80},{6,96},{7,112},{8,88},{9,... | collective-permute-start | bytes 393224 | tf_op jit(solution)/shard_map/ppermute | solution.py:30
  90.9 10.3 %collective-permute-start.27 = (bf16[512,128]{1,0:T(8,128)(2,1)S(1)}, bf16[512,128]{1,0:T(8,128)(2,1)S(1)}, u32[]{:S(2)}, u32[]{:S(2)}) collective-permute-start(bf16[512,128]{1,0:T(8,128)(2,1)S(1)} %clamp_convert_fusion), channel_id=1, source_target_pairs={{0,16},{1,32},{2,48},{3,0},{4,80},{5,96},{6,112},{7,64},{8,120},{9... | collective-permute-start | bytes 393224 | tf_op jit(solution)/shard_map/ppermute | solution.py:30
  94.7 10.2 %collective-permute-start.28 = (bf16[512,128]{1,0:T(8,128)(2,1)S(1)}, bf16[512,128]{1,0:T(8,128)(2,1)S(1)}, u32[]{:S(2)}, u32[]{:S(2)}) collective-permute-start(bf16[512,128]{1,0:T(8,128)(2,1)S(1)} %clamp_convert_fusion), channel_id=1, source_target_pairs={{0,48},{1,0},{2,16},{3,32},{4,112},{5,64},{6,80},{7,96},{8,104},{9... | collective-permute-start | bytes 393224 | tf_op jit(solution)/shard_map/ppermute | solution.py:30
  99.1 10.7 %collective-permute-start.25 = (bf16[512,128]{1,0:T(8,128)(2,1)S(1)}, bf16[512,128]{1,0:T(8,128)(2,1)S(1)}, u32[]{:S(2)}, u32[]{:S(2)}) collective-permute-start(bf16[512,128]{1,0:T(8,128)(2,1)S(1)} %clamp_convert_fusion), channel_id=1, source_target_pairs={{0,32},{1,48},{2,0},{3,16},{4,96},{5,112},{6,64},{7,80},{8,72},{9,... | collective-permute-start | bytes 393224 | tf_op jit(solution)/shard_map/ppermute | solution.py:30
  99.1 10.7 %collective-permute-start.29 = (bf16[512,128]{1,0:T(8,128)(2,1)S(1)}, bf16[512,128]{1,0:T(8,128)(2,1)S(1)}, u32[]{:S(2)}, u32[]{:S(2)}) collective-permute-start(bf16[512,128]{1,0:T(8,128)(2,1)S(1)} %collective-permute-done.26.refs_0_), channel_id=1, source_target_pairs={{0,8},{1,9},{2,10},{3,11},{4,12},{5,13},{6,14},{7,15},{8,0},{9,1},... | collective-permute-start | bytes 393224 | tf_op jit(solution)/shard_map/ppermute | solution.py:30
  101.2 8.6 %collective-permute-start.30 = (bf16[512,128]{1,0:T(8,128)(2,1)S(1)}, bf16[512,128]{1,0:T(8,128)(2,1)S(1)}, u32[]{:S(2)}, u32[]{:S(2)}) collective-permute-start(bf16[512,128]{1,0:T(8,128)(2,1)S(1)} %collective-permute-done.27.refs_1_), channel_id=1, source_target_pairs={{0,8},{1,9},{2,10},{3,11},{4,12},{5,13},{6,14},{7,15},{8,0},{9,1},... | collective-permute-start | bytes 393224 | tf_op jit(solution)/shard_map/ppermute | solution.py:30
  114.2 6.6 %collective-permute-start.34 = (f16[512,128]{1,0:T(8,128)(2,1)S(1)}, f16[512,128]{1,0:T(8,128)(2,1)S(1)}, u32[]{:S(2)}, u32[]{:S(2)}) collective-permute-start(f16[512,128]{1,0:T(8,128)(2,1)S(1)} %pad_maximum_fusion.7), channel_id=1, source_target_pairs={{0,2},{1,3},{2,0},{3,1},{4,6},{5,7},{6,4},{7,5},{8,14},{9,15},{10,... | collective-permute-start | bytes 393224 | tf_op jit(solution)/shard_map/ppermute | solution.py:30
  115.8 7.9 %collective-permute-start.35 = (f16[512,128]{1,0:T(8,128)(2,1)S(1)}, f16[512,128]{1,0:T(8,128)(2,1)S(1)}, u32[]{:S(2)}, u32[]{:S(2)}) collective-permute-start(f16[512,128]{1,0:T(8,128)(2,1)S(1)} %pad_maximum_fusion.8), channel_id=1, source_target_pairs={{0,1},{1,0},{2,3},{3,2},{4,5},{5,4},{6,7},{7,6},{8,13},{9,12},{10,... | collective-permute-start | bytes 393224 | tf_op jit(solution)/shard_map/ppermute | solution.py:30
  116.6 7.1 %collective-permute-start.36 = (f16[512,128]{1,0:T(8,128)(2,1)S(1)}, f16[512,128]{1,0:T(8,128)(2,1)S(1)}, u32[]{:S(2)}, u32[]{:S(2)}) collective-permute-start(f16[512,128]{1,0:T(8,128)(2,1)S(1)} %pad_maximum_fusion.9), channel_id=1, source_target_pairs={{0,3},{1,2},{2,1},{3,0},{4,7},{5,6},{6,5},{7,4},{8,15},{9,14},{10,... | collective-permute-start | bytes 393224 | tf_op jit(solution)/shard_map/ppermute | solution.py:30
  129.1 9.9 %collective-permute-start.40 = (bf16[512,128]{1,0:T(8,128)(2,1)S(1)}, bf16[512,128]{1,0:T(8,128)(2,1)S(1)}, u32[]{:S(2)}, u32[]{:S(2)}) collective-permute-start(bf16[512,128]{1,0:T(8,128)(2,1)S(1)} %fusion.11), channel_id=1, source_target_pairs={{0,0},{1,16},{2,32},{3,48},{4,64},{5,80},{6,96},{7,112},{8,88},{9,... | collective-permute-start | bytes 393224 | tf_op jit(solution)/shard_map/ppermute | solution.py:30
  129.8 10.4 %collective-permute-start.41 = (bf16[512,128]{1,0:T(8,128)(2,1)S(1)}, bf16[512,128]{1,0:T(8,128)(2,1)S(1)}, u32[]{:S(2)}, u32[]{:S(2)}) collective-permute-start(bf16[512,128]{1,0:T(8,128)(2,1)S(1)} %fusion.11), channel_id=1, source_target_pairs={{0,16},{1,32},{2,48},{3,0},{4,80},{5,96},{6,112},{7,64},{8,120},{9... | collective-permute-start | bytes 393224 | tf_op jit(solution)/shard_map/ppermute | solution.py:30
  133.7 11.5 %collective-permute-start.42 = (bf16[512,128]{1,0:T(8,128)(2,1)S(1)}, bf16[512,128]{1,0:T(8,128)(2,1)S(1)}, u32[]{:S(2)}, u32[]{:S(2)}) collective-permute-start(bf16[512,128]{1,0:T(8,128)(2,1)S(1)} %fusion.11), channel_id=1, source_target_pairs={{0,48},{1,0},{2,16},{3,32},{4,112},{5,64},{6,80},{7,96},{8,104},{9... | collective-permute-start | bytes 393224 | tf_op jit(solution)/shard_map/ppermute | solution.py:30
  139.0 10.5 %collective-permute-start.39 = (bf16[512,128]{1,0:T(8,128)(2,1)S(1)}, bf16[512,128]{1,0:T(8,128)(2,1)S(1)}, u32[]{:S(2)}, u32[]{:S(2)}) collective-permute-start(bf16[512,128]{1,0:T(8,128)(2,1)S(1)} %fusion.11), channel_id=1, source_target_pairs={{0,32},{1,48},{2,0},{3,16},{4,96},{5,112},{6,64},{7,80},{8,72},{9,... | collective-permute-start | bytes 393224 | tf_op jit(solution)/shard_map/ppermute | solution.py:30
  139.0 10.5 %collective-permute-start.44 = (bf16[512,128]{1,0:T(8,128)(2,1)S(1)}, bf16[512,128]{1,0:T(8,128)(2,1)S(1)}, u32[]{:S(2)}, u32[]{:S(2)}) collective-permute-start(bf16[512,128]{1,0:T(8,128)(2,1)S(1)} %collective-permute-done.40.refs_0_), channel_id=1, source_target_pairs={{0,8},{1,9},{2,10},{3,11},{4,12},{5,13},{6,14},{7,15},{8,0},{9,1},... | collective-permute-start | bytes 393224 | tf_op jit(solution)/shard_map/ppermute | solution.py:30
  140.2 9.3 %collective-permute-start.45 = (bf16[512,128]{1,0:T(8,128)(2,1)S(1)}, bf16[512,128]{1,0:T(8,128)(2,1)S(1)}, u32[]{:S(2)}, u32[]{:S(2)}) collective-permute-start(bf16[512,128]{1,0:T(8,128)(2,1)S(1)} %collective-permute-done.41.refs_1_), channel_id=1, source_target_pairs={{0,8},{1,9},{2,10},{3,11},{4,12},{5,13},{6,14},{7,15},{8,0},{9,1},... | collective-permute-start | bytes 393224 | tf_op jit(solution)/shard_map/ppermute | solution.py:30
  (22 other events, 271.2 us)
